TPU v7x, 32 devices: a whole 2x2x4 slice. The times are simulated.
32 devices in a mesh: rep: 8 (over z, y), grp: 4 (over x, core).
Axes of the slice: x: 2, y: 2, z: 4, core: 2. Of those that a mesh axis runs over, the one named last changes fastest.
Arguments:
- tokens: int32 [32, 1024], P(('rep', 'grp')), may hold values from 0 to 32
- mask: int32 [32, 1024], P(('rep', 'grp')), may hold values from 0 to 1, as said below
- targets: int32 [32, 1024], P(('rep', 'grp')), may hold values from 0 to 32
- mats_d: float32 [1, 480, 3840], P(None, 'grp')
- mats_down: float32 [1, 1920, 480], P(None, 'grp'), may hold values from -0.125 to 0.125
- mom_d: float32 [1, 480, 3840], P(None, 'grp'), may hold values from -4.5776367e-05 to 4.5776367e-05
- mom_down: float32 [1, 1920, 480], P(None, 'grp'), may hold values from -4.5776367e-05 to 4.5776367e-05
- err_d: float32 [8, 1, 480, 3840], P('rep', None, 'grp'), may hold values from -0.0009765625 to 0.0009765625
- err_down: float32 [8, 1, 1920, 480], P('rep', None, 'grp'), may hold values from -0.0009765625 to 0.0009765625
- q_d: float32 [1, 3840, 8], replicated, may hold values from -5 to 5
- q_down: float32 [1, 480, 8], replicated, may hold values from -5 to 5
- vectors: float32 [1, 6240], replicated
- vec_mom: float32 [1, 6240], replicated, may hold values from -0.00021362305 to 0.00021362305
- final_norm: float32 [2, 480], replicated
- final_mom: float32 [2, 480], replicated, may hold values from -0.00021362305 to 0.00021362305
- embed: float32 [33, 480], replicated, may hold values from -5 to 5
- embed_mom: float32 [33, 480], replicated, may hold values from -9.1552734e-05 to 9.1552734e-05
- head: float32 [481, 33], replicated, may hold values from -0.25 to 0.25
- head_mom: float32 [481, 33], replicated, may hold values from -9.1552734e-05 to 9.1552734e-05
Outputs:
- loss_sum: float32 [], replicated
- count: float32 [], replicated
- grad_norm: float32 [], replicated
- new_mats_d: float32 [1, 480, 3840], P(None, 'grp')
- new_mats_down: float32 [1, 1920, 480], P(None, 'grp')
- new_mom_d: float32 [1, 480, 3840], P(None, 'grp')
- new_mom_down: float32 [1, 1920, 480], P(None, 'grp')
- new_err_d: float32 [8, 1, 480, 3840], P('rep', None, 'grp')
- new_err_down: float32 [8, 1, 1920, 480], P('rep', None, 'grp')
- p_d: float32 [1, 480, 8], P(None, 'grp')
- p_down: float32 [1, 1920, 8], P(None, 'grp')
- new_q_d: float32 [1, 3840, 8], replicated
- new_q_down: float32 [1, 480, 8], replicated
- new_vectors: float32 [1, 6240], replicated
- new_vec_mom: float32 [1, 6240], replicated
- new_final_norm: float32 [2, 480], replicated
- new_final_mom: float32 [2, 480], replicated
- new_embed: float32 [33, 480], replicated
- new_embed_mom: float32 [33, 480], replicated
- new_head: float32 [481, 33], replicated
- new_head_mom: float32 [481, 33], replicated
Inputs may be any that keep to these rules, and one draw needn't show every extreme that they name: `mask`: position 0 of every sequence counts.
All inputs are finite; a program needn't handle non-finite values.
Results may differ from a plain program's by a relative error of at most 0.015.
The roundings to bfloat16 on the way count: a program that leaves them out, or rounds other values in their place, can miss the bound.
Values may be sent and summed in bfloat16 or wider, within the bound.
No kernel may reach another device: no remote copies, remote signals or barrier semaphores. Data moves between devices by JAX's collectives and lax.ppermute only.
A program may use at most 320 MiB of HBM per device.

v0:
```python
from functools import partial

import jax
import jax.numpy as jnp
from jax import lax
from jax.sharding import PartitionSpec as P

D = 480
HEADS = 20
HDIM = 24
V = 33


EPS = 1e-05
BETA = 0.9
RATE_WIDE = 20000.0
RATE_LOWER = 3000.0
RATE_VECTOR = 20000.0
RATE_FINAL = 40000.0
RATE_EMBED = 60000.0
RATE_HEAD = 3000.0
CLIP = 0.005
HIGHEST = lax.Precision.HIGHEST


def to_half(value):
    return value.astype(jnp.bfloat16)


def product(left, right):
    return jnp.dot(left, right, preferred_element_type=jnp.float32)


def product_left(left, right):
    return lax.dot_general(
        left, right, (((0,), (0,)), ((), ())), preferred_element_type=jnp.float32
    )


def product_right(left, right):
    return lax.dot_general(
        left, right, (((1,), (1,)), ((), ())), preferred_element_type=jnp.float32
    )


def exact_einsum(form, first, second):
    return jnp.einsum(form, first, second, precision=HIGHEST)


def layer_norm(value, gain, shift):
    center = value - jnp.mean(value, -1, keepdims=True)
    spread = jnp.mean(center * center, -1, keepdims=True)
    return center * lax.rsqrt(spread + EPS) * gain + shift


def tables(length, width):
    half = width // 2
    freq = 10000.0 ** (-jnp.arange(half, dtype=jnp.float32) * 2.0 / width)
    angle = jnp.arange(length, dtype=jnp.float32)[:, None] * freq[None, :]
    angle = jnp.concatenate([angle, angle], -1)
    return (jnp.cos(angle), jnp.sin(angle))


def rotary(value, cosine, sine):
    half = value.shape[-1] // 2
    turned = jnp.concatenate([-value[..., half:], value[..., :half]], -1)
    return value * cosine[:, None, :] + turned * sine[:, None, :]


def heads_of(cosine, sine, act):
    length = act.shape[0]
    query = rotary(act[:, :D].reshape(length, HEADS, HDIM), cosine, sine) * HDIM ** (-0.5)
    keys = rotary(act[:, D : 2 * D].reshape(length, HEADS, HDIM), cosine, sine)
    values = act[:, 2 * D : 3 * D].reshape(length, HEADS, HDIM)
    return (query, keys, values)


def attend(query, keys, values):
    length = query.shape[0]
    block = min(length, 512)

    def one_block(piece):
        scores = jnp.einsum("qhe,khe->hqk", piece, keys, preferred_element_type=jnp.float32)
        top = jnp.max(scores, -1, keepdims=True)
        expo = jnp.exp(scores - top)
        total = jnp.sum(expo, -1, keepdims=True)
        mixed = jnp.einsum(
            "hqk,khe->qhe", to_half(expo / total), values, preferred_element_type=jnp.float32
        )
        return (mixed, (top + jnp.log(total))[..., 0])

    mixed, logsum = lax.map(one_block, query.reshape(length // block, block, HEADS, HDIM))
    return (mixed.reshape(length, D), logsum)


def attend_back(query, keys, values, logsum, grad_mixed):
    length = query.shape[0]
    block = min(length, 512)

    def one_block(carry, item):
        grad_keys, grad_values = carry
        piece, block_sum, grad_piece = item
        scores = jnp.einsum("qhe,khe->hqk", piece, keys, preferred_element_type=jnp.float32)
        probs = jnp.exp(scores - block_sum[..., None])
        grad_values = grad_values + jnp.einsum(
            "hqk,qhe->khe", to_half(probs), grad_piece, preferred_element_type=jnp.float32
        )
        grad_probs = jnp.einsum(
            "qhe,khe->hqk", grad_piece, values, preferred_element_type=jnp.float32
        )
        grad_scores = to_half(probs * (grad_probs - jnp.sum(grad_probs * probs, -1, keepdims=True)))
        grad_query = jnp.einsum(
            "hqk,khe->qhe", grad_scores, keys, preferred_element_type=jnp.float32
        )
        grad_keys = grad_keys + jnp.einsum(
            "hqk,qhe->khe", grad_scores, piece, preferred_element_type=jnp.float32
        )
        return ((grad_keys, grad_values), grad_query)

    blocks = length // block
    empty = jnp.zeros((length, HEADS, HDIM), jnp.float32)
    items = (
        query.reshape(blocks, block, HEADS, HDIM),
        logsum,
        grad_mixed.reshape(blocks, block, HEADS, HDIM),
    )
    (grad_keys, grad_values), grad_query = lax.scan(one_block, (empty, empty), items)
    return (grad_query.reshape(length, HEADS, HDIM), grad_keys, grad_values)


def layer_forward(resid, wide, down, vec, cosine, sine):
    normed = to_half(layer_norm(resid, vec[0:D], vec[D : 2 * D]))
    act = product(normed, wide[:, : 3 * D]) + vec[2 * D : 5 * D]
    query, keys, values = heads_of(cosine, sine, act)
    query, keys, values = (to_half(query), to_half(keys), to_half(values))
    mixed, logsum = attend(query, keys, values)
    mixed = to_half(mixed)
    middle = resid + product(mixed, wide[:, 3 * D : 4 * D]) + vec[5 * D : 6 * D]
    normed2 = to_half(layer_norm(middle, vec[6 * D : 7 * D], vec[7 * D : 8 * D]))
    upper = product(normed2, wide[:, 4 * D :]) + vec[9 * D :]
    hidden = to_half(jax.nn.gelu(upper, approximate=False))
    output = middle + product(hidden, down) + vec[8 * D : 9 * D]
    return (
        output,
        (resid, normed, query, keys, values, logsum, mixed, middle, normed2, upper, hidden),
    )


def feed_back(grad_out, kept, wide, down, vec):
    middle, normed2, upper, hidden = (kept[7], kept[8], kept[9], kept[10])
    grad_y = to_half(grad_out)
    grad_lower = product_left(hidden, grad_y)
    grad_hidden = product_right(grad_y, down)
    _, gelu_pull = jax.vjp(partial(jax.nn.gelu, approximate=False), upper)
    grad_upper = to_half(gelu_pull(grad_hidden)[0])
    grad_up = product_left(normed2, grad_upper)
    grad_normed = product_right(grad_upper, wide[:, 4 * D :])
    _, norm_pull = jax.vjp(layer_norm, middle, vec[6 * D : 7 * D], vec[7 * D : 8 * D])
    grad_mid, grad_gain, grad_shift = norm_pull(grad_normed)
    parts = (
        grad_gain,
        grad_shift,
        jnp.sum(grad_y.astype(jnp.float32), 0),
        jnp.sum(grad_upper.astype(jnp.float32), 0),
    )
    return (grad_mid + grad_out, grad_lower, grad_up, parts)


def attention_back(grad_mid, kept, wide, vec, cosine, sine):
    resid, normed, query, keys, values, logsum, mixed = kept[:7]
    length = resid.shape[0]
    grad_branch = to_half(grad_mid)
    grad_out_w = product_left(mixed, grad_branch)
    grad_mixed = to_half(product_right(grad_branch, wide[:, 3 * D : 4 * D]))
    grads = attend_back(query, keys, values, logsum, grad_mixed)
    _, heads_pull = jax.vjp(
        partial(heads_of, cosine, sine), jnp.zeros((length, 3 * D), jnp.float32)
    )
    grad_act = to_half(heads_pull(grads)[0])
    grad_in_w = product_left(normed, grad_act)
    grad_normed = product_right(grad_act, wide[:, : 3 * D])
    _, norm_pull = jax.vjp(layer_norm, resid, vec[0:D], vec[D : 2 * D])
    grad_resid, grad_gain, grad_shift = norm_pull(grad_normed)
    parts = (
        grad_gain,
        grad_shift,
        jnp.sum(grad_act.astype(jnp.float32), 0),
        jnp.sum(grad_branch.astype(jnp.float32), 0),
    )
    return (grad_resid + grad_mid, grad_in_w, grad_out_w, parts)


def masked_loss(picks, weight_mask, logits):
    shifted = logits - jnp.max(logits, -1, keepdims=True)
    logp = shifted - jnp.log(jnp.sum(jnp.exp(shifted), -1, keepdims=True))
    return -jnp.sum(jnp.sum(logp * picks, -1) * weight_mask)


def gram_of(sketch):
    return exact_einsum("lrk,lrj->lkj", sketch, sketch)


def basis_of(sketch, gram):
    lower = jnp.linalg.cholesky(gram)
    return lax.linalg.triangular_solve(lower, sketch, left_side=False, lower=True, transpose_a=True)


def renew(weight, moment, grad, scale, rate):
    new_moment = BETA * moment + scale * grad
    return (weight - rate * new_moment, new_moment)


def shards(
    tokens,
    mask,
    targets,
    mats_d,
    mats_down,
    mom_d,
    mom_down,
    err_d,
    err_down,
    q_d,
    q_down,
    vectors,
    vec_mom,
    final_norm,
    final_mom,
    embed,
    embed_mom,
    head,
    head_mom,
):
    wide_all, down_all = (
        lax.all_gather(to_half(mats_d), "grp", axis=1, tiled=True),
        lax.all_gather(to_half(mats_down), "grp", axis=1, tiled=True),
    )
    token_ids = tokens[0]
    length = token_ids.shape[0]
    cosine, sine = tables(length, HDIM)
    onehot = (token_ids[:, None] == jnp.arange(V, dtype=jnp.int32)[None, :]).astype(jnp.float32)
    resid = exact_einsum("tv,vd->td", onehot, embed)
    layers = wide_all.shape[0]
    index = 0
    resid, kept = layer_forward(
        resid, wide_all[index], down_all[index], vectors[index], cosine, sine
    )
    kept_all = [kept]
    table_half = to_half(head[:D])
    final_half = to_half(layer_norm(resid, final_norm[0], final_norm[1]))
    logits = product(final_half, table_half) + head[D]
    weight_mask = mask[0].astype(jnp.float32)
    picks = (targets[0][:, None] == jnp.arange(V, dtype=jnp.int32)[None, :]).astype(jnp.float32)
    local_loss, loss_pull = jax.vjp(partial(masked_loss, picks, weight_mask), logits)
    loss_sum, count = lax.psum((local_loss, jnp.sum(weight_mask)), ("rep", "grp"))
    grad_logits = to_half(loss_pull(1.0 / count)[0])
    grad_head = jnp.concatenate(
        [product_left(final_half, grad_logits), jnp.sum(grad_logits.astype(jnp.float32), 0)[None]],
        0,
    )
    _, final_pull = jax.vjp(layer_norm, resid, final_norm[0], final_norm[1])
    grad_resid, grad_fgain, grad_fshift = final_pull(product_right(grad_logits, table_half))
    grad_final = jnp.stack([grad_fgain, grad_fshift])
    wide_grads = [None] * layers
    down_grads = [None] * layers
    vec_grads = [None] * layers
    for index in reversed(range(layers)):
        kept = kept_all[index]
        grad_mid, grad_lower, grad_up, feed_parts = feed_back(
            grad_resid, kept, wide_all[index], down_all[index], vectors[index]
        )
        grad_resid, grad_in_w, grad_out_w, attn_parts = attention_back(
            grad_mid, kept, wide_all[index], vectors[index], cosine, sine
        )
        wide_grads[index] = jnp.concatenate([grad_in_w, grad_out_w, grad_up], 1)
        down_grads[index] = grad_lower
        vec_grads[index] = jnp.concatenate(attn_parts + feed_parts)
    grad_wide = jnp.stack(wide_grads)
    grad_down = jnp.stack(down_grads)
    grad_vec = jnp.stack(vec_grads)
    grad_embed = exact_einsum("tv,td->vd", onehot, grad_resid)
    grad_wide, grad_down = (
        lax.psum_scatter(
            grad_wide.astype(jnp.bfloat16), "grp", scatter_dimension=1, tiled=True
        ).astype(jnp.float32),
        lax.psum_scatter(
            grad_down.astype(jnp.bfloat16), "grp", scatter_dimension=1, tiled=True
        ).astype(jnp.float32),
    )
    merged_wide = grad_wide + err_d[0]
    merged_down = grad_down + err_down[0]
    sketch_wide = exact_einsum("lrc,lck->lrk", merged_wide, q_d)
    sketch_down = exact_einsum("lrc,lck->lrk", merged_down, q_down)
    sketch_wide, sketch_down = lax.psum((sketch_wide, sketch_down), "rep")
    gram_wide, gram_down = lax.psum((gram_of(sketch_wide), gram_of(sketch_down)), "grp")
    basis_wide = basis_of(sketch_wide, gram_wide)
    basis_down = basis_of(sketch_down, gram_down)
    factor_wide = exact_einsum("lrc,lrk->lck", merged_wide, basis_wide)
    factor_down = exact_einsum("lrc,lrk->lck", merged_down, basis_down)
    factor_wide, factor_down, grad_vec, grad_final, grad_embed, grad_head = lax.psum(
        (factor_wide, factor_down, grad_vec, grad_final, grad_embed, grad_head), ("rep", "grp")
    )
    approx_wide = exact_einsum("lrk,lck->lrc", basis_wide, factor_wide)
    approx_down = exact_einsum("lrk,lck->lrc", basis_down, factor_down)
    replicas = lax.axis_size("rep")
    new_err_wide = (merged_wide - approx_wide / replicas)[None]
    new_err_down = (merged_down - approx_down / replicas)[None]
    side_square = (
        jnp.sum(grad_vec * grad_vec)
        + jnp.sum(grad_final * grad_final)
        + jnp.sum(grad_embed * grad_embed)
        + jnp.sum(grad_head * grad_head)
    )
    matrix_square = lax.psum(
        jnp.sum(approx_wide * approx_wide) + jnp.sum(approx_down * approx_down), "grp"
    )
    grad_norm = jnp.sqrt(matrix_square + side_square)
    scale = jnp.minimum(1.0, CLIP / grad_norm)
    new_wide, new_mom_wide = renew(mats_d, mom_d, approx_wide, scale, RATE_WIDE)
    new_down, new_mom_dn = renew(mats_down, mom_down, approx_down, scale, RATE_LOWER)
    new_vec, new_vmom = renew(vectors, vec_mom, grad_vec, scale, RATE_VECTOR)
    new_fin, new_fmom = renew(final_norm, final_mom, grad_final, scale, RATE_FINAL)
    new_emb, new_emom = renew(embed, embed_mom, grad_embed, scale, RATE_EMBED)
    new_head, new_hmom = renew(head, head_mom, grad_head, scale, RATE_HEAD)
    return (
        loss_sum,
        count,
        grad_norm,
        new_wide,
        new_down,
        new_mom_wide,
        new_mom_dn,
        new_err_wide,
        new_err_down,
        basis_wide,
        basis_down,
        factor_wide,
        factor_down,
        new_vec,
        new_vmom,
        new_fin,
        new_fmom,
        new_emb,
        new_emom,
        new_head,
        new_hmom,
    )


def solution(mesh):
    placed = (
        P(("rep", "grp"), None),
        P(("rep", "grp"), None),
        P(("rep", "grp"), None),
        P(None, "grp", None),
        P(None, "grp", None),
        P(None, "grp", None),
        P(None, "grp", None),
        P("rep", None, "grp", None),
        P("rep", None, "grp", None),
        P(),
        P(),
        P(),
        P(),
        P(),
        P(),
        P(),
        P(),
        P(),
        P(),
    )
    return jax.shard_map(
        shards,
        mesh=mesh,
        in_specs=placed,
        out_specs=(
            P(),
            P(),
            P(),
            P(None, "grp", None),
            P(None, "grp", None),
            P(None, "grp", None),
            P(None, "grp", None),
            P("rep", None, "grp", None),
            P("rep", None, "grp", None),
            P(None, "grp", None),
            P(None, "grp", None),
            P(),
            P(),
            P(),
            P(),
            P(),
            P(),
            P(),
            P(),
            P(),
            P(),
        ),
        check_vma=False,
    )
```

profile of v0, /device:TPU:0, one launch (start us, length us, event | category | flops | bytes accessed | tf_op | source)
XLA Modules:
  0.0 873.4 jit_solution(10041717550778009711)
XLA Ops:
  7.3 2.6 convert_element_type.111
  13.1 42.4 %psum.92 = f32[]{:T(128)} all-reduce(f32[]{:T(128)} %convert_reduce_fusion.6), channel_id=1, replica_groups=mesh['rep'=8,'grp'=4] {'rep','grp'}, use_global_device_ids=true, to_apply=%region_16.17 | all-reduce | flops 1 | bytes 8 | tf_op jit(solution)/shard_map/psum | solution.py:255
  58.3 2.1 fusion.82
  64.4 3.3 convolution_add_fusion
  67.9 2.4 fusion.104
  70.3 3.9 reshape.463
  74.2 1.9 fusion.107
  77.8 2.1 concatenate.50
  79.9 1.8 reshape.488
  81.7 3.6 fusion.47
  88.6 99.4 %while.27 = (s32[]{:T(128)}, bf16[2,512,20,24]{1,3,2,0:T(8,128)(2,1)}, f32[2,20,512]{2,1,0:T(8,128)S(1)}, bf16[2,512,20,24]{1,3,2,0:T(8,128)(2,1)S(1)}, bf16[102...) while((s32[]{:T(128)}, bf16[2,512,20,24]{1,3,2,0:T(8,128)(2,1)}, ...), condition=%wide.region_5.6_spmd, body=%wide.region_2.5_spmd.sunk | while | flops 1069537280 | bytes 137502864 | solution.py:92
  88.6 16.2 %fusion.168 = (f32[20,512]{1,0:T(8,128)S(1)}, f32[20,512,1024]{2,1,0:T(8,128)}) fusion(bf16[1024,20,24]{0,2,1:T(8,128)(2,1)S(1)} %get-tuple-element.469, bf16[2,512,20,24]{1,3,2,0:T(8,128)(2,1)S(1)} %get-tuple-element.468, s32[]{:T(128)S(6)} %copy.168), kind=kOutput, calls=%fused_computation.238.clone.1 | convolution fusion | flops 513792000 | bytes 43458564 | tf_op jit(solution)/shard_map/while/body/eval_jaxpr/qhe,khe->hqk/dot_general | solution.py:83
  104.8 17.5 %fusion.169 = f32[20,512]{1,0:T(8,128)S(1)} fusion(f32[20,512,1024]{2,1,0:T(8,128)} %get-tuple-element.438, f32[20,512]{1,0:T(8,128)S(1)} %get-tuple-element.439), kind=kLoop, calls=%fused_computation.2.clone.1 | loop fusion | flops 20961280 | bytes 42024960 | tf_op jit(solution)/shard_map/while/body/eval_jaxpr/reduce_sum | solution.py:86
  122.3 15.0 %fusion.170 = bf16[2,512,20,24]{1,3,2,0:T(8,128)(2,1)S(1)} fusion(bf16[2,512,20,24]{1,3,2,0:T(8,128)(2,1)S(1)} %copy-done.31, s32[]{:T(128)S(6)} %copy.168, bf16[1024,20,24]{0,2,1:T(8,128)(2,1)S(1)} %get-tuple-element.470, f32[20,512,1024]{2,1,0:T(8,128)} %get-tuple-element.438, f32[20,512]{1,0:T(8,128)S(1)} %fusion.169, ...), kind=kOutput, calls=%fused_computation.5.clone.1 | convolution fusion | flops 534773760 | bytes 44007428 | tf_op jit(solution)/shard_map/while/body/eval_jaxpr/hqk,khe->qhe/dot_general | solution.py:87
  138.3 16.2 %fusion.168 = (f32[20,512]{1,0:T(8,128)S(1)}, f32[20,512,1024]{2,1,0:T(8,128)}) fusion(bf16[1024,20,24]{0,2,1:T(8,128)(2,1)S(1)} %get-tuple-element.469, bf16[2,512,20,24]{1,3,2,0:T(8,128)(2,1)S(1)} %get-tuple-element.468, s32[]{:T(128)S(6)} %copy.168), kind=kOutput, calls=%fused_computation.238.clone.1 | convolution fusion | flops 513792000 | bytes 43458564 | tf_op jit(solution)/shard_map/while/body/eval_jaxpr/qhe,khe->hqk/dot_general | solution.py:83
  154.6 17.5 %fusion.169 = f32[20,512]{1,0:T(8,128)S(1)} fusion(f32[20,512,1024]{2,1,0:T(8,128)} %get-tuple-element.438, f32[20,512]{1,0:T(8,128)S(1)} %get-tuple-element.439), kind=kLoop, calls=%fused_computation.2.clone.1 | loop fusion | flops 20961280 | bytes 42024960 | tf_op jit(solution)/shard_map/while/body/eval_jaxpr/reduce_sum | solution.py:86
  172.0 15.0 %fusion.170 = bf16[2,512,20,24]{1,3,2,0:T(8,128)(2,1)S(1)} fusion(bf16[2,512,20,24]{1,3,2,0:T(8,128)(2,1)S(1)} %copy-done.31, s32[]{:T(128)S(6)} %copy.168, bf16[1024,20,24]{0,2,1:T(8,128)(2,1)S(1)} %get-tuple-element.470, f32[20,512,1024]{2,1,0:T(8,128)} %get-tuple-element.438, f32[20,512]{1,0:T(8,128)S(1)} %fusion.169, ...), kind=kOutput, calls=%fused_computation.5.clone.1 | convolution fusion | flops 534773760 | bytes 44007428 | tf_op jit(solution)/shard_map/while/body/eval_jaxpr/hqk,khe->qhe/dot_general | solution.py:87
  188.1 3.0 copy.74
  191.3 2.4 fusion.112
  194.6 22.8 %multiply_convert_fusion.1 = (bf16[1024,1920]{1,0:T(8,128)(2,1)}, f32[1024,1920]{1,0:T(8,128)}, f32[1024,1920]{1,0:T(8,128)}) fusion(f32[1920]{0:T(1024)S(1)} %copy-done.95, bf16[480,3840]{1,0:T(8,128)(2,1)S(1)} %bitcast.279, f32[1024,480]{0,1:T(8,128)S(1)} %get-tuple-element.333, f32[480]{0:T(512)S(1)} %bitcast.306, f32[480]{0:T(512)S(1)} %bitcast.300, ...), kind=kOutput, calls=%fused_computation.39 | convolution fusion | flops 2019655680 | bytes 23490560 | tf_op jit(solution)/shard_map/dot_general | solution.py:31
  217.5 5.0 fusion.113
  229.8 3.4 fusion.36
  233.3 7.8 convert_reduce_fusion
  241.0 3.2 multiply_reduce_fusion.3
  249.6 8.9 %copy.86 = bf16[1,1920,480]{2,0,1:T(2,128)(2,1)} copy(bf16[1,1920,480]{1,2,0:T(8,128)(2,1)} %fusion.36) | data formatting | bytes 3686400
  258.5 4.0 copy.159
  264.1 284.2 %while.28 = (s32[]{:T(128)}, f32[1024,20,24]{0,2,1:T(8,128)S(1)}, f32[1024,20,24]{0,2,1:T(8,128)}, f32[2,512,20,24]{1,0,3,2:T(2,128)}, bf16[2,512,20,24]{1,3,2,0...) while((s32[]{:T(128)}, f32[1024,20,24]{0,2,1:T(8,128)S(1)}, ...), condition=%wide.region_26.27_spmd.clone, body=%wide.region_24.26_spmd.clone.sunk | while | flops 2612910080 | bytes 336486560 | solution.py:127
  264.3 18.2 %fusion.180 = f32[20,512,1024]{2,1,0:T(8,128)} fusion(bf16[1024,20,24]{0,2,1:T(8,128)(2,1)S(1)} %get-tuple-element.499, bf16[2,512,20,24]{1,3,2,0:T(8,128)(2,1)} %get-tuple-element.498, s32[]{:T(128)S(6)} %copy.178), kind=kOutput, calls=%fused_computation.24.clone.1 | convolution fusion | flops 503316480 | bytes 43417604 | tf_op jit(solution)/shard_map/while/body/eval_jaxpr/qhe,khe->hqk/dot_general | solution.py:103
  282.5 17.7 %bitcast_add_fusion.17 = f32[1024,20,24]{0,2,1:T(8,128)} fusion(f32[1024,20,24]{0,2,1:T(8,128)} %get-tuple-element.485, f32[20,512,1024]{2,1,0:T(8,128)} %fusion.180, f32[20,512]{1,0:T(8,128)S(1)} %dynamic-slice_bitcast_fusion.2, pred[]{:T(512)S(6)} %compare.37, bf16[2,512,20,24]{1,3,2,0:T(8,128)(2,1)} %get-tuple-element.501, s32[]{:T(128)S(6)} %copy.178), kind=kOutput, calls=%fused_computation.17.clone.1 | convolution fusion | flops 525271040 | bytes 46407684 | tf_op jit(solution)/shard_map/while/body/eval_jaxpr/hqk,qhe->khe/dot_general | solution.py:105
  300.2 27.7 %multiply_reduce_fusion.18 = (f32[20,512]{1,0:T(8,128)S(1)}, f32[20,512,1024]{2,1,0:T(8,128)}) fusion(f32[20,512,1024]{2,1,0:T(8,128)} %fusion.180, f32[20,512]{1,0:T(8,128)S(1)} %dynamic-slice_bitcast_fusion.2, bf16[1024,20,24]{0,2,1:T(8,128)(2,1)} %get-tuple-element.502, bf16[2,512,20,24]{1,3,2,0:T(8,128)(2,1)} %get-tuple-element.501, s32[]{:T(128)S(6)} %copy.178), kind=kOutput, calls=%fused_computation.12.clone.1 | convolution fusion | flops 534763520 | bytes 85442560 | tf_op jit(solution)/shard_map/while/body/eval_jaxpr/qhe,khe->hqk/dot_general | solution.py:108
  328.0 34.0 %multiply_convert_fusion.3 = bf16[20,512,1024]{2,1,0:T(8,128)(2,1)} fusion(f32[20,512,1024]{2,1,0:T(8,128)} %get-tuple-element.449, f32[20,512,1024]{2,1,0:T(8,128)} %fusion.180, f32[20,512]{1,0:T(8,128)S(1)} %get-tuple-element.450, f32[20,512]{1,0:T(8,128)S(1)} %dynamic-slice_bitcast_fusion.2), kind=kLoop, calls=%fused_computation.11.clone.1 | loop fusion | flops 41943040 | bytes 104939520 | tf_op jit(solution)/shard_map/while/body/eval_jaxpr/convert_element_type | solution.py:27
  362.0 9.9 %convolution_bitcast_fusion.6 = f32[1,512,20,24]{1,3,2,0:T(8,128)S(1)} fusion(bf16[20,512,1024]{2,1,0:T(8,128)(2,1)} %multiply_convert_fusion.3, bf16[1024,20,24]{0,2,1:T(8,128)(2,1)S(1)} %get-tuple-element.499), kind=kOutput, calls=%fused_computation.19.clone.1 | convolution fusion | flops 503316480 | bytes 22937600 | tf_op jit(solution)/shard_map/while/body/eval_jaxpr/hqk,khe->qhe/dot_general | solution.py:112
  371.9 8.5 bitcast_add_fusion.16
  380.4 2.0 copy.161
  382.3 24.0 %dynamic_update_slice.19 = f32[2,512,20,24]{1,0,3,2:T(2,128)} dynamic-update-slice(f32[2,512,20,24]{1,0,3,2:T(2,128)} %get-tuple-element.486, f32[1,512,20,24]{1,0,3,2:T(1,128)} %copy.161, s32[]{:T(128)S(6)} %copy.178, s32[]{:T(128)} %constant.80.clone.1..sunk, s32[]{:T(128)} %constant.80.clone.1..sunk, s32[]{:T(128)} %constant.80.clone.1..sunk) | dynamic-update-slice | bytes 1966084 | tf_op jit(solution)/shard_map/while/body/jit(dynamic_update_index_in_dim)/dynamic_update_slice | solution.py:92
  406.3 17.4 %fusion.180 = f32[20,512,1024]{2,1,0:T(8,128)} fusion(bf16[1024,20,24]{0,2,1:T(8,128)(2,1)S(1)} %get-tuple-element.499, bf16[2,512,20,24]{1,3,2,0:T(8,128)(2,1)} %get-tuple-element.498, s32[]{:T(128)S(6)} %copy.178), kind=kOutput, calls=%fused_computation.24.clone.1 | convolution fusion | flops 503316480 | bytes 43417604 | tf_op jit(solution)/shard_map/while/body/eval_jaxpr/qhe,khe->hqk/dot_general | solution.py:103
  423.7 18.1 %bitcast_add_fusion.17 = f32[1024,20,24]{0,2,1:T(8,128)} fusion(f32[1024,20,24]{0,2,1:T(8,128)} %get-tuple-element.485, f32[20,512,1024]{2,1,0:T(8,128)} %fusion.180, f32[20,512]{1,0:T(8,128)S(1)} %dynamic-slice_bitcast_fusion.2, pred[]{:T(512)S(6)} %compare.37, bf16[2,512,20,24]{1,3,2,0:T(8,128)(2,1)} %get-tuple-element.501, s32[]{:T(128)S(6)} %copy.178), kind=kOutput, calls=%fused_computation.17.clone.1 | convolution fusion | flops 525271040 | bytes 46407684 | tf_op jit(solution)/shard_map/while/body/eval_jaxpr/hqk,qhe->khe/dot_general | solution.py:105
  441.8 27.7 %multiply_reduce_fusion.18 = (f32[20,512]{1,0:T(8,128)S(1)}, f32[20,512,1024]{2,1,0:T(8,128)}) fusion(f32[20,512,1024]{2,1,0:T(8,128)} %fusion.180, f32[20,512]{1,0:T(8,128)S(1)} %dynamic-slice_bitcast_fusion.2, bf16[1024,20,24]{0,2,1:T(8,128)(2,1)} %get-tuple-element.502, bf16[2,512,20,24]{1,3,2,0:T(8,128)(2,1)} %get-tuple-element.501, s32[]{:T(128)S(6)} %copy.178), kind=kOutput, calls=%fused_computation.12.clone.1 | convolution fusion | flops 534763520 | bytes 85442560 | tf_op jit(solution)/shard_map/while/body/eval_jaxpr/qhe,khe->hqk/dot_general | solution.py:108
  469.6 34.0 %multiply_convert_fusion.3 = bf16[20,512,1024]{2,1,0:T(8,128)(2,1)} fusion(f32[20,512,1024]{2,1,0:T(8,128)} %get-tuple-element.449, f32[20,512,1024]{2,1,0:T(8,128)} %fusion.180, f32[20,512]{1,0:T(8,128)S(1)} %get-tuple-element.450, f32[20,512]{1,0:T(8,128)S(1)} %dynamic-slice_bitcast_fusion.2), kind=kLoop, calls=%fused_computation.11.clone.1 | loop fusion | flops 41943040 | bytes 104939520 | tf_op jit(solution)/shard_map/while/body/eval_jaxpr/convert_element_type | solution.py:27
  503.6 9.9 %convolution_bitcast_fusion.6 = f32[1,512,20,24]{1,3,2,0:T(8,128)S(1)} fusion(bf16[20,512,1024]{2,1,0:T(8,128)(2,1)} %multiply_convert_fusion.3, bf16[1024,20,24]{0,2,1:T(8,128)(2,1)S(1)} %get-tuple-element.499), kind=kOutput, calls=%fused_computation.19.clone.1 | convolution fusion | flops 503316480 | bytes 22937600 | tf_op jit(solution)/shard_map/while/body/eval_jaxpr/hqk,khe->qhe/dot_general | solution.py:112
  513.5 8.5 bitcast_add_fusion.16
  522.0 2.0 copy.161
  523.9 24.0 %dynamic_update_slice.19 = f32[2,512,20,24]{1,0,3,2:T(2,128)} dynamic-update-slice(f32[2,512,20,24]{1,0,3,2:T(2,128)} %get-tuple-element.486, f32[1,512,20,24]{1,0,3,2:T(1,128)} %copy.161, s32[]{:T(128)S(6)} %copy.178, s32[]{:T(128)} %constant.80.clone.1..sunk, s32[]{:T(128)} %constant.80.clone.1..sunk, s32[]{:T(128)} %constant.80.clone.1..sunk) | dynamic-update-slice | bytes 1966084 | tf_op jit(solution)/shard_map/while/body/jit(dynamic_update_index_in_dim)/dynamic_update_slice | solution.py:92
  548.3 4.0 reshape.469
  552.3 1.7 broadcast_multiply_fusion
  560.4 1.9 copy-done.8
  562.4 3.0 fusion.34
  565.4 3.6 fusion.35
  569.0 6.6 concatenate.58
  577.7 4.1 multiply_reduce_fusion.1
  584.3 5.4 fusion.44
  593.3 24.2 %reduce-scatter.5.cloned.1.call-done = bf16[1,120,3840]{2,1,0:T(8,128)(2,1)} async-done(((bf16[1,480,3840]{2,1,0:T(8,128)(2,1)}), bf16[1,120,3840]{2,1,0:T(8,128)(2,1)}) %reduce-scatter.5.cloned.1.call-update) | async-done | bytes 921616 | tf_op jit(solution)/shard_map/reduce_scatter | solution.py:283
  617.6 2.7 fusion.50
  620.3 37.1 %all-reduce.8 = (f32[480,8]{0,1:T(8,128)S(1)}, f32[120,8]{0,1:T(8,128)S(1)}) all-reduce(f32[480,8]{0,1:T(8,128)S(1)} %fusion.64, f32[120,8]{0,1:T(8,128)S(1)} %fusion.50), channel_id=1, replica_groups=mesh['rep'=8,'grp'=4] {'rep'}, use_global_device_ids=true, to_apply=%region_35.37 | all-reduce | flops 4800 | bytes 38400 | tf_op jit(solution)/shard_map/psum | solution.py:294
  657.6 6.1 all-reduce.9
  669.5 1.9 convolution_bitcast_fusion.2
  671.5 41.1 %all-reduce.14 = (f32[]{:T(128)}, f32[1,480,8]{1,2,0:T(8,128)}, f32[1,6240]{1,0:T(1,128)S(1)}, f32[2,480]{1,0:T(2,128)S(1)}, f32[33,480]{1,0:T(8,128)S(1)}, /*index=5*/f32[481,33]{0,1:T(8,128)S(1)}) all-reduce(f32[]{:T(128)S(6)} %neg.58, ...), channel_id=1, replica_groups=mesh['rep'=8,'grp'=4] {'rep','grp'}, use_global_device_ids=true, to_apply=%region_14.15 | all-reduce | flops 42754 | bytes 342032 | tf_op jit(solution)/shard_map/psum | solution.py:255
  714.4 3.0 convolution_bitcast_fusion.1
  717.5 3.4 multiply_reduce_fusion.11
  723.5 115.4 %all-reduce.13.cloned.1.call-done = f32[1,3840,8]{1,2,0:T(8,128)} async-done(((f32[1,3840,8]{1,2,0:T(8,128)}), f32[1,3840,8]{1,2,0:T(8,128)}) %all-reduce.13.cloned.1.call-update) | async-done | bytes 122896 | tf_op jit(solution)/shard_map/psum | solution.py:300
  838.9 4.4 multiply_reduce_fusion.10
  845.2 7.5 psum.99
  856.8 4.2 multiply_subtract_fusion.1
  861.9 2.9 multiply_subtract_fusion
  (347 shorter events, 58.6 us)
Async XLA Ops:
  7.2 610.4 %copy-start = (f32[1,3840,8]{1,2,0:T(8,128)S(1)}, f32[1,3840,8]{1,2,0:T(8,128)}, u32[]{:S(2)}) copy-start(f32[1,3840,8]{1,2,0:T(8,128)} %param.33) | copy-start | bytes 368644
  7.2 57.2 %all-gather.3.cloned.1.call-start = ((), (), s32[]{:S(2)}) async-start(), calls=%async_computation.2 | async-start | bytes 4608000 | tf_op jit(solution)/shard_map/all_gather | solution.py:235
  9.9 47.7 %copy-start.83 = (f32[2,480]{1,0:T(2,128)S(1)}, f32[2,480]{1,0:T(2,128)}, u32[]{:S(2)}) copy-start(f32[2,480]{1,0:T(2,128)} %param.37) | copy-start | bytes 11524
  9.9 51.6 %copy-start.45 = (f32[33,480]{1,0:T(8,128)S(1)}, f32[33,480]{1,0:T(8,128)}, u32[]{:S(2)}) copy-start(f32[33,480]{1,0:T(8,128)} %param.39) | copy-start | bytes 190084
  9.9 51.6 %copy-start.76 = (s32[1,1024]{1,0:T(1,128)S(1)}, s32[1,1024]{1,0:T(1,128)}, u32[]{:S(2)}) copy-start(s32[1,1024]{1,0:T(1,128)} %param.24) | copy-start | bytes 12292
  9.9 207.5 %all-gather.5.cloned.1.call-start = ((), (), s32[]{:S(2)}) async-start(), calls=%async_computation.3 | async-start | bytes 2457600 | tf_op jit(solution)/shard_map/all_gather | solution.py:236
  10.8 578.9 %reduce-scatter.7.cloned.1.call-start = ((), (), s32[]{:S(2)}) async-start(), calls=%async_computation.6 | async-start | bytes 2457600
  11.5 52.2 %copy-start.68 = (f32[1,1024]{1,0:T(1,128)}, f32[1,1024]{1,0:T(1,128)S(1)}, u32[]{:S(2)}) copy-start(f32[1,1024]{1,0:T(1,128)S(1)} %convert_element_type.121) | copy-start | bytes 12292
  13.0 51.4 %copy-start.74 = (f32[1,480]{1,0:T(1,128)}, f32[1,480]{1,0:T(1,128)S(1)}, u32[]{:S(2)}) copy-start(f32[1,480]{1,0:T(1,128)S(1)} %get-tuple-element.325) | copy-start | bytes 5764
  13.0 51.4 %copy-start.99 = (f32[1,480]{1,0:T(1,128)}, f32[1,480]{1,0:T(1,128)S(1)}, u32[]{:S(2)}) copy-start(f32[1,480]{1,0:T(1,128)S(1)} %get-tuple-element.324) | copy-start | bytes 5764
  61.5 25.7 %copy-start.33 = (f32[1024,24]{0,1:T(8,128)}, f32[1024,24]{0,1:T(8,128)S(1)}, u32[]{:S(2)}) copy-start(f32[1024,24]{0,1:T(8,128)S(1)} %get-tuple-element.317) | copy-start | bytes 294916
  62.7 5.1 copy-start.53
  63.8 4.0 copy-start.62
  63.8 4.0 copy-start.56
  104.8 17.5 %copy-start.31 = (bf16[2,512,20,24]{1,3,2,0:T(8,128)(2,1)S(1)}, bf16[2,512,20,24]{1,3,2,0:T(8,128)(2,1)}, u32[]{:S(2)}) copy-start(bf16[2,512,20,24]{1,3,2,0:T(8,128)(2,1)} %get-tuple-element.459) | copy-start | bytes 2949124 | tf_op jit(solution)/shard_map/while
  154.5 17.5 %copy-start.31 = (bf16[2,512,20,24]{1,3,2,0:T(8,128)(2,1)S(1)}, bf16[2,512,20,24]{1,3,2,0:T(8,128)(2,1)}, u32[]{:S(2)}) copy-start(bf16[2,512,20,24]{1,3,2,0:T(8,128)(2,1)} %get-tuple-element.459) | copy-start | bytes 2949124 | tf_op jit(solution)/shard_map/while
  188.1 3.2 copy-start.2
  188.1 3.2 copy-start.3
  188.1 3.2 copy-start.7
  188.1 3.3 copy-start.93
  191.3 2.8 copy-start.58
  193.8 50.5 %copy-start.12 = (f32[1024,480]{0,1:T(8,128)}, f32[1024,480]{0,1:T(8,128)S(1)}, u32[]{:S(2)}) copy-start(f32[1024,480]{0,1:T(8,128)S(1)} %get-tuple-element.333) | copy-start | bytes 5898244
  193.8 50.4 %copy-start.70 = (f32[1024]{0:T(1024)}, f32[1024]{0:T(1024)S(1)}, u32[]{:S(2)}) copy-start(f32[1024]{0:T(1024)S(1)} %broadcast_multiply_fusion.7) | copy-start | bytes 12292
  194.1 50.1 %copy-start.85 = (f32[1024]{0:T(1024)}, f32[1024]{0:T(1024)S(1)}, u32[]{:S(2)}) copy-start(f32[1024]{0:T(1024)S(1)} %fusion.96) | copy-start | bytes 12292
  194.6 22.9 %copy-start.103 = (f32[1,480]{1,0:T(1,128)S(1)}, f32[1,480]{1,0:T(1,128)}, u32[]{:S(2)}) copy-start(f32[1,480]{1,0:T(1,128)} %get-tuple-element.320) | copy-start | bytes 5764
  223.7 3.3 copy-start.17
  227.0 2.8 copy-start.109
  227.5 17.4 %copy-start.9 = (f32[1024,480]{0,1:T(8,128)}, f32[1024,480]{0,1:T(8,128)S(1)}, u32[]{:S(2)}) copy-start(f32[1024,480]{0,1:T(8,128)S(1)} %get-tuple-element.295) | copy-start | bytes 5898244
  227.5 17.4 %copy-start.51 = (f32[1024]{0:T(1024)}, f32[1024]{0:T(1024)S(1)}, u32[]{:S(2)}) copy-start(f32[1024]{0:T(1024)S(1)} %negate_multiply_fusion.3) | copy-start | bytes 12292
  227.5 5.7 slice-start
  229.8 3.5 copy-start.106
  229.8 3.5 slice-start.1
  233.3 7.8 copy-start.59
  241.0 3.2 copy-start.107
  262.5 355.0 %reduce-scatter.5.cloned.1.call-start = ((), (), s32[]{:S(2)}) async-start(), calls=%async_computation.4 | async-start | bytes 4608000 | tf_op jit(solution)/shard_map/reduce_scatter | solution.py:283
  362.0 9.9 %copy-start.4 = (bf16[2,512,20,24]{1,3,2,0:T(8,128)(2,1)S(1)}, bf16[2,512,20,24]{1,3,2,0:T(8,128)(2,1)}, u32[]{:S(2)}) copy-start(bf16[2,512,20,24]{1,3,2,0:T(8,128)(2,1)} %get-tuple-element.498) | copy-start | bytes 2949124 | tf_op jit(solution)/shard_map/while
  503.6 9.9 %copy-start.4 = (bf16[2,512,20,24]{1,3,2,0:T(8,128)(2,1)S(1)}, bf16[2,512,20,24]{1,3,2,0:T(8,128)(2,1)}, u32[]{:S(2)}) copy-start(bf16[2,512,20,24]{1,3,2,0:T(8,128)(2,1)} %get-tuple-element.498) | copy-start | bytes 2949124 | tf_op jit(solution)/shard_map/while
  548.3 4.0 copy-start.44
  559.7 5.7 copy-start.27
  562.3 3.1 copy-start.13
  562.3 3.1 copy-start.71
  562.3 3.1 copy-start.86
  562.3 3.1 copy-start.90
  562.3 3.1 copy-start.98
  562.4 3.1 copy-start.108
  575.7 263.2 %all-reduce.13.cloned.1.call-start = ((), (), s32[]{:S(2)}) async-start(), calls=%async_computation.5 | async-start | bytes 245760 | tf_op jit(solution)/shard_map/psum | solution.py:300
  577.7 4.1 copy-start.67
  584.3 8.1 copy-start.16
  584.3 8.1 copy-start.78
  589.7 27.9 %copy-start.15 = (f32[1,1,120,3840]{3,2,1,0:T(8,128)S(1)}, f32[1,1,120,3840]{3,2,1,0:T(8,128)}, u32[]{:S(2)}) copy-start(f32[1,1,120,3840]{3,2,1,0:T(8,128)} %param.31) | copy-start | bytes 5529604
  666.7 50.8 %copy-start.55 = (f32[480,8]{0,1:T(8,128)}, f32[480,8]{0,1:T(8,128)S(1)}, u32[]{:S(2)}) copy-start(f32[480,8]{0,1:T(8,128)S(1)} %fusion.89) | copy-start | bytes 46084
  671.5 167.4 %copy-start.79 = (f32[120,8]{0,1:T(8,128)}, f32[120,8]{0,1:T(8,128)S(1)}, u32[]{:S(2)}) copy-start(f32[120,8]{0,1:T(8,128)S(1)} %fusion.91) | copy-start | bytes 11524
  717.5 136.0 %copy-start.84 = (f32[2,480]{1,0:T(2,128)S(1)}, f32[2,480]{1,0:T(2,128)}, u32[]{:S(2)}) copy-start(f32[2,480]{1,0:T(2,128)} %param.37) | copy-start | bytes 11524
  717.5 137.3 %copy-start.48 = (f32[1,6240]{1,0:T(1,128)S(1)}, f32[1,6240]{1,0:T(1,128)}, u32[]{:S(2)}) copy-start(f32[1,6240]{1,0:T(1,128)} %param.35) | copy-start | bytes 74884
  717.5 137.3 %copy-start.73 = (f32[1,6240]{1,0:T(1,128)S(1)}, f32[1,6240]{1,0:T(1,128)}, u32[]{:S(2)}) copy-start(f32[1,6240]{1,0:T(1,128)} %param.36) | copy-start | bytes 74884
  717.5 137.9 %copy-start.38 = (f32[481,33]{0,1:T(8,128)S(1)}, f32[481,33]{0,1:T(8,128)}, u32[]{:S(2)}) copy-start(f32[481,33]{0,1:T(8,128)} %param.41) | copy-start | bytes 190480
  717.5 137.9 %copy-start.49 = (f32[481,33]{0,1:T(8,128)S(1)}, f32[481,33]{0,1:T(8,128)}, u32[]{:S(2)}) copy-start(f32[481,33]{0,1:T(8,128)} %param.42) | copy-start | bytes 190480
  717.5 138.6 %copy-start.46 = (f32[33,480]{1,0:T(8,128)S(1)}, f32[33,480]{1,0:T(8,128)}, u32[]{:S(2)}) copy-start(f32[33,480]{1,0:T(8,128)} %param.39) | copy-start | bytes 190084
  717.5 138.6 %copy-start.50 = (f32[33,480]{1,0:T(8,128)S(1)}, f32[33,480]{1,0:T(8,128)}, u32[]{:S(2)}) copy-start(f32[33,480]{1,0:T(8,128)} %param.40) | copy-start | bytes 190084
  856.8 4.2 copy-start.20
  856.8 4.2 copy-start.22
  856.8 4.2 copy-start.23
  856.8 5.1 copy-start.28
  861.9 2.9 copy-start.42
  (56 other events, 80.8 us)
Sparse Core Ops, SparseCore 0:
  10.2 34.7 all-gather.2
  47.1 21.8 all-gather.4
  262.7 30.6 reduce-scatter.6
  575.8 41.7 reduce-scatter.4
  717.7 121.1 all-reduce.12
where the time goes:
time: 888 us; the launch traced here: 873 us
  matrix products  312 us (35%)
  other arithmetic  148 us (17%)
  waiting for transfers between devices  140 us (16%)
  blocking collectives  134 us (15%)
  local copies, waits for them, and re-layouts  116 us (13%)
  between operations  22.4 us (3%)
    psum x1, waiting for transfers between devices, shards(): lax.psum((factor_wide, factor_down, grad_vec, grad_final, grad_embed, gra...  115 us
    psum x2, blocking collectives, shards(): lax.psum((local_loss, jnp.sum(weight_mask)), ('rep', 'grp'))  83.5 us
    convert_element_type x7, other arithmetic, to_half(): return value.astype(jnp.bfloat16)  76 us
    dot_general x4, matrix products, one_block(): jnp.einsum('qhe,khe->hqk', piece, keys, preferred_element_type=jnp.float32)  68.1 us
    dot_general x2, matrix products, one_block(): jnp.einsum('qhe,khe->hqk', grad_piece, values, preferred_element_type=jnp...  55.5 us
    dynamic_update_slice x4, local copies, waits for them, and re-layouts, attend(): lax.map(one_block, query.reshape(length // block, block, HEADS, HDIM))  51.9 us
    psum x1, blocking collectives, shards(): sketch_wide, sketch_down = lax.psum((sketch_wide, sketch_down), 'rep')  37.1 us
    dot_general x2, matrix products, one_block(): jnp.einsum('hqk,qhe->khe', to_half(probs), grad_piece, preferred_element_...  35.8 us
  transfers between devices with their start and end apart: 5, of which 2 were waited for; matrix products, arithmetic and copies ran while one was open for 55% of the time, Pallas kernels for 0%

commit v1 on v0

v1 whole, which is shorter than its diff:
```python
from functools import partial

import jax
import jax.numpy as jnp
import numpy as np
from jax import lax
from jax.experimental import pallas as pl
from jax.experimental.pallas import tpu as pltpu
from jax.sharding import PartitionSpec as P

D = 480
HEADS = 20
HDIM = 24
V = 33
PAD = 32
TOK = 40
WIDE = 512
EPS = 1e-05
BETA = 0.9
RATE_WIDE = 20000.0
RATE_LOWER = 3000.0
RATE_VECTOR = 20000.0
RATE_FINAL = 40000.0
RATE_EMBED = 60000.0
RATE_HEAD = 3000.0
CLIP = 0.005
F32 = jnp.float32
B16 = jnp.bfloat16
MIB = 2**20


def params(limit=56):
    return pltpu.CompilerParams(vmem_limit_bytes=limit * MIB)


def nn(left, right):
    return jnp.dot(left, right, preferred_element_type=F32)


def nt(left, right):
    return lax.dot_general(left, right, (((1,), (1,)), ((), ())), preferred_element_type=F32)


def tn(left, right):
    return lax.dot_general(left, right, (((0,), (0,)), ((), ())), preferred_element_type=F32)


def thirds(value):
    top = value.astype(B16)
    rest = value - top.astype(F32)
    middle = rest.astype(B16)
    return top, middle, (rest - middle.astype(F32)).astype(B16)


def thirds_rows(value):
    return jnp.concatenate([part.astype(F32) for part in thirds(value)], 0).astype(B16)


def fold_rows(value):
    return value[0:8] + value[8:16] + value[16:24]


def exact_nt(left, right):
    return lax.dot_general(
        left, right, (((1,), (1,)), ((), ())),
        precision=lax.Precision.HIGHEST, preferred_element_type=F32,
    )


def exact_nn(left, right):
    return jnp.dot(left, right, precision=lax.Precision.HIGHEST, preferred_element_type=F32)


def norm_parts(value):
    center = value - jnp.mean(value, -1, keepdims=True)
    spread = jnp.mean(center * center, -1, keepdims=True)
    rstd = lax.rsqrt(spread + EPS)
    return center * rstd, rstd


def norm_back(grad, unit, rstd, gain):
    inner = grad * gain
    first = jnp.mean(inner, -1, keepdims=True)
    second = jnp.mean(inner * unit, -1, keepdims=True)
    return (
        rstd * (inner - first - unit * second),
        jnp.sum(grad * unit, 0, keepdims=True),
        jnp.sum(grad, 0, keepdims=True),
    )


def half_turn(value):
    return jnp.concatenate([value[HDIM // 2 :], value[: HDIM // 2]], 0)


def tail(rows, cols, ones):
    index = lax.broadcasted_iota(jnp.int32, (rows, cols), 0)
    return jnp.where(index < ones, 1.0, 0.0).astype(F32)


def lane_tail(rows, cols):
    index = lax.broadcasted_iota(jnp.int32, (rows, cols), 1)
    return jnp.where(index == 0, 1.0, 0.0).astype(F32)


def tables(length):
    half = HDIM // 2
    freq = np.float32(10000.0) ** (-np.arange(half, dtype=np.float32) * np.float32(2.0) / np.float32(HDIM))
    angle = np.arange(length, dtype=np.float32)[None, :] * freq.astype(np.float32)[:, None]
    cosine, sine = np.cos(angle), np.sin(angle)
    return (
        jnp.asarray(np.concatenate([cosine, cosine], 0), F32),
        jnp.asarray(np.concatenate([-sine, sine], 0), F32),
    )


def error_kernel(group, err_ref, errd_ref, q_ref, qd_ref, out_ref, row_ref):
    rows = err_ref.shape[0]
    out_ref[...] = jnp.zeros_like(out_ref)
    row_ref[...] = jnp.zeros_like(row_ref)
    row_ref[:, 0:rows] = exact_nt(q_ref[...], err_ref[...])
    out_ref[0:8, :] = pltpu.roll(row_ref[...], rows * group[0], 1)
    start = pl.multiple_of(8 + 8 * group[0], 8)
    out_ref[pl.ds(start, 8), 0:D] = exact_nt(qd_ref[...], errd_ref[...])


def embed_kernel(tok_ref, emb_ref, w_ref, vec_ref, bias_ref, cos_ref, sin_ref,
                 x_ref, h_ref, q_ref, k_ref, v_ref, emb_s):
    step = tok_ref.shape[1]

    @pl.when(pl.program_id(0) == 0)
    def _():
        emb_s[...] = jnp.zeros_like(emb_s)
        emb_s[0:V, :] = emb_ref[...]

    index = lax.broadcasted_iota(jnp.int32, (TOK, step), 0)
    hot = jnp.where(index == tok_ref[...], 1.0, 0.0).astype(F32)
    hot = jnp.concatenate([hot, hot, hot], 0).astype(B16)
    x = tn(hot, thirds_rows(emb_s[...]))
    x_ref[...] = x
    unit, _ = norm_parts(x)
    normed = unit * vec_ref[0:1, :] + vec_ref[1:2, :]
    act = nn(normed.astype(B16), w_ref[...]) + bias_ref[...]
    h_ref[...] = jnp.concatenate([normed.T, tail(16, step, 1)], 0).astype(B16)
    turned = act.T
    cosine, sine = cos_ref[...], sin_ref[...]
    zeros = tail(PAD - HDIM, step, 0)
    ones = tail(PAD - HDIM, step, 3)
    for head in range(HEADS):
        low = HDIM * head
        query = turned[low : low + HDIM]
        query = (query * cosine + half_turn(query) * sine) * HDIM ** (-0.5)
        q_ref[head] = jnp.concatenate([query, zeros], 0).astype(B16)
        keys = turned[D + low : D + low + HDIM]
        keys = keys * cosine + half_turn(keys) * sine
        k_ref[head] = jnp.concatenate([keys, zeros], 0).astype(B16)
        value = turned[2 * D + low : 2 * D + low + HDIM]
        v_ref[head] = jnp.concatenate([value, ones], 0).astype(B16)


def rows_of(value):
    return value.astype(F32).T.astype(B16)


def attend_kernel(q_ref, k_ref, v_ref, mix_ref, inv_ref, p_ref):
    scores = nn(rows_of(k_ref[0]), q_ref[0])
    top = jnp.max(scores, 0, keepdims=True)
    probs = jnp.exp(scores - top).astype(B16)
    p_ref[0] = probs
    out = nn(v_ref[0], probs)
    inverse = 1.0 / out[HDIM : HDIM + 1]
    mix_ref[...] = out[0:HDIM] * inverse
    inv_ref[0] = inverse


def gelu_parts(upper):
    size = jnp.abs(upper) * (0.5**0.5)
    bell = jnp.exp(-0.5 * upper * upper)
    t = 1.0 / (1.0 + 0.3275911 * size)
    poly = t * (0.254829592 + t * (-0.284496736 + t * (1.421413741 + t * (-1.453152027 + t * 1.061405429))))
    lower = 0.5 * poly * bell
    cdf = jnp.where(upper < 0, lower, 1.0 - lower)
    return upper * cdf, cdf + upper * (0.3989422804014327 * bell)


def middle_kernel(mix_ref, inv_ref, x_ref, mask_ref, tgt_ref, count_ref, vec_ref, bu_ref, fin_ref,
                  head_ref, wo_ref, wu_ref, wd_ref, q_ref, qd_ref,
                  dm_ref, dx_ref, go_ref, gu_ref, gd_ref, s_ref, e_ref,
                  acc_o, acc_u, acc_d, head_s, hid_s, slope_s):
    pid = pl.program_id(0)
    step = x_ref.shape[0]
    wide = wu_ref.shape[1]

    @pl.when(pid == 0)
    def _():
        acc_o[...] = jnp.zeros_like(acc_o)
        acc_u[...] = jnp.zeros_like(acc_u)
        acc_d[...] = jnp.zeros_like(acc_d)
        e_ref[...] = jnp.zeros_like(e_ref)
        s_ref[...] = jnp.zeros_like(s_ref)
        head_s[...] = jnp.zeros_like(head_s)
        head_s[0:V, 0 : D + 1] = head_ref[...]

    mix = mix_ref[...]
    mixed = jnp.concatenate([mix, tail(16, step, 1)], 0).astype(B16)
    middle = x_ref[...] + tn(mixed[0:D], wo_ref[...]) + vec_ref[5:6, :]
    unit2, rstd2 = norm_parts(middle)
    normed2 = unit2 * vec_ref[6:7, :] + vec_ref[7:8, :]
    normed2 = jnp.concatenate([normed2, lane_tail(step, WIDE - D)], 1).astype(B16)
    block = 384
    for low in range(0, wide, block):
        cut = slice(low, low + block)
        upper = nn(normed2[:, 0:D], wu_ref[:, cut]) + bu_ref[:, cut]
        hidden, slope = gelu_parts(upper)
        hid_s[:, cut] = hidden.astype(B16)
        slope_s[:, cut] = slope
    resid = middle + nn(hid_s[...], wd_ref[...]) + vec_ref[8:9, :]
    unit3, rstd3 = norm_parts(resid)
    final = unit3 * fin_ref[0:1, :] + fin_ref[1:2, :]
    final = jnp.concatenate([final, lane_tail(step, WIDE - D)], 1).astype(B16)

    lanes = lax.broadcasted_iota(jnp.int32, (TOK, WIDE), 1)
    bias = jnp.sum(jnp.where(lanes == D, head_s[...], 0.0), 1, keepdims=True)
    table = head_s[:, 0:D].astype(B16)
    rows = lax.broadcasted_iota(jnp.int32, (TOK, step), 0)
    logits = jnp.where(rows < V, nt(table, final[:, 0:D]) + bias, -1e30)
    shifted = logits - jnp.max(logits, 0, keepdims=True)
    expo = jnp.exp(shifted)
    total = jnp.sum(expo, 0, keepdims=True)
    picks = rows == tgt_ref[...]
    weight = mask_ref[...].astype(F32)
    picked = jnp.sum(jnp.where(picks, shifted, 0.0), 0, keepdims=True)
    loss = jnp.sum((jnp.log(total) - picked) * weight, 1, keepdims=True)
    grad_logits = (expo / total - jnp.where(picks, 1.0, 0.0)) * (weight * (1.0 / count_ref[...]))
    grad_logits = grad_logits.astype(B16)
    e_ref[16 : 16 + TOK, :] += nn(grad_logits, final)
    grad_resid, grad_fg, grad_fb = norm_back(tn(grad_logits, table), unit3, rstd3, fin_ref[0:1, :])

    grad_y = grad_resid.astype(B16)
    acc_d[...] += tn(hid_s[...], grad_y)
    for low in range(0, wide, block):
        cut = slice(low, low + block)
        grad_hidden = nt(grad_y, wd_ref[cut, :])
        hid_s[:, cut] = (grad_hidden * slope_s[:, cut]).astype(B16)
    acc_u[...] += tn(normed2, hid_s[...])
    grad_mid, grad_g2, grad_b2 = norm_back(nt(hid_s[...], wu_ref[...]), unit2, rstd2, vec_ref[6:7, :])
    grad_mid = grad_mid + grad_resid
    dx_ref[...] = grad_mid
    branch = grad_mid.astype(B16)
    acc_o[...] += nn(mixed, branch)
    grad_mixed = nt(wo_ref[...], branch).astype(B16).astype(F32)
    zeros = tail(PAD - HDIM - 3, step, 0)
    for head in range(HEADS):
        cut = slice(HDIM * head, HDIM * head + HDIM)
        scaled = (grad_mixed[cut] * inv_ref[head]).astype(B16).astype(F32)
        delta = -jnp.sum(scaled * mix[cut], 0, keepdims=True)
        top, mid, low = thirds(delta)
        dm_ref[head] = jnp.concatenate(
            [scaled, top.astype(F32), mid.astype(F32), low.astype(F32), zeros], 0
        ).astype(B16)
    e_ref[1:2, 0:D] += grad_g2
    e_ref[2:3, 0:D] += grad_b2
    e_ref[3:4, 0:D] += jnp.sum(grad_y.astype(F32), 0, keepdims=True)
    e_ref[8:9, 0:D] += grad_fg
    e_ref[9:10, 0:D] += grad_fb
    e_ref[10:11, :] += jnp.broadcast_to(loss, (1, WIDE))

    @pl.when(pid == pl.num_programs(0) - 1)
    def _():
        e_ref[0:1, 0:D] = acc_o[D : D + 1, :]
        for part in range(wide // D):
            e_ref[4 + part : 5 + part, 0:D] = acc_u[D : D + 1, D * part : D * part + D]
        go = acc_o[0:D, :].astype(B16)
        gu = acc_u[0:D, :].astype(B16)
        go_ref[...] = go
        gu_ref[...] = gu
        gd_ref[...] = acc_d[...].astype(B16)
        sketch = nt(thirds_rows(q_ref[:, 3 * D : 4 * D]), go) + nt(thirds_rows(q_ref[:, 4 * D :]), gu)
        s_ref[0:8, 0:D] = fold_rows(sketch)
        start = thirds_rows(qd_ref[...])
        for part in range(wide // D):
            piece = nt(start, gd_ref[D * part : D * part + D, :])
            s_ref[8 + 8 * part : 16 + 8 * part, 0:D] = fold_rows(piece)


def attend_back_kernel(p_ref, q_ref, k_ref, v_ref, dm_ref, cos_ref, sin_ref, da_ref):
    cosine, sine = cos_ref[...], sin_ref[...]
    parts = [[], [], []]
    for head in range(p_ref.shape[0]):
        probs = p_ref[head]
        grad = dm_ref[head]
        slope = nn(rows_of(v_ref[head]), grad)
        grad_scores = (probs.astype(F32) * slope).astype(B16)
        grad_value = nt(grad, probs)[0:HDIM]
        grad_keys = nt(q_ref[head], grad_scores)[0:HDIM]
        grad_query = nn(k_ref[head], grad_scores)[0:HDIM] * HDIM ** (-0.5)
        parts[0].append(grad_query * cosine + half_turn(grad_query * sine))
        parts[1].append(grad_keys * cosine + half_turn(grad_keys * sine))
        parts[2].append(grad_value)
    for index in range(3):
        da_ref[index] = jnp.concatenate(parts[index], 0).astype(B16)


def input_kernel(tok_ref, da_ref, h_ref, x_ref, dx_ref, w_ref, vec_ref, q_ref, s_ref, serr_ref, e_ref,
                 g_ref, out_ref, acc_w, acc_e):
    pid = pl.program_id(0)
    step = x_ref.shape[0]

    @pl.when(pid == 0)
    def _():
        acc_w[...] = jnp.zeros_like(acc_w)
        acc_e[...] = jnp.zeros_like(acc_e)
        out_ref[...] = jnp.zeros_like(out_ref)

    da = da_ref[...].reshape(3 * D, step)
    acc_w[...] += nt(h_ref[...], da)
    grad = nn(w_ref[...], da).T
    unit, rstd = norm_parts(x_ref[...])
    grad_x, grad_g, grad_b = norm_back(grad, unit, rstd, vec_ref[0:1, :])
    grad_x = grad_x + dx_ref[...]
    index = lax.broadcasted_iota(jnp.int32, (TOK, step), 0)
    hot = jnp.where(index == tok_ref[...], 1.0, 0.0).astype(B16)
    for part in thirds(grad_x):
        acc_e[...] += nn(hot, part)
    out_ref[40:41, 0:D] += grad_g
    out_ref[41:42, 0:D] += grad_b

    @pl.when(pid == pl.num_programs(0) - 1)
    def _():
        for part in range(3):
            out_ref[42 + part : 43 + part, 0:D] = acc_w[D : D + 1, D * part : D * part + D]
        g = acc_w[0:D, :].astype(B16)
        g_ref[...] = g
        out_ref[0:40, :] = s_ref[...] + serr_ref[...]
        out_ref[0:8, 0:D] += fold_rows(nt(thirds_rows(q_ref[:, 0 : 3 * D]), g))
        out_ref[48:104, :] = e_ref[...]
        out_ref[104 : 104 + TOK, 0:D] = acc_e[...]


def orthonormal(sketch, gram):
    basis = jnp.zeros_like(sketch[0])
    count = gram.shape[0]
    index = lax.broadcasted_iota(jnp.int32, (count, 1), 0)
    out = [jnp.zeros_like(part) for part in sketch]
    left = list(sketch)
    for step in range(count):
        pivot = gram[step : step + 1, step : step + 1]
        scale = 1.0 / jnp.sqrt(pivot)
        column = gram[:, step : step + 1] * scale
        row = gram[step : step + 1, :] * scale
        column = jnp.where(index > step, column, 0.0)
        gram = gram - column * row
        for place in range(len(left)):
            base = left[place][step : step + 1, :] * scale
            out[place] = jnp.where(index == step, base, out[place])
            left[place] = left[place] - column * base
    return out


def factor_kernel(group, a_ref, gi_ref, go_ref, gu_ref, gd_ref, err_ref, errd_ref,
                  p_ref, own_ref, f_ref, pad_s):
    rows = err_ref.shape[0]
    parts = gd_ref.shape[0] // D
    wide = a_ref[0:8, 0:D]
    down = [a_ref[8 + 8 * part : 16 + 8 * part, 0:D] for part in range(parts)]
    gram = exact_nt(wide, wide)
    (wide,) = orthonormal([wide], gram)
    gram = exact_nt(down[0], down[0])
    for part in range(1, parts):
        gram = gram + exact_nt(down[part], down[part])
    down = orthonormal(down, gram)
    p_ref[...] = jnp.zeros_like(p_ref)
    p_ref[0:8, 0:D] = wide
    for part in range(parts):
        p_ref[8 + 8 * part : 16 + 8 * part, 0:D] = down[part]
    own = pltpu.roll(p_ref[0:8, :], (WIDE - rows * group[0]) % WIDE, 1)
    start = pl.multiple_of(8 + 8 * group[0], 8)
    own_down = p_ref[pl.ds(start, 8), :]
    own_ref[0:8, :] = own
    own_ref[8:16, :] = own_down
    total = exact_nn(own[:, 0:rows], err_ref[...])
    three = thirds_rows(wide)
    f_ref[...] = jnp.zeros_like(f_ref)
    f_ref[0:8, :] = total
    f_ref[0:8, 0 : 3 * D] += fold_rows(nn(three, gi_ref[...]))
    f_ref[0:8, 3 * D : 4 * D] += fold_rows(nn(three, go_ref[...]))
    f_ref[0:8, 4 * D :] += fold_rows(nn(three, gu_ref[...]))
    total = exact_nn(own_down[:, 0:D], errd_ref[...])
    for part in range(parts):
        total = total + fold_rows(nn(thirds_rows(down[part]), gd_ref[D * part : D * part + D, :]))
    f_ref[8:16, 0:D] = total


def six(left, right):
    first, second = thirds(left), thirds(right)
    order = ((0, 0), (0, 1), (1, 0), (1, 1), (0, 2), (2, 0))
    left = jnp.concatenate([first[i].astype(F32) for i, _ in order], 0).astype(B16)
    right = jnp.concatenate([second[j].astype(F32) for _, j in order], 0).astype(B16)
    return tn(left, right)


def renew(weight, moment, grad, scale, rate):
    new_moment = BETA * moment + scale * grad
    return weight - rate * new_moment, new_moment


def finish_kernel(replicas, a_ref, p_ref, own_ref, f_ref, gi_ref, gr_ref, gd_ref,
                  w_ref, wd_ref, m_ref, md_ref, err_ref, errd_ref,
                  vec_ref, vmom_ref, fin_ref, fmom_ref, emb_ref, emom_ref, head_ref, hmom_ref,
                  norm_ref, nw_ref, nwd_ref, nm_ref, nmd_ref, ne_ref, ned_ref,
                  nvec_ref, nvmom_ref, nfin_ref, nfmom_ref, nemb_ref, nemom_ref, nhead_ref, nhmom_ref):
    rows = err_ref.shape[0]
    a = a_ref[...]
    square = jnp.sum(a[40:45, 0:D] * a[40:45, 0:D]) + jnp.sum(a[48:58, 0:D] * a[48:58, 0:D])
    square = square + jnp.sum(a[104 : 104 + V, 0:D] * a[104 : 104 + V, 0:D])
    lanes = lax.broadcasted_iota(jnp.int32, (V, WIDE), 1)
    square = square + jnp.sum(jnp.where(lanes <= D, a[64 : 64 + V] * a[64 : 64 + V], 0.0))
    basis = p_ref[...]
    factor = f_ref[...]
    gram = exact_nt(basis[0:8, 0:D], basis[0:8, 0:D])
    square = square + jnp.sum(gram * exact_nt(factor[0:8], factor[0:8]))
    gram = jnp.zeros((8, 8), F32)
    for part in range(1, basis.shape[0] // 8):
        piece = basis[8 * part : 8 * part + 8, 0:D]
        gram = gram + exact_nt(piece, piece)
    square = square + jnp.sum(gram * exact_nt(factor[8:16, 0:D], factor[8:16, 0:D]))
    norm = jnp.sqrt(square)
    norm_ref[...] = jnp.broadcast_to(norm, norm_ref.shape)
    scale = jnp.minimum(1.0, CLIP / norm)

    approx = six(own_ref[0:8, 0:rows], factor[0:8])
    nw_ref[...], nm_ref[...] = renew(w_ref[...], m_ref[...], approx, scale, RATE_WIDE)
    share = approx * (1.0 / replicas)
    ne_ref[:, 0 : 3 * D] = gi_ref[...].astype(F32) + err_ref[:, 0 : 3 * D] - share[:, 0 : 3 * D]
    ne_ref[:, 3 * D :] = gr_ref[...].astype(F32) + err_ref[:, 3 * D :] - share[:, 3 * D :]
    approx = six(own_ref[8:16, 0:D], factor[8:16, 0:D])
    nwd_ref[...], nmd_ref[...] = renew(wd_ref[...], md_ref[...], approx, scale, RATE_LOWER)
    ned_ref[...] = gd_ref[...].astype(F32) + errd_ref[...] - approx * (1.0 / replicas)

    places = (40, 41, 42, 43, 44, 48, 49, 50, 51, 52, 53, 54, 55)
    for row, place in enumerate(places):
        cut = slice(row, row + 1)
        nvec_ref[cut, :], nvmom_ref[cut, :] = renew(
            vec_ref[cut, :], vmom_ref[cut, :], a[place : place + 1, 0:D], scale, RATE_VECTOR
        )
    nfin_ref[...], nfmom_ref[...] = renew(fin_ref[...], fmom_ref[...], a[56:58, 0:D], scale, RATE_FINAL)
    nemb_ref[...], nemom_ref[...] = renew(
        emb_ref[...], emom_ref[...], a[104 : 104 + V, 0:D], scale, RATE_EMBED
    )
    nhead_ref[...], nhmom_ref[...] = renew(
        head_ref[...], hmom_ref[...], a[64 : 64 + V, 0 : D + 1], scale, RATE_HEAD
    )


def swap(value, axis, bit):
    size = lax.axis_size(axis)
    return lax.ppermute(value, axis, [(i, i ^ bit) for i in range(size)])


def bits_of(axis):
    size, bit, out = lax.axis_size(axis), 1, []
    while bit < size:
        out.append(bit)
        bit *= 2
    return out


def gather_rows(value, axis):
    place = lax.axis_index(axis)
    value = value[None]
    for bit in reversed(bits_of(axis)):
        other = swap(value, axis, bit)
        mine = (place & bit) == 0
        value = jnp.stack([jnp.where(mine, value, other), jnp.where(mine, other, value)], -3)
    return value.reshape(-1, value.shape[-1])


def add_all(value):
    for axis in ("grp", "rep"):
        for bit in bits_of(axis):
            value = value + swap(value, axis, bit)
    return value


def whole(shape):
    return pl.BlockSpec(shape, lambda *_: (0,) * len(shape))


def shards(tokens, mask, targets, mats_d, mats_down, mom_d, mom_down, err_d, err_down, q_d, q_down,
           vectors, vec_mom, final_norm, final_mom, embed, embed_mom, head, head_mom):
    length = tokens.shape[1]
    wide = mats_d.shape[2]
    hidden = wide - 4 * D
    rows = mats_d.shape[1]
    rows_down = mats_down.shape[1]
    step = 256
    steps = length // step
    group = lax.axis_index("grp").astype(jnp.int32).reshape(1)
    cosine, sine = tables(length)
    q_t, qd_t = q_d[0].T, q_down[0].T
    head_t = head.T
    vec = vectors.reshape(-1, D)
    err, errd = err_d[0, 0], err_down[0, 0]

    wide16 = mats_d[0].astype(B16)
    w_in = gather_rows(wide16[:, : 3 * D], "grp")
    w_rest = lax.all_gather(wide16[:, 3 * D :], "grp", axis=0, tiled=True)
    w_down = lax.all_gather(mats_down[0].astype(B16), "grp", axis=0, tiled=True)
    w_out, w_up = w_rest[:, :D], w_rest[:, D:]
    counted = jnp.broadcast_to(jnp.sum(mask.astype(F32)), (8, 128))
    counted = add_all(counted)[0:1, 0:1]

    prefetch = lambda grid, ins, outs, scratch: pltpu.PrefetchScalarGridSpec(
        num_scalar_prefetch=1, grid=grid, in_specs=ins, out_specs=outs, scratch_shapes=scratch
    )
    err_sketch = pl.pallas_call(
        error_kernel,
        grid_spec=prefetch(
            (1,),
            [whole((rows, wide)), whole((rows_down, D)), whole((8, wide)), whole((8, D))],
            whole((40, WIDE)),
            [pltpu.VMEM((8, WIDE), F32)],
        ),
        out_shape=jax.ShapeDtypeStruct((40, WIDE), F32),
        compiler_params=params(),
        name="error_sketch",
    )(group, err, errd, q_t, qd_t)

    cols = pl.BlockSpec((1, step), lambda i: (0, i))
    flat = pl.BlockSpec((step, D), lambda i: (i, 0))
    heads = pl.BlockSpec((HEADS, PAD, step), lambda i: (0, 0, i))
    wave = pl.BlockSpec((HDIM, step), lambda i: (0, i))
    x, h_t, query, keys, value = pl.pallas_call(
        embed_kernel,
        grid=(steps,),
        in_specs=[cols, whole((V, D)), whole((D, 3 * D)), whole(vec.shape), whole((1, 3 * D)), wave, wave],
        out_specs=[flat, pl.BlockSpec((D + 16, step), lambda i: (0, i)), heads, heads, heads],
        out_shape=[
            jax.ShapeDtypeStruct((length, D), F32),
            jax.ShapeDtypeStruct((D + 16, length), B16),
        ]
        + [jax.ShapeDtypeStruct((HEADS, PAD, length), B16)] * 3,
        scratch_shapes=[pltpu.VMEM((TOK, D), F32)],
        compiler_params=params(),
        name="embed_project",
    )(tokens, embed, w_in, vec, vectors[:, 2 * D : 5 * D], cosine, sine)

    one = pl.BlockSpec((1, PAD, length), lambda i: (i, 0, 0))
    mix, inverse, probs = pl.pallas_call(
        attend_kernel,
        grid=(HEADS,),
        in_specs=[one, one, one],
        out_specs=[
            pl.BlockSpec((HDIM, length), lambda i: (i, 0)),
            pl.BlockSpec((1, 1, length), lambda i: (i, 0, 0)),
            pl.BlockSpec((1, length, length), lambda i: (i, 0, 0)),
        ],
        out_shape=[
            jax.ShapeDtypeStruct((D, length), F32),
            jax.ShapeDtypeStruct((HEADS, 1, length), F32),
            jax.ShapeDtypeStruct((HEADS, length, length), B16),
        ],
        compiler_params=params(),
        name="attend",
    )(query, keys, value)

    grad_mix, grad_mid, g_out, g_up, g_down, sketch, early = pl.pallas_call(
        middle_kernel,
        grid=(steps,),
        in_specs=[
            pl.BlockSpec((D, step), lambda i: (0, i)),
            pl.BlockSpec((HEADS, 1, step), lambda i: (0, 0, i)),
            flat, cols, cols, whole((1, 1)), whole(vec.shape), whole((1, hidden)), whole((2, D)),
            whole((V, D + 1)), whole((D, D)), whole((D, hidden)), whole((hidden, D)),
            whole((8, wide)), whole((8, D)),
        ],
        out_specs=[
            heads, flat, whole((D, D)), whole((D, hidden)), whole((hidden, D)),
            whole((40, WIDE)), whole((56, WIDE)),
        ],
        out_shape=[
            jax.ShapeDtypeStruct((HEADS, PAD, length), B16),
            jax.ShapeDtypeStruct((length, D), F32),
            jax.ShapeDtypeStruct((D, D), B16),
            jax.ShapeDtypeStruct((D, hidden), B16),
            jax.ShapeDtypeStruct((hidden, D), B16),
            jax.ShapeDtypeStruct((40, WIDE), F32),
            jax.ShapeDtypeStruct((56, WIDE), F32),
        ],
        scratch_shapes=[
            pltpu.VMEM((D + 16, D), F32),
            pltpu.VMEM((WIDE, hidden), F32),
            pltpu.VMEM((hidden, D), F32),
            pltpu.VMEM((TOK, WIDE), F32),
            pltpu.VMEM((step, hidden), B16),
            pltpu.VMEM((step, hidden), F32),
        ],
        compiler_params=params(),
        name="feed_and_loss",
    )(mix, inverse, x, mask, targets, counted, vec, vectors[:, 9 * D :], final_norm, head_t,
      w_out, w_up, w_down, q_t, qd_t)

    own_rest = lax.psum_scatter(
        jnp.concatenate([g_out, g_up], 1), "grp", scatter_dimension=0, tiled=True
    )
    own_down = lax.psum_scatter(g_down, "grp", scatter_dimension=0, tiled=True)

    pair = 2
    two = pl.BlockSpec((pair, PAD, length), lambda i: (i, 0, 0))
    grad_act = pl.pallas_call(
        attend_back_kernel,
        grid=(HEADS // pair,),
        in_specs=[
            pl.BlockSpec((pair, length, length), lambda i: (i, 0, 0)),
            two, two, two, two, whole((HDIM, length)), whole((HDIM, length)),
        ],
        out_specs=pl.BlockSpec((3, pair * HDIM, length), lambda i: (0, i, 0)),
        out_shape=jax.ShapeDtypeStruct((3, D, length), B16),
        compiler_params=params(),
        name="attend_back",
    )(probs, query, keys, value, grad_mix, cosine, sine)

    g_in, shared = pl.pallas_call(
        input_kernel,
        grid=(steps,),
        in_specs=[
            cols, pl.BlockSpec((3, D, step), lambda i: (0, 0, i)),
            pl.BlockSpec((D + 16, step), lambda i: (0, i)), flat, flat, whole((D, 3 * D)),
            whole(vec.shape), whole((8, wide)), whole((40, WIDE)), whole((40, WIDE)), whole((56, WIDE)),
        ],
        out_specs=[whole((D, 3 * D)), whole((160, WIDE))],
        out_shape=[jax.ShapeDtypeStruct((D, 3 * D), B16), jax.ShapeDtypeStruct((160, WIDE), F32)],
        scratch_shapes=[pltpu.VMEM((D + 16, 3 * D), F32), pltpu.VMEM((TOK, D), F32)],
        compiler_params=params(),
        name="input_grads",
    )(tokens, grad_act, h_t, x, grad_mid, w_in, vec, q_t, sketch, err_sketch, early)

    own_in = lax.psum_scatter(g_in, "grp", scatter_dimension=0, tiled=True)
    shared = add_all(shared)

    basis, own, factor = pl.pallas_call(
        factor_kernel,
        grid_spec=prefetch(
            (1,),
            [
                whole((160, WIDE)), whole((D, 3 * D)), whole((D, D)), whole((D, hidden)), whole((hidden, D)),
                whole((rows, wide)), whole((rows_down, D)),
            ],
            [whole((40, WIDE)), whole((16, WIDE)), whole((16, wide))],
            [pltpu.VMEM((8, WIDE), F32)],
        ),
        out_shape=[
            jax.ShapeDtypeStruct((40, WIDE), F32),
            jax.ShapeDtypeStruct((16, WIDE), F32),
            jax.ShapeDtypeStruct((16, wide), F32),
        ],
        compiler_params=params(),
        name="left_factors",
    )(group, shared, g_in, g_out, g_up, g_down, err, errd)

    packed = add_all(jnp.concatenate([factor[0:8], factor[8:16, 0:D]], 1))
    factor_wide, factor_down = packed[:, :wide], packed[:, wide:]
    factor = jnp.concatenate([factor_wide, jnp.pad(factor_down, ((0, 0), (0, wide - D)))], 0)

    same = lambda value: jax.ShapeDtypeStruct(value.shape, F32)
    replicas = lax.axis_size("rep")
    small = (vec, vec_mom.reshape(-1, D), final_norm, final_mom, embed, embed_mom, head_t, head_mom.T)
    outs = pl.pallas_call(
        partial(finish_kernel, replicas),
        out_shape=[
            jax.ShapeDtypeStruct((8, 128), F32),
            same(mats_d[0]), same(mats_down[0]), same(mats_d[0]), same(mats_down[0]),
            same(err), same(errd),
        ]
        + [same(item) for item in small],
        compiler_params=params(),
        name="finish",
    )(shared, basis, own, factor, own_in, own_rest, own_down,
      mats_d[0], mats_down[0], mom_d[0], mom_down[0], err, errd, *small)
    (norm, new_wide, new_down, new_mom_wide, new_mom_dn, new_err, new_errd,
     new_vec, new_vmom, new_fin, new_fmom, new_emb, new_emom, new_head, new_hmom) = outs
    return (
        shared[58, 0],
        counted[0, 0],
        norm[0, 0],
        new_wide[None],
        new_down[None],
        new_mom_wide[None],
        new_mom_dn[None],
        new_err[None, None],
        new_errd[None, None],
        own[0:8, :rows].T[None],
        own[8:16, :rows_down].T[None],
        factor_wide.T[None],
        factor_down.T[None],
        new_vec.reshape(1, -1),
        new_vmom.reshape(1, -1),
        new_fin,
        new_fmom,
        new_emb,
        new_emom,
        new_head.T,
        new_hmom.T,
    )


def solution(mesh):
    whole_seq = P(("rep", "grp"), None)
    by_rows = P(None, "grp", None)
    by_replica = P("rep", None, "grp", None)
    placed = (
        (whole_seq,) * 3 + (by_rows,) * 4 + (by_replica,) * 2 + (P(),) * 10
    )
    given = (P(),) * 3 + (by_rows,) * 4 + (by_replica,) * 2 + (by_rows,) * 2 + (P(),) * 10
    return jax.shard_map(shards, mesh=mesh, in_specs=placed, out_specs=given, check_vma=False)
```

time: 888 us -> 320 us (0.36); the launches traced: 873 us -> 319 us
  matrix products: 312 us -> 0 us
  Pallas kernels: 0 us -> 166 us
  other arithmetic: 148 us -> 9.03 us
  blocking collectives: 134 us -> 0 us
  local copies, waits for them, and re-layouts: 116 us -> 21.4 us
  waiting for transfers between devices: 140 us -> 84.5 us
  starting transfers between devices: 0.38 us -> 24 us
    dot_general x39 -> x0, matrix products: 312 us -> none  [the longest x4 68.1 us: one_block(): jnp.einsum('qhe,khe->hqk', piece, keys, preferred_element_type=jnp.float32)]
    pallas_call x0 -> x8, Pallas kernels: none -> 166 us  [the longest x1 47.1 us: shards(): pl.pallas_call(attend_back_kernel, grid=(HEADS // pair,), in_specs=[pl.Bl...]
    psum x5 -> x0, blocking collectives: 134 us -> none  [the longest x2 83.5 us: shards(): lax.psum((local_loss, jnp.sum(weight_mask)), ('rep', 'grp'))]
    psum x1 -> x0, waiting for transfers between devices: 115 us -> none  [shards(): lax.psum((factor_wide, factor_down, grad_vec, grad_final, grad_embed, gra...]
    convert_element_type x8 -> x2, other arithmetic: 76 us -> 2.52 us  [the longest x1 1.67 us: shards(): wide16 = mats_d[0].astype(B16)]
    ppermute x0 -> x17, waiting for transfers between devices: none -> 69.3 us  [swap(): return lax.ppermute(value, axis, [(i, i ^ bit) for i in range(size)])]
    dynamic_update_slice x4 -> x0, local copies, waits for them, and re-layouts: 51.9 us -> none  [attend(): lax.map(one_block, query.reshape(length // block, block, HEADS, HDIM))]
    reduce_sum x21 -> x1, other arithmetic: 46.3 us -> 0.61 us  [shards(): counted = jnp.broadcast_to(jnp.sum(mask.astype(F32)), (8, 128))]
  transfers between devices with their start and end apart: 5 -> 22, of which waited for: 2 -> 16; matrix products, arithmetic and copies ran while one was open for 55% -> 7% of each run, Pallas kernels for 0% -> 19%
where the time goes in v1:
time: 320 us; the launch traced here: 319 us
  Pallas kernels  166 us (52%)
  waiting for transfers between devices  84.5 us (26%)
  starting transfers between devices  24 us (8%)
  local copies, waits for them, and re-layouts  21.4 us (7%)
  between operations  14 us (4%)
  other arithmetic  9.03 us (3%)
    ppermute x17, waiting for transfers between devices, swap(): return lax.ppermute(value, axis, [(i, i ^ bit) for i in range(size)])  69.3 us
    pallas_call x1, Pallas kernels, shards(): pl.pallas_call(attend_back_kernel, grid=(HEADS // pair,), in_specs=[pl.Bl...  47.1 us
    pallas_call x1, Pallas kernels, shards(): pl.pallas_call(attend_kernel, grid=(HEADS,), in_specs=[one, one, one], ou...  40.8 us
    pallas_call x1, Pallas kernels, shards(): pl.pallas_call(middle_kernel, grid=(steps,), in_specs=[pl.BlockSpec((D, s...  37.5 us
    ppermute x17, starting transfers between devices, swap(): return lax.ppermute(value, axis, [(i, i ^ bit) for i in range(size)])  23.8 us
    unnamed x6, waiting for transfers between devices  15.1 us
    pallas_call x1, Pallas kernels, shards(): pl.pallas_call(input_kernel, grid=(steps,), in_specs=[cols, pl.BlockSpec(...  11.7 us
    pallas_call x1, Pallas kernels, shards(): pl.pallas_call(partial(finish_kernel, replicas), out_shape=[jax.ShapeDtyp...  9.32 us
  transfers between devices with their start and end apart: 22, of which 16 were waited for; matrix products, arithmetic and copies ran while one was open for 7% of the time, Pallas kernels for 19%

profile of v1, /device:TPU:0, one launch (start us, length us, event | category | flops | bytes accessed | tf_op | source)
XLA Modules:
  0.0 319.0 jit_solution(12808964717313151842)
XLA Ops:
  7.2 1.7 bitcast_convert_fusion.1
  8.9 1.0 slice.61
  10.0 0.8 bitcast_convert_fusion
  11.0 3.0 collective-permute-start
  14.0 10.1 %collective-permute-done = bf16[1,120,1440]{2,1,0:T(8,128)(2,1)S(1)} collective-permute-done((bf16[1,120,1440]{2,1,0:T(8,128)(2,1)S(1)}, bf16[1,120,1440]{2,1,0:T(8,128)(2,1)S(1)}, u32[]{:S(2)}, u32[]{:S(2)}) %collective-permute-start) | collective-permute-done | bytes 345632 | tf_op jit(solution)/shard_map/ppermute | solution.py:457
  24.4 0.6 convert_reduce_fusion
  25.0 0.6 broadcast_in_dim.37
  25.6 0.6 collective-permute-start.2
  26.2 0.8 collective-permute-done.2
  27.0 0.6 broadcast_add_fusion
  27.7 2.6 collective-permute-start.3
  30.2 1.6 collective-permute-done.3
  31.9 0.6 fusion.1
  32.5 1.3 collective-permute-start.4
  33.8 2.4 collective-permute-done.4
  36.2 1.4 collective-permute-start.5
  37.6 2.2 collective-permute-done.5
  39.8 2.5 collective-permute-start.6
  42.3 0.7 slice.46.bias_ref
  43.0 0.7 slice.48.bu_ref
  43.8 0.7 reshape.61.vec_ref
  44.4 4.8 %error_sketch.1.serr_ref = f32[40,512]{1,0:T(8,128)} custom-call(s32[1]{0:T(128)} %bitcast.13.group, f32[120,3840]{1,0:T(8,128)} %bitcast.60, f32[480,480]{1,0:T(8,128)} %bitcast.65, f32[8,3840]{1,0:T(8,128)} %bitcast.71, f32[8,480]{1,0:T(8,128)} %bitcast.78), custom_call_target="tpu_custom_call" | custom-call | tf_op jit(solution)/shard_map/error_sketch/pallas_call | solution.py:516
  50.1 1.2 copy.43
  51.3 7.4 %embed_project.1 = (f32[1024,480]{1,0:T(8,128)}, bf16[496,1024]{1,0:T(8,128)(2,1)}, bf16[20,32,1024]{2,1,0:T(8,128)(2,1)}, bf16[20,32,1024]{2,1,0:T(8,128)(2,1)}, bf16[20,32,1024]{2,1,0:T(8,128)(2,1)}) custom-call(s32[1,1024]{1,0:T(1,128)} %tok_ref.3, f32[33,480]{1,0:T(8,128)} %emb_ref.3, bf16[480,1440]{1,0:T(8,128)(2,1)} %bitcast.63, ...), custom_call_target="tpu_custom_call" | custom-call | tf_op jit(solution)/shard_map/embed_project/pallas_call | solution.py:533
  58.7 40.8 %attend.1 = (f32[480,1024]{1,0:T(8,128)}, f32[20,1,1024]{2,1,0:T(1,128)}, bf16[20,1024,1024]{2,1,0:T(8,128)(2,1)}) custom-call(bf16[20,32,1024]{2,1,0:T(8,128)(2,1)} %get-tuple-element.56.q_ref, bf16[20,32,1024]{2,1,0:T(8,128)(2,1)} %get-tuple-element.57.k_ref, bf16[20,32,1024]{2,1,0:T(8,128)(2,1)} %get-tuple-element.58.v_ref), custom_call_target="tpu_custom_call" | custom-call | tf_op jit(solution)/shard_map/attend/pallas_call | solution.py:549
  99.4 1.8 slice.62.wo_ref
  101.3 3.6 %slice.63.wu_ref = bf16[480,1920]{1,0:T(8,128)(2,1)} slice(bf16[480,2400]{1,0:T(8,128)(2,1)} %all-gather.3.cloned.1.call-done), slice={[0:480], [480:2400]} | slice | bytes 3686400 | tf_op jit(solution)/shard_map/slice | solution.py:509
  104.9 37.5 %feed_and_loss.1 = (bf16[20,32,1024]{2,1,0:T(8,128)(2,1)}, f32[1024,480]{1,0:T(8,128)}, bf16[480,480]{1,0:T(8,128)(2,1)}, bf16[480,1920]{1,0:T(8,128)(2,1)}, bf1...) custom-call(f32[480,1024]{1,0:T(8,128)} %get-tuple-element.60.mix_ref, ...), custom_call_target="tpu_custom_call" | custom-call | tf_op jit(solution)/shard_map/feed_and_loss/pallas_call | solution.py:567
  142.4 47.1 %attend_back.1.da_ref = bf16[3,480,1024]{2,1,0:T(8,128)(2,1)} custom-call(bf16[20,1024,1024]{2,1,0:T(8,128)(2,1)} %get-tuple-element.59.p_ref, bf16[20,32,1024]{2,1,0:T(8,128)(2,1)} %get-tuple-element.56.q_ref, bf16[20,32,1024]{2,1,0:T(8,128)(2,1)} %get-tuple-element.57.k_ref, bf16[20,32,1024]{2,1,0:T(8,128)(2,1)} %get-tuple-element.58.v_ref, ...), custom_call_target="tpu_custom_call" | custom-call | tf_op jit(solution)/shard_map/attend_back/pallas_call | solution.py:610
  189.5 11.7 %input_grads.1 = (bf16[480,1440]{1,0:T(8,128)(2,1)}, f32[160,512]{1,0:T(8,128)}) custom-call(s32[1,1024]{1,0:T(1,128)} %tok_ref.3, bf16[3,480,1024]{2,1,0:T(8,128)(2,1)} %attend_back.1.da_ref, bf16[496,1024]{1,0:T(8,128)(2,1)} %get-tuple-element.64.h_ref, f32[1024,480]{1,0:T(8,128)} %get-tuple-element.62.x_ref, f32[1024,480]{1,0:T(8,128)} %get-tuple-element.65.dx_ref, ...), custom_call_target="tpu_custom_call" | custom-call | tf_op jit(solution)/shard_map/input_grads/pallas_call | solution.py:623
  202.2 1.6 collective-permute-done.7
  203.9 2.1 collective-permute-start.8
  206.0 8.0 %collective-permute-done.8 = f32[160,512]{1,0:T(8,128)S(1)} collective-permute-done((f32[160,512]{1,0:T(8,128)S(1)}, f32[160,512]{1,0:T(8,128)S(1)}, u32[]{:S(2)}, u32[]{:S(2)}) %collective-permute-start.8) | collective-permute-done | bytes 327712 | tf_op jit(solution)/shard_map/ppermute | solution.py:457
  214.0 1.7 collective-permute-start.9
  215.7 7.6 %collective-permute-done.9 = f32[160,512]{1,0:T(8,128)S(1)} collective-permute-done((f32[160,512]{1,0:T(8,128)S(1)}, f32[160,512]{1,0:T(8,128)S(1)}, u32[]{:S(2)}, u32[]{:S(2)}) %collective-permute-start.9) | collective-permute-done | bytes 327712 | tf_op jit(solution)/shard_map/ppermute | solution.py:457
  223.4 1.8 collective-permute-start.10
  225.2 2.3 pad_maximum_fusion
  227.5 4.4 %collective-permute-done.10 = f32[160,512]{1,0:T(8,128)S(1)} collective-permute-done((f32[160,512]{1,0:T(8,128)S(1)}, f32[160,512]{1,0:T(8,128)S(1)}, u32[]{:S(2)}, u32[]{:S(2)}) %collective-permute-start.10) | collective-permute-done | bytes 327712 | tf_op jit(solution)/shard_map/ppermute | solution.py:457
  232.3 15.2 %collective-permute-done.11 = f32[160,512]{1,0:T(8,128)S(1)} collective-permute-done((f32[160,512]{1,0:T(8,128)S(1)}, f32[160,512]{1,0:T(8,128)S(1)}, u32[]{:S(2)}, u32[]{:S(2)}) %collective-permute-start.11) | collective-permute-done | bytes 327712 | tf_op jit(solution)/shard_map/ppermute | solution.py:457
  247.5 0.8 add.62.a_ref
  248.2 7.4 %left_factors.1 = (f32[40,512]{1,0:T(8,128)}, f32[16,512]{1,0:T(8,128)}, f32[16,3840]{1,0:T(8,128)}) custom-call(s32[1]{0:T(128)} %bitcast.13.group, f32[160,512]{1,0:T(8,128)} %add.62.a_ref, bf16[480,1440]{1,0:T(8,128)(2,1)} %get-tuple-element.69.gi_ref, bf16[480,480]{1,0:T(8,128)(2,1)} %get-tuple-element.70.go_ref, ...), custom_call_target="tpu_custom_call" | custom-call | tf_op jit(solution)/shard_map/left_factors/pallas_call | solution.py:641
  255.7 0.7 slice.54
  256.4 0.9 slice.53
  257.4 1.3 collective-permute-done.12
  258.8 1.1 collective-permute-start.13
  259.9 4.7 %collective-permute-done.13 = f32[8,4320]{1,0:T(8,128)S(1)} collective-permute-done((f32[8,4320]{1,0:T(8,128)S(1)}, f32[8,4320]{1,0:T(8,128)S(1)}, u32[]{:S(2)}, u32[]{:S(2)}) %collective-permute-start.13) | collective-permute-done | bytes 138272 | tf_op jit(solution)/shard_map/ppermute | solution.py:457
  264.6 1.8 collective-permute-start.14
  266.4 0.7 reshape.63.vmom_ref
  267.1 1.2 slice.64
  268.3 1.4 collective-permute-done.14
  269.7 1.4 collective-permute-start.15
  271.1 0.6 slice_bitcast_fusion.1
  271.7 3.1 collective-permute-done.15
  274.9 2.3 collective-permute-start.16
  277.2 0.6 slice_bitcast_fusion.2
  277.8 4.6 %collective-permute-done.16 = f32[8,4320]{1,0:T(8,128)S(1)} collective-permute-done((f32[8,4320]{1,0:T(8,128)S(1)}, f32[8,4320]{1,0:T(8,128)S(1)}, u32[]{:S(2)}, u32[]{:S(2)}) %collective-permute-start.16) | collective-permute-done | bytes 138272 | tf_op jit(solution)/shard_map/ppermute | solution.py:457
  282.4 0.6 slice_bitcast_fusion.3
  283.0 0.7 slice_bitcast_fusion.4
  283.7 0.7 select_maximum_fusion.f_ref
  284.4 14.6 %reduce-scatter.10.cloned.1.call-done.gr_ref = bf16[120,2400]{1,0:T(8,128)(2,1)} async-done(((bf16[480,2400]{1,0:T(8,128)(2,1)}), bf16[120,2400]{1,0:T(8,128)(2,1)}) %reduce-scatter.10.cloned.1.call-update) | async-done | bytes 576016
  299.0 9.3 %finish.1 = (f32[8,128]{1,0:T(8,128)}, f32[120,3840]{1,0:T(8,128)}, f32[480,480]{1,0:T(8,128)}, f32[120,3840]{1,0:T(8,128)}, f32[480,480]{1,0:T(8,128)}, /*index...) custom-call(f32[160,512]{1,0:T(8,128)} %add.62.a_ref, ...), custom_call_target="tpu_custom_call" | custom-call | tf_op jit(solution)/shard_map/finish/pallas_call | solution.py:668
  308.3 1.2 slice.57
  309.5 1.5 reshape.64
  311.0 1.5 reshape.65
  (57 shorter events, 2.9 us)
Async XLA Ops:
  7.2 2.8 copy-start.1
  7.2 92.2 %all-gather.3.cloned.1.call-start = ((), (), s32[]{:S(2)}) async-start(), calls=%async_computation.3 | async-start | bytes 2918400 | tf_op jit(solution)/shard_map/all_gather | solution.py:507
  10.0 94.9 %all-gather.5.cloned.1.call-start = ((), (), s32[]{:S(2)}) async-start(), calls=%async_computation.4 | async-start | bytes 2457600 | tf_op jit(solution)/shard_map/all_gather | solution.py:508
  10.9 13.4 %copy-start.7 = (s32[1,1024]{1,0:T(1,128)S(1)}, s32[1,1024]{1,0:T(1,128)}, u32[]{:S(2)}) copy-start(s32[1,1024]{1,0:T(1,128)} %mask_ref.1) | copy-start | bytes 12292
  10.9 31.4 %copy-start.5 = (f32[1,6240]{1,0:T(1,128)S(1)}, f32[1,6240]{1,0:T(1,128)}, u32[]{:S(2)}) copy-start(f32[1,6240]{1,0:T(1,128)} %param.32) | copy-start | bytes 74884
  10.9 273.5 %reduce-scatter.6.cloned.1.call-start = ((), (), s32[]{:S(2)}) async-start(), calls=%async_computation.5 | async-start | bytes 1843200 | tf_op jit(solution)/shard_map/reduce_scatter | solution.py:638
  11.0 13.1 %collective-permute-start = (bf16[1,120,1440]{2,1,0:T(8,128)(2,1)S(1)}, bf16[1,120,1440]{2,1,0:T(8,128)(2,1)S(1)}, u32[]{:S(2)}, u32[]{:S(2)}) collective-permute-start(bf16[1,120,1440]{2,1,0:T(8,128)(2,1)S(1)} %slice_bitcast_fusion), channel_id=1, source_target_pairs={{0,2},{1,3},{2,0},{3,1},{4,6},{5,7},{6,4},{7,5},{8,10},{9,11},{10,... | collective-permute-start | bytes 1036808 | tf_op jit(solution)/shard_map/ppermute | solution.py:457
  24.3 25.5 %collective-permute-start.1 = (bf16[1,2,120,1440]{3,2,1,0:T(8,128)(2,1)S(1)}, bf16[1,2,120,1440]{3,2,1,0:T(8,128)(2,1)S(1)}, u32[]{:S(2)}, u32[]{:S(2)}) collective-permute-start(bf16[1,2,120,1440]{3,2,1,0:T(8,128)(2,1)S(1)} %pad_maximum_fusion.2), channel_id=1, source_target_pairs={{0,1},{1,0},{2,3},{3,2},{4,5},{5,4},{6,7},{7,6},{8,9},{9,8},{10,11... | collective-permute-start | bytes 2073608 | tf_op jit(solution)/shard_map/ppermute | solution.py:457
  25.6 1.4 collective-permute-start.2
  27.7 4.2 %collective-permute-start.3 = (f32[8,128]{1,0:T(8,128)S(1)}, f32[8,128]{1,0:T(8,128)S(1)}, u32[]{:S(2)}, u32[]{:S(2)}) collective-permute-start(f32[8,128]{1,0:T(8,128)S(1)} %broadcast_add_fusion), channel_id=1, source_target_pairs={{0,2},{1,3},{2,0},{3,1},{4,6},{5,7},{6,4},{7,5},{8,10},{9,11},{10,... | collective-permute-start | bytes 12296 | tf_op jit(solution)/shard_map/ppermute | solution.py:457
  32.5 3.7 %collective-permute-start.4 = (f32[8,128]{1,0:T(8,128)S(1)}, f32[8,128]{1,0:T(8,128)S(1)}, u32[]{:S(2)}, u32[]{:S(2)}) collective-permute-start(f32[8,128]{1,0:T(8,128)S(1)} %fusion.1), channel_id=1, source_target_pairs={{0,4},{4,0},{8,12},{12,8},{16,20},{20,16},{24,28},{28,24},{1,5},{5... | collective-permute-start | bytes 12296 | tf_op jit(solution)/shard_map/ppermute | solution.py:457
  36.2 3.6 %collective-permute-start.5 = (f32[8,128]{1,0:T(8,128)S(1)}, f32[8,128]{1,0:T(8,128)S(1)}, u32[]{:S(2)}, u32[]{:S(2)}) collective-permute-start(f32[8,128]{1,0:T(8,128)S(1)} %add.55), channel_id=1, source_target_pairs={{0,8},{4,12},{8,0},{12,4},{16,24},{20,28},{24,16},{28,20},{1,9},{5... | collective-permute-start | bytes 12296 | tf_op jit(solution)/shard_map/ppermute | solution.py:457
  39.8 9.5 %collective-permute-start.6 = (f32[8,128]{1,0:T(8,128)S(1)}, f32[8,128]{1,0:T(8,128)S(1)}, u32[]{:S(2)}, u32[]{:S(2)}) collective-permute-start(f32[8,128]{1,0:T(8,128)S(1)} %add.56), channel_id=1, source_target_pairs={{0,16},{4,20},{8,24},{12,28},{16,0},{20,4},{24,8},{28,12},{1,17},{... | collective-permute-start | bytes 12296 | tf_op jit(solution)/shard_map/ppermute | solution.py:457
  201.2 1.0 copy-start.3
  201.2 83.2 %reduce-scatter.8.cloned.1.call-start = ((), (), s32[]{:S(2)}) async-start(), calls=%async_computation.6 | async-start | bytes 2457600 | tf_op jit(solution)/shard_map/reduce_scatter | solution.py:606
  201.8 23.4 %copy-start = (bf16[480,1920]{1,0:T(8,128)(2,1)S(1)}, bf16[480,1920]{1,0:T(8,128)(2,1)}, u32[]{:S(2)}) copy-start(bf16[480,1920]{1,0:T(8,128)(2,1)} %get-tuple-element.71.gu_ref) | copy-start | bytes 5529604
  201.8 23.4 %copy-start.2 = (bf16[480,480]{1,0:T(8,128)(2,1)S(1)}, bf16[480,480]{1,0:T(8,128)(2,1)}, u32[]{:S(2)}) copy-start(bf16[480,480]{1,0:T(8,128)(2,1)} %get-tuple-element.70.go_ref) | copy-start | bytes 1382404
  201.9 97.1 %reduce-scatter.10.cloned.1.call-start = ((), (), s32[]{:S(2)}) async-start(), calls=%async_computation.7 | async-start | bytes 2918400
  202.2 1.6 collective-permute-start.7
  203.9 10.1 %collective-permute-start.8 = (f32[160,512]{1,0:T(8,128)S(1)}, f32[160,512]{1,0:T(8,128)S(1)}, u32[]{:S(2)}, u32[]{:S(2)}) collective-permute-start(f32[160,512]{1,0:T(8,128)S(1)} %add.58), channel_id=1, source_target_pairs={{0,2},{1,3},{2,0},{3,1},{4,6},{5,7},{6,4},{7,5},{8,10},{9,11},{10,... | collective-permute-start | bytes 983048 | tf_op jit(solution)/shard_map/ppermute | solution.py:457
  214.0 9.3 %collective-permute-start.9 = (f32[160,512]{1,0:T(8,128)S(1)}, f32[160,512]{1,0:T(8,128)S(1)}, u32[]{:S(2)}, u32[]{:S(2)}) collective-permute-start(f32[160,512]{1,0:T(8,128)S(1)} %add.59), channel_id=1, source_target_pairs={{0,4},{4,0},{8,12},{12,8},{16,20},{20,16},{24,28},{28,24},{1,5},{5... | collective-permute-start | bytes 983048 | tf_op jit(solution)/shard_map/ppermute | solution.py:457
  223.4 8.5 %collective-permute-start.10 = (f32[160,512]{1,0:T(8,128)S(1)}, f32[160,512]{1,0:T(8,128)S(1)}, u32[]{:S(2)}, u32[]{:S(2)}) collective-permute-start(f32[160,512]{1,0:T(8,128)S(1)} %add.60), channel_id=1, source_target_pairs={{0,8},{4,12},{8,0},{12,4},{16,24},{20,28},{24,16},{28,20},{1,9},{5... | collective-permute-start | bytes 983048 | tf_op jit(solution)/shard_map/ppermute | solution.py:457
  232.0 15.5 %collective-permute-start.11 = (f32[160,512]{1,0:T(8,128)S(1)}, f32[160,512]{1,0:T(8,128)S(1)}, u32[]{:S(2)}, u32[]{:S(2)}) collective-permute-start(f32[160,512]{1,0:T(8,128)S(1)} %add.61), channel_id=1, source_target_pairs={{0,16},{4,20},{8,24},{12,28},{16,0},{20,4},{24,8},{28,12},{1,17},{... | collective-permute-start | bytes 983048 | tf_op jit(solution)/shard_map/ppermute | solution.py:457
  248.2 18.1 %copy-start.6 = (f32[1,6240]{1,0:T(1,128)S(1)}, f32[1,6240]{1,0:T(1,128)}, u32[]{:S(2)}) copy-start(f32[1,6240]{1,0:T(1,128)} %param.33) | copy-start | bytes 74884
  255.7 15.5 %copy-start.4 = (f32[16,512]{1,0:T(8,128)S(1)}, f32[16,512]{1,0:T(8,128)}, u32[]{:S(2)}) copy-start(f32[16,512]{1,0:T(8,128)} %get-tuple-element.74.own_ref) | copy-start | bytes 98308
  257.3 1.4 collective-permute-start.12
  258.8 5.8 %collective-permute-start.13 = (f32[8,4320]{1,0:T(8,128)S(1)}, f32[8,4320]{1,0:T(8,128)S(1)}, u32[]{:S(2)}, u32[]{:S(2)}) collective-permute-start(f32[8,4320]{1,0:T(8,128)S(1)} %fusion), channel_id=1, source_target_pairs={{0,2},{1,3},{2,0},{3,1},{4,6},{5,7},{6,4},{7,5},{8,10},{9,11},{10,... | collective-permute-start | bytes 414728 | tf_op jit(solution)/shard_map/ppermute | solution.py:457
  264.6 5.1 %collective-permute-start.14 = (f32[8,4320]{1,0:T(8,128)S(1)}, f32[8,4320]{1,0:T(8,128)S(1)}, u32[]{:S(2)}, u32[]{:S(2)}) collective-permute-start(f32[8,4320]{1,0:T(8,128)S(1)} %add.64), channel_id=1, source_target_pairs={{0,4},{4,0},{8,12},{12,8},{16,20},{20,16},{24,28},{28,24},{1,5},{5... | collective-permute-start | bytes 414728 | tf_op jit(solution)/shard_map/ppermute | solution.py:457
  269.7 5.1 %collective-permute-start.15 = (f32[8,4320]{1,0:T(8,128)S(1)}, f32[8,4320]{1,0:T(8,128)S(1)}, u32[]{:S(2)}, u32[]{:S(2)}) collective-permute-start(f32[8,4320]{1,0:T(8,128)S(1)} %add.65), channel_id=1, source_target_pairs={{0,8},{4,12},{8,0},{12,4},{16,24},{20,28},{24,16},{28,20},{1,9},{5... | collective-permute-start | bytes 414728 | tf_op jit(solution)/shard_map/ppermute | solution.py:457
  274.9 7.5 %collective-permute-start.16 = (f32[8,4320]{1,0:T(8,128)S(1)}, f32[8,4320]{1,0:T(8,128)S(1)}, u32[]{:S(2)}, u32[]{:S(2)}) collective-permute-start(f32[8,4320]{1,0:T(8,128)S(1)} %add.66), channel_id=1, source_target_pairs={{0,16},{4,20},{8,24},{12,28},{16,0},{20,4},{24,8},{28,12},{1,17},{... | collective-permute-start | bytes 414728 | tf_op jit(solution)/shard_map/ppermute | solution.py:457
Sparse Core Ops, SparseCore 0:
  10.2 26.7 all-gather.2
  39.1 23.1 all-gather.4
  201.4 27.5 reduce-scatter.5
  231.5 30.6 reduce-scatter.7
  264.6 34.2 reduce-scatter.9

commit v2 on v1

v2 whole, which is shorter than its diff:
```python
from functools import partial

import jax
import jax.numpy as jnp
import numpy as np
from jax import lax
from jax.experimental import pallas as pl
from jax.experimental.pallas import tpu as pltpu
from jax.sharding import PartitionSpec as P

D = 480
HEADS = 20
HDIM = 24
V = 33
PAD = 32
TOK = 40
WIDE = 512
EPS = 1e-05
BETA = 0.9
RATE_WIDE = 20000.0
RATE_LOWER = 3000.0
RATE_VECTOR = 20000.0
RATE_FINAL = 40000.0
RATE_EMBED = 60000.0
RATE_HEAD = 3000.0
CLIP = 0.005
F32 = jnp.float32
B16 = jnp.bfloat16
MIB = 2**20


def params(limit=56):
    return pltpu.CompilerParams(vmem_limit_bytes=limit * MIB)


def nn(left, right):
    return jnp.dot(left, right, preferred_element_type=F32)


def nt(left, right):
    return lax.dot_general(left, right, (((1,), (1,)), ((), ())), preferred_element_type=F32)


def tn(left, right):
    return lax.dot_general(left, right, (((0,), (0,)), ((), ())), preferred_element_type=F32)


def thirds(value):
    top = value.astype(B16)
    rest = value - top.astype(F32)
    middle = rest.astype(B16)
    return top, middle, (rest - middle.astype(F32)).astype(B16)


def thirds_rows(value):
    return jnp.concatenate([part.astype(F32) for part in thirds(value)], 0).astype(B16)


def fold_rows(value):
    return value[0:8] + value[8:16] + value[16:24]


def exact_nt(left, right):
    return lax.dot_general(
        left, right, (((1,), (1,)), ((), ())),
        precision=lax.Precision.HIGHEST, preferred_element_type=F32,
    )


def exact_nn(left, right):
    return jnp.dot(left, right, precision=lax.Precision.HIGHEST, preferred_element_type=F32)


def norm_parts(value):
    center = value - jnp.mean(value, -1, keepdims=True)
    spread = jnp.mean(center * center, -1, keepdims=True)
    rstd = lax.rsqrt(spread + EPS)
    return center * rstd, rstd


def norm_back(grad, unit, rstd, gain):
    inner = grad * gain
    first = jnp.mean(inner, -1, keepdims=True)
    second = jnp.mean(inner * unit, -1, keepdims=True)
    return (
        rstd * (inner - first - unit * second),
        jnp.sum(grad * unit, 0, keepdims=True),
        jnp.sum(grad, 0, keepdims=True),
    )


def half_turn(value):
    return jnp.concatenate([value[HDIM // 2 :], value[: HDIM // 2]], 0)


def tail(rows, cols, ones):
    index = lax.broadcasted_iota(jnp.int32, (rows, cols), 0)
    return jnp.where(index < ones, 1.0, 0.0).astype(F32)


def lane_tail(rows, cols):
    index = lax.broadcasted_iota(jnp.int32, (rows, cols), 1)
    return jnp.where(index == 0, 1.0, 0.0).astype(F32)


def tables(length):
    half = HDIM // 2
    freq = np.float32(10000.0) ** (-np.arange(half, dtype=np.float32) * np.float32(2.0) / np.float32(HDIM))
    angle = np.arange(length, dtype=np.float32)[None, :] * freq.astype(np.float32)[:, None]
    cosine, sine = np.cos(angle), np.sin(angle)
    return (
        jnp.asarray(np.concatenate([cosine, cosine], 0), F32),
        jnp.asarray(np.concatenate([-sine, sine], 0), F32),
    )


def error_kernel(group, err_ref, errd_ref, q_ref, qd_ref, out_ref, row_ref):
    rows = err_ref.shape[0]
    out_ref[...] = jnp.zeros_like(out_ref)
    row_ref[...] = jnp.zeros_like(row_ref)
    row_ref[:, 0:rows] = exact_nt(q_ref[...], err_ref[...])
    out_ref[0:8, :] = pltpu.roll(row_ref[...], rows * group[0], 1)
    start = pl.multiple_of(8 + 8 * group[0], 8)
    out_ref[pl.ds(start, 8), 0:D] = exact_nt(qd_ref[...], errd_ref[...])


def embed_kernel(tok_ref, emb_ref, w_ref, vec_ref, cos_ref, sin_ref,
                 x_ref, h_ref, q_ref, k_ref, v_ref, emb_s):
    step = tok_ref.shape[1]

    @pl.when(pl.program_id(0) == 0)
    def _():
        emb_s[...] = jnp.zeros_like(emb_s)
        emb_s[0:V, :] = emb_ref[...]

    index = lax.broadcasted_iota(jnp.int32, (TOK, step), 0)
    hot = jnp.where(index == tok_ref[...], 1.0, 0.0).astype(F32)
    hot = jnp.concatenate([hot, hot, hot], 0).astype(B16)
    x = tn(hot, thirds_rows(emb_s[...]))
    x_ref[...] = x
    unit, _ = norm_parts(x)
    normed = unit * vec_ref[:, 0:D] + vec_ref[:, D : 2 * D]
    act = nn(normed.astype(B16), w_ref[...]) + vec_ref[:, 2 * D : 5 * D]
    h_ref[...] = jnp.concatenate([normed.T, tail(16, step, 1)], 0).astype(B16)
    turned = act.T
    cosine, sine = cos_ref[...], sin_ref[...]
    zeros = tail(PAD - HDIM, step, 0)
    ones = tail(PAD - HDIM, step, 3)
    for head in range(HEADS):
        low = HDIM * head
        query = turned[low : low + HDIM]
        query = (query * cosine + half_turn(query) * sine) * HDIM ** (-0.5)
        q_ref[head] = jnp.concatenate([query, zeros], 0).astype(B16)
        keys = turned[D + low : D + low + HDIM]
        keys = keys * cosine + half_turn(keys) * sine
        k_ref[head] = jnp.concatenate([keys, zeros], 0).astype(B16)
        value = turned[2 * D + low : 2 * D + low + HDIM]
        v_ref[head] = jnp.concatenate([value, ones], 0).astype(B16)


def rows_of(value):
    return value.astype(F32).T.astype(B16)


def attend_kernel(q_ref, k_ref, v_ref, mix_ref, inv_ref, p_ref):
    scores = nn(rows_of(k_ref[0]), q_ref[0])
    top = jnp.max(scores, 0, keepdims=True)
    probs = jnp.exp(scores - top).astype(B16)
    p_ref[0] = probs
    out = nn(v_ref[0], probs)
    inverse = 1.0 / out[HDIM : HDIM + 1]
    mix_ref[...] = out[0:HDIM] * inverse
    inv_ref[0] = inverse


def gelu_parts(upper):
    size = jnp.abs(upper) * (0.5**0.5)
    bell = jnp.exp(-0.5 * upper * upper)
    t = 1.0 / (1.0 + 0.3275911 * size)
    poly = t * (0.254829592 + t * (-0.284496736 + t * (1.421413741 + t * (-1.453152027 + t * 1.061405429))))
    lower = 0.5 * poly * bell
    cdf = jnp.where(upper < 0, lower, 1.0 - lower)
    return upper * cdf, cdf + upper * (0.3989422804014327 * bell)


def middle_kernel(mixa_ref, mixb_ref, inva_ref, invb_ref, x_ref, mask_ref, tgt_ref, count_ref, vec_ref, fin_ref,
                  head_ref, wr_ref, wd_ref, q_ref, qd_ref,
                  dm_ref, dx_ref, gr_ref, gd_ref, s_ref, e_ref,
                  acc_o, acc_u, acc_d, head_s, hid_s, slope_s):
    pid = pl.program_id(0)
    step = x_ref.shape[0]
    wide = wd_ref.shape[0]
    wo = slice(wide, wide + D)

    @pl.when(pid == 0)
    def _():
        acc_o[...] = jnp.zeros_like(acc_o)
        acc_u[...] = jnp.zeros_like(acc_u)
        acc_d[...] = jnp.zeros_like(acc_d)
        e_ref[...] = jnp.zeros_like(e_ref)
        s_ref[...] = jnp.zeros_like(s_ref)
        head_s[...] = jnp.zeros_like(head_s)
        head_s[0:V, 0 : D + 1] = head_ref[...]

    mix = jnp.concatenate([mixa_ref[...], mixb_ref[...]], 0)
    half = inva_ref.shape[0]
    mixed = jnp.concatenate([mix, tail(16, step, 1)], 0).astype(B16)
    middle = x_ref[...] + tn(mixed[0:D], wr_ref[:, wo]) + vec_ref[:, 5 * D : 6 * D]
    unit2, rstd2 = norm_parts(middle)
    gain2 = vec_ref[:, 6 * D : 7 * D]
    normed2 = unit2 * gain2 + vec_ref[:, 7 * D : 8 * D]
    normed2 = jnp.concatenate([normed2, lane_tail(step, WIDE - D)], 1).astype(B16)
    bias_up = vec_ref[:, 9 * D :]
    block = 384
    for low in range(0, wide, block):
        cut = slice(low, low + block)
        upper = nn(normed2[:, 0:D], wr_ref[:, cut]) + bias_up[:, cut]
        hidden, slope = gelu_parts(upper)
        hid_s[:, cut] = hidden.astype(B16)
        slope_s[:, cut] = slope
    resid = middle + nn(hid_s[...], wd_ref[...]) + vec_ref[:, 8 * D : 9 * D]
    unit3, rstd3 = norm_parts(resid)
    final = unit3 * fin_ref[0:1, :] + fin_ref[1:2, :]
    final = jnp.concatenate([final, lane_tail(step, WIDE - D)], 1).astype(B16)

    lanes = lax.broadcasted_iota(jnp.int32, (TOK, WIDE), 1)
    bias = jnp.sum(jnp.where(lanes == D, head_s[...], 0.0), 1, keepdims=True)
    table = head_s[:, 0:D].astype(B16)
    rows = lax.broadcasted_iota(jnp.int32, (TOK, step), 0)
    logits = jnp.where(rows < V, nt(table, final[:, 0:D]) + bias, -1e30)
    shifted = logits - jnp.max(logits, 0, keepdims=True)
    expo = jnp.exp(shifted)
    total = jnp.sum(expo, 0, keepdims=True)
    picks = rows == tgt_ref[...]
    weight = mask_ref[...].astype(F32)
    picked = jnp.sum(jnp.where(picks, shifted, 0.0), 0, keepdims=True)
    loss = jnp.sum((jnp.log(total) - picked) * weight, 1, keepdims=True)
    grad_logits = (expo / total - jnp.where(picks, 1.0, 0.0)) * (weight * (1.0 / count_ref[...]))
    grad_logits = grad_logits.astype(B16)
    e_ref[16 : 16 + TOK, :] += nn(grad_logits, final)
    grad_resid, grad_fg, grad_fb = norm_back(tn(grad_logits, table), unit3, rstd3, fin_ref[0:1, :])

    grad_y = grad_resid.astype(B16)
    acc_d[...] += tn(hid_s[...], grad_y)
    for low in range(0, wide, block):
        cut = slice(low, low + block)
        grad_hidden = nt(grad_y, wd_ref[cut, :])
        hid_s[:, cut] = (grad_hidden * slope_s[:, cut]).astype(B16)
    acc_u[...] += tn(normed2, hid_s[...])
    grad_mid, grad_g2, grad_b2 = norm_back(nt(hid_s[...], wr_ref[:, 0:wide]), unit2, rstd2, gain2)
    grad_mid = grad_mid + grad_resid
    dx_ref[...] = grad_mid
    branch = grad_mid.astype(B16)
    acc_o[...] += nn(mixed, branch)
    grad_mixed = nt(wr_ref[:, wo], branch).astype(B16).astype(F32)
    zeros = tail(PAD - HDIM - 3, step, 0)
    for head in range(HEADS):
        cut = slice(HDIM * head, HDIM * head + HDIM)
        inverse = inva_ref[head] if head < half else invb_ref[head - half]
        scaled = (grad_mixed[cut] * inverse).astype(B16).astype(F32)
        delta = -jnp.sum(scaled * mix[cut], 0, keepdims=True)
        top, mid, low = thirds(delta)
        dm_ref[head] = jnp.concatenate(
            [scaled, top.astype(F32), mid.astype(F32), low.astype(F32), zeros], 0
        ).astype(B16)
    e_ref[1:2, 0:D] += grad_g2
    e_ref[2:3, 0:D] += grad_b2
    e_ref[3:4, 0:D] += jnp.sum(grad_y.astype(F32), 0, keepdims=True)
    e_ref[8:9, 0:D] += grad_fg
    e_ref[9:10, 0:D] += grad_fb
    e_ref[10:11, :] += jnp.broadcast_to(loss, (1, WIDE))

    @pl.when(pid == pl.num_programs(0) - 1)
    def _():
        e_ref[0:1, 0:D] = acc_o[D : D + 1, :]
        for part in range(wide // D):
            e_ref[4 + part : 5 + part, 0:D] = acc_u[D : D + 1, D * part : D * part + D]
        go = acc_o[0:D, :].astype(B16)
        gu = acc_u[0:D, :].astype(B16)
        gr_ref[:, 0:wide] = gu
        gr_ref[:, wo] = go
        gd_ref[...] = acc_d[...].astype(B16)
        sketch = nt(thirds_rows(q_ref[:, 3 * D : 4 * D]), go) + nt(thirds_rows(q_ref[:, 4 * D :]), gu)
        s_ref[0:8, 0:D] = fold_rows(sketch)
        start = thirds_rows(qd_ref[...])
        for part in range(wide // D):
            piece = nt(start, gd_ref[D * part : D * part + D, :])
            s_ref[8 + 8 * part : 16 + 8 * part, 0:D] = fold_rows(piece)


def attend_back_kernel(p_ref, q_ref, k_ref, v_ref, dm_ref, cos_ref, sin_ref, da_ref):
    cosine, sine = cos_ref[...], sin_ref[...]
    parts = [[], [], []]
    for head in range(p_ref.shape[0]):
        probs = p_ref[head]
        grad = dm_ref[head]
        slope = nn(rows_of(v_ref[head]), grad)
        grad_scores = (probs.astype(F32) * slope).astype(B16)
        grad_value = nt(grad, probs)[0:HDIM]
        grad_keys = nt(q_ref[head], grad_scores)[0:HDIM]
        grad_query = nn(k_ref[head], grad_scores)[0:HDIM] * HDIM ** (-0.5)
        parts[0].append(grad_query * cosine + half_turn(grad_query * sine))
        parts[1].append(grad_keys * cosine + half_turn(grad_keys * sine))
        parts[2].append(grad_value)
    for index in range(3):
        da_ref[index] = jnp.concatenate(parts[index], 0).astype(B16)


def input_kernel(group, tok_ref, daa_ref, dab_ref, h_ref, x_ref, dx_ref, w_ref, vec_ref, q_ref, s_ref, serr_ref, e_ref,
                 g_ref, *rest):
    *out_refs, out_ref, acc_w, acc_e = rest
    pid = pl.program_id(0)
    step = x_ref.shape[0]

    @pl.when(pid == 0)
    def _():
        acc_w[...] = jnp.zeros_like(acc_w)
        acc_e[...] = jnp.zeros_like(acc_e)
        out_ref[...] = jnp.zeros_like(out_ref)

    da = jnp.concatenate([ref[part] for part in range(3) for ref in (daa_ref, dab_ref)], 0)
    acc_w[...] += nt(h_ref[...], da)
    grad = nn(w_ref[...], da).T
    unit, rstd = norm_parts(x_ref[...])
    grad_x, grad_g, grad_b = norm_back(grad, unit, rstd, vec_ref[:, 0:D])
    grad_x = grad_x + dx_ref[...]
    index = lax.broadcasted_iota(jnp.int32, (TOK, step), 0)
    hot = jnp.where(index == tok_ref[...], 1.0, 0.0).astype(B16)
    for part in thirds(grad_x):
        acc_e[...] += nn(hot, part)
    out_ref[40:41, 0:D] += grad_g
    out_ref[41:42, 0:D] += grad_b

    @pl.when(pid == pl.num_programs(0) - 1)
    def _():
        for part in range(3):
            out_ref[42 + part : 43 + part, 0:D] = acc_w[D : D + 1, D * part : D * part + D]
        g = acc_w[0:D, :].astype(B16)
        g_ref[...] = g
        out_ref[0:40, :] = s_ref[...] + serr_ref[...]
        out_ref[0:8, 0:D] += fold_rows(nt(thirds_rows(q_ref[:, 0 : 3 * D]), g))
        out_ref[45:48, :] = e_ref[8:11, :]
        out_ref[48:56, :] = e_ref[0:8, :]
        out_ref[56 : 56 + V, 0:D] = acc_e[0:V, :]
        out_ref[56 + V : 56 + 2 * V, :] = e_ref[16 : 16 + V, :]
        size = out_refs[0].shape[0]
        for place, ref in enumerate(out_refs):
            ref[...] = out_ref[pl.ds(pl.multiple_of((group[0] ^ place) * size, 8), size), :]


def orthonormal(sketch, gram):
    basis = jnp.zeros_like(sketch[0])
    count = gram.shape[0]
    index = lax.broadcasted_iota(jnp.int32, (count, 1), 0)
    out = [jnp.zeros_like(part) for part in sketch]
    left = list(sketch)
    for step in range(count):
        pivot = gram[step : step + 1, step : step + 1]
        scale = 1.0 / jnp.sqrt(pivot)
        column = gram[:, step : step + 1] * scale
        row = gram[step : step + 1, :] * scale
        column = jnp.where(index > step, column, 0.0)
        gram = gram - column * row
        for place in range(len(left)):
            base = left[place][step : step + 1, :] * scale
            out[place] = jnp.where(index == step, base, out[place])
            left[place] = left[place] - column * base
    return out


def factor_kernel(group, *refs):
    count = (len(refs) - 10) // 2
    chunks, rest = refs[:count], refs[count:]
    gi_ref, gr_ref, gd_ref, err_ref, errd_ref, a_ref, p_ref, own_ref, ownd_ref = rest[:9]
    out_refs, f_s = rest[9:-1], rest[-1]
    rows, wide_cols = err_ref.shape
    parts = gd_ref.shape[0] // D
    hidden = gd_ref.shape[0]
    size = chunks[0].shape[0]
    for place, ref in enumerate(chunks):
        a_ref[pl.ds(pl.multiple_of((group[0] ^ place) * size, 8), size), :] = ref[...]
    wide = a_ref[0:8, 0:D]
    down = [a_ref[8 + 8 * part : 16 + 8 * part, 0:D] for part in range(parts)]
    gram = exact_nt(wide, wide)
    (wide,) = orthonormal([wide], gram)
    gram = exact_nt(down[0], down[0])
    for part in range(1, parts):
        gram = gram + exact_nt(down[part], down[part])
    down = orthonormal(down, gram)
    p_ref[...] = jnp.zeros_like(p_ref)
    p_ref[0:8, 0:D] = wide
    for part in range(parts):
        p_ref[8 + 8 * part : 16 + 8 * part, 0:D] = down[part]
    own = pltpu.roll(p_ref[0:8, :], (WIDE - rows * group[0]) % WIDE, 1)[:, 0:rows]
    own_down = p_ref[pl.ds(pl.multiple_of(8 + 8 * group[0], 8), 8), :][:, 0:D]
    own_ref[...] = own
    ownd_ref[...] = own_down
    three = thirds_rows(wide)
    f_s[...] = jnp.zeros_like(f_s)
    f_s[:, 0:wide_cols] = exact_nn(own, err_ref[...])
    f_s[:, 0 : 3 * D] += fold_rows(nn(three, gi_ref[...]))
    f_s[:, 4 * D : 4 * D + hidden] += fold_rows(nn(three, gr_ref[:, 0:hidden]))
    f_s[:, 3 * D : 4 * D] += fold_rows(nn(three, gr_ref[:, hidden:]))
    total = exact_nn(own_down, errd_ref[...])
    for part in range(parts):
        total = total + fold_rows(nn(thirds_rows(down[part]), gd_ref[D * part : D * part + D, :]))
    f_s[:, wide_cols : wide_cols + D] = total
    size = out_refs[0].shape[1]
    for place, ref in enumerate(out_refs):
        ref[...] = f_s[:, pl.ds(pl.multiple_of((group[0] ^ place) * size, 128), size)]


def six(left, right):
    first, second = thirds(left), thirds(right)
    order = ((0, 0), (0, 1), (1, 0), (1, 1), (0, 2), (2, 0))
    left = jnp.concatenate([first[i].astype(F32) for i, _ in order], 0).astype(B16)
    right = jnp.concatenate([second[j].astype(F32) for _, j in order], 0).astype(B16)
    return tn(left, right)


def renew(weight, moment, grad, scale, rate):
    new_moment = BETA * moment + scale * grad
    return weight - rate * new_moment, new_moment


def finish_kernel(replicas, group, *refs):
    count = len(refs) - 39
    chunks, rest = refs[:count], refs[count:]
    (a_ref, p_ref, own_ref, ownd_ref, gi_ref, gr_ref, gd_ref,
     w_ref, wd_ref, m_ref, md_ref, err_ref, errd_ref,
     vec_ref, vmom_ref, fin_ref, fmom_ref, emb_ref, emom_ref, head_ref, hmom_ref,
     norm_ref, nq_ref, nqd_ref, nw_ref, nwd_ref, nm_ref, nmd_ref, ne_ref, ned_ref,
     nvec_ref, nvmom_ref, nfin_ref, nfmom_ref, nemb_ref, nemom_ref, nhead_ref, nhmom_ref, f_s) = rest
    wide_cols = err_ref.shape[1]
    hidden = wide_cols - 4 * D
    size = chunks[0].shape[1]
    for place, ref in enumerate(chunks):
        f_s[:, pl.ds(pl.multiple_of((group[0] ^ place) * size, 128), size)] = ref[...]
    factor, factor_down = f_s[:, 0:wide_cols], f_s[:, wide_cols : wide_cols + D]
    nq_ref[...] = factor
    nqd_ref[...] = factor_down
    a = a_ref[...]
    square = jnp.sum(a[40:47, 0:D] * a[40:47, 0:D]) + jnp.sum(a[48:56, 0:D] * a[48:56, 0:D])
    emb, top = a[56 : 56 + V, 0:D], a[56 + V : 56 + 2 * V, 0 : D + 1]
    square = square + jnp.sum(emb * emb) + jnp.sum(top * top)
    basis = p_ref[...]
    gram = exact_nt(basis[0:8, 0:D], basis[0:8, 0:D])
    square = square + jnp.sum(gram * exact_nt(factor, factor))
    gram = jnp.zeros((8, 8), F32)
    for part in range(1, basis.shape[0] // 8):
        piece = basis[8 * part : 8 * part + 8, 0:D]
        gram = gram + exact_nt(piece, piece)
    square = square + jnp.sum(gram * exact_nt(factor_down, factor_down))
    norm = jnp.sqrt(square)
    norm_ref[...] = jnp.broadcast_to(norm, norm_ref.shape)
    scale = jnp.minimum(1.0, CLIP / norm)

    approx = six(own_ref[...], factor)
    nw_ref[...], nm_ref[...] = renew(w_ref[...], m_ref[...], approx, scale, RATE_WIDE)
    share = approx * (1.0 / replicas)
    for cut, ref, start in (
        (slice(0, 3 * D), gi_ref, 0), (slice(3 * D, 4 * D), gr_ref, hidden), (slice(4 * D, wide_cols), gr_ref, 0),
    ):
        size = cut.stop - cut.start
        ne_ref[:, cut] = ref[:, start : start + size].astype(F32) + err_ref[:, cut] - share[:, cut]
    approx = six(ownd_ref[...], factor_down)
    nwd_ref[...], nmd_ref[...] = renew(wd_ref[...], md_ref[...], approx, scale, RATE_LOWER)
    ned_ref[...] = gd_ref[...].astype(F32) + errd_ref[...] - approx * (1.0 / replicas)

    places = (40, 41, 42, 43, 44, 48, 49, 50, 51, 52, 53, 54, 55)
    for row, place in enumerate(places):
        cut = slice(D * row, D * row + D)
        nvec_ref[:, cut], nvmom_ref[:, cut] = renew(
            vec_ref[:, cut], vmom_ref[:, cut], a[place : place + 1, 0:D], scale, RATE_VECTOR
        )
    nfin_ref[...], nfmom_ref[...] = renew(fin_ref[...], fmom_ref[...], a[45:47, 0:D], scale, RATE_FINAL)
    nemb_ref[...], nemom_ref[...] = renew(emb_ref[...], emom_ref[...], emb, scale, RATE_EMBED)
    nhead_ref[...], nhmom_ref[...] = renew(head_ref[...], hmom_ref[...], top, scale, RATE_HEAD)


def swap(value, axis, bit):
    size = lax.axis_size(axis)
    return lax.ppermute(value, axis, [(i, i ^ bit) for i in range(size)])


def bits_of(axis):
    size, bit, out = lax.axis_size(axis), 1, []
    while bit < size:
        out.append(bit)
        bit *= 2
    return out


def tie(*values):
    return lax.optimization_barrier(values)


def add_chunks(pieces):
    got = [swap(piece, "grp", place) for place, piece in enumerate(pieces) if place]
    total = pieces[0]
    for piece in got:
        total = total + piece
    for bit in bits_of("rep"):
        total = total + swap(total, "rep", bit)
    return [total] + [swap(total, "grp", place) for place in range(1, len(pieces))]


def whole(shape):
    return pl.BlockSpec(shape, lambda *_: (0,) * len(shape))


def shards(tokens, mask, targets, mats_d, mats_down, mom_d, mom_down, err_d, err_down, q_d, q_down,
           vectors, vec_mom, final_norm, final_mom, embed, embed_mom, head, head_mom):
    length = tokens.shape[1]
    wide = mats_d.shape[2]
    hidden = wide - 4 * D
    rows = mats_d.shape[1]
    rows_down = mats_down.shape[1]
    step = 256
    steps = length // step
    index = lax.axis_index("grp").astype(jnp.int32)
    group = index.reshape(1)
    members = lax.axis_size("grp")
    cosine, sine = tables(length)
    q_t, qd_t = q_d[0].T, q_down[0].T
    head_t = head.T
    err, errd = err_d[0, 0], err_down[0, 0]

    def call(kernel, name, grid, ins, outs, shapes, scratch=()):
        return pl.pallas_call(
            kernel,
            grid_spec=pltpu.PrefetchScalarGridSpec(
                num_scalar_prefetch=1, grid=grid, in_specs=ins, out_specs=outs, scratch_shapes=scratch
            ),
            out_shape=shapes,
            compiler_params=params(),
            name=name,
        )

    shape = jax.ShapeDtypeStruct
    rounds = [("grp", bit) for bit in bits_of("grp")] + [("rep", bit) for bit in bits_of("rep")]

    def advance(value, times=1):
        for _ in range(min(times, len(rounds))):
            value = value + swap(value, *rounds.pop(0))
        return value

    wide16 = mats_d[0].astype(B16)
    w_in = wide16[None, :, : 3 * D]
    counted = jnp.broadcast_to(jnp.sum(mask.astype(F32)), (8, 128))
    for turn, bit in enumerate(reversed(bits_of("grp"))):
        other = swap(w_in, "grp", bit)
        more = advance(counted)
        if turn == 0:
            err_sketch = call(
                error_kernel, "error_sketch", (1,),
                [whole((rows, wide)), whole((rows_down, D)), whole((8, wide)), whole((8, D))],
                whole((40, WIDE)), shape((40, WIDE), F32), [pltpu.VMEM((8, WIDE), F32)],
            )(group, err, errd, q_t, qd_t)
            other, more, err_sketch = tie(other, more, err_sketch)
        else:
            other, more = tie(other, more)
        counted = more
        mine = (index & bit) == 0
        w_in = jnp.stack([jnp.where(mine, w_in, other), jnp.where(mine, other, w_in)], -3)
    w_in = w_in.reshape(-1, 3 * D)
    w_rest = lax.all_gather(
        jnp.concatenate([wide16[:, 4 * D :], wide16[:, 3 * D : 4 * D]], 1), "grp", axis=0, tiled=True
    )
    w_down = lax.all_gather(mats_down[0].astype(B16), "grp", axis=0, tiled=True)

    cols = pl.BlockSpec((1, step), lambda i, *_: (0, i))
    flat = pl.BlockSpec((step, D), lambda i, *_: (i, 0))
    heads = pl.BlockSpec((HEADS, PAD, step), lambda i, *_: (0, 0, i))
    wave = pl.BlockSpec((HDIM, step), lambda i, *_: (0, i))
    ext = pl.BlockSpec((D + 16, step), lambda i, *_: (0, i))
    more = advance(counted)
    x, h_t, query, keys, value = pl.pallas_call(
        embed_kernel,
        grid=(steps,),
        in_specs=[cols, whole((V, D)), whole((D, 3 * D)), whole(vectors.shape), wave, wave],
        out_specs=[flat, ext, heads, heads, heads],
        out_shape=[shape((length, D), F32), shape((D + 16, length), B16)]
        + [shape((HEADS, PAD, length), B16)] * 3,
        scratch_shapes=[pltpu.VMEM((TOK, D), F32)],
        compiler_params=params(),
        name="embed_project",
    )(tokens, embed, w_in, vectors, cosine, sine)
    query, counted = tie(query, more)

    half = HEADS // 2
    mixes, inverses, probs = [], [], []
    for part in range(2):
        one = pl.BlockSpec((1, PAD, length), lambda i, part=part: (i + half * part, 0, 0))
        more = advance(counted, 1 + part * len(rounds))
        mix, inverse, prob = pl.pallas_call(
            attend_kernel,
            grid=(half,),
            in_specs=[one, one, one],
            out_specs=[
                pl.BlockSpec((HDIM, length), lambda i: (i, 0)),
                pl.BlockSpec((1, 1, length), lambda i: (i, 0, 0)),
                pl.BlockSpec((1, length, length), lambda i: (i, 0, 0)),
            ],
            out_shape=[
                shape((half * HDIM, length), F32),
                shape((half, 1, length), F32),
                shape((half, length, length), B16),
            ],
            compiler_params=params(),
            name="attend",
        )(query, keys, value)
        mix, query, counted = tie(mix, query, more)
        mixes.append(mix)
        inverses.append(inverse)
        probs.append(prob)
    counted = counted[0:1, 0:1]

    grad_mix, grad_mid, g_rest, g_down, sketch, early = pl.pallas_call(
        middle_kernel,
        grid=(steps,),
        in_specs=[pl.BlockSpec((half * HDIM, step), lambda i: (0, i))] * 2
        + [pl.BlockSpec((half, 1, step), lambda i: (0, 0, i))] * 2
        + [
            flat, cols, cols, whole((1, 1)), whole(vectors.shape), whole((2, D)),
            whole((V, D + 1)), whole((D, D + hidden)), whole((hidden, D)),
            whole((8, wide)), whole((8, D)),
        ],
        out_specs=[
            heads, flat, whole((D, D + hidden)), whole((hidden, D)), whole((40, WIDE)), whole((56, WIDE)),
        ],
        out_shape=[
            shape((HEADS, PAD, length), B16),
            shape((length, D), F32),
            shape((D, D + hidden), B16),
            shape((hidden, D), B16),
            shape((40, WIDE), F32),
            shape((56, WIDE), F32),
        ],
        scratch_shapes=[
            pltpu.VMEM((D + 16, D), F32),
            pltpu.VMEM((WIDE, hidden), F32),
            pltpu.VMEM((hidden, D), F32),
            pltpu.VMEM((TOK, WIDE), F32),
            pltpu.VMEM((step, hidden), B16),
            pltpu.VMEM((step, hidden), F32),
        ],
        compiler_params=params(),
        name="feed_and_loss",
    )(*mixes, *inverses, x, mask, targets, counted, vectors, final_norm, head_t,
      w_rest, w_down, q_t, qd_t)

    scatter = partial(lax.psum_scatter, axis_name="grp", scatter_dimension=0, tiled=True)
    own_down = scatter(g_down)
    own_rest = scatter(g_rest)
    pair = 2
    turned = half // pair
    grad_acts = []
    for part in range(2):
        two = pl.BlockSpec((pair, PAD, length), lambda i, part=part: (i + turned * part, 0, 0))
        grad_act = pl.pallas_call(
            attend_back_kernel,
            grid=(turned,),
            in_specs=[
                pl.BlockSpec((pair, length, length), lambda i: (i, 0, 0)),
                two, two, two, two, whole((HDIM, length)), whole((HDIM, length)),
            ],
            out_specs=pl.BlockSpec((3, pair * HDIM, length), lambda i: (0, i, 0)),
            out_shape=shape((3, half * HDIM, length), B16),
            compiler_params=params(),
            name="attend_back",
        )(probs[part], query, keys, value, grad_mix, cosine, sine)
        if part == 0:
            own_down, grad_act, grad_mix = tie(own_down, grad_act, grad_mix)
        grad_acts.append(grad_act)

    act = pl.BlockSpec((3, half * HDIM, step), lambda i, *_: (0, 0, i))
    size = 128 // members
    g_in, *pieces = call(
        input_kernel, "input_grads", (steps,),
        [
            cols, act, act, ext, flat, flat, whole((D, 3 * D)),
            whole(vectors.shape), whole((8, wide)), whole((40, WIDE)), whole((40, WIDE)), whole((56, WIDE)),
        ],
        [whole((D, 3 * D))] + [whole((size, WIDE))] * members,
        [shape((D, 3 * D), B16)] + [shape((size, WIDE), F32)] * members,
        [pltpu.VMEM((128, WIDE), F32), pltpu.VMEM((D + 16, 3 * D), F32), pltpu.VMEM((TOK, D), F32)],
    )(group, tokens, *grad_acts, h_t, x, grad_mid, w_in, vectors, q_t, sketch, err_sketch, early)
    own_rest, *pieces = tie(own_rest, *pieces)
    own_in = scatter(g_in)

    chunks = add_chunks(pieces)
    span = -(-(wide + WIDE) // (128 * members)) * 128
    shared, basis, own, ownd, *pieces = call(
        factor_kernel, "left_factors", (1,),
        [whole((size, WIDE))] * members
        + [
            whole((D, 3 * D)), whole((D, D + hidden)), whole((hidden, D)),
            whole((rows, wide)), whole((rows_down, D)),
        ],
        [whole((128, WIDE)), whole((40, WIDE)), whole((8, rows)), whole((8, rows_down))]
        + [whole((8, span))] * members,
        [
            shape((128, WIDE), F32), shape((40, WIDE), F32), shape((8, rows), F32), shape((8, rows_down), F32),
        ]
        + [shape((8, span), F32)] * members,
        [pltpu.VMEM((8, span * members), F32)],
    )(group, *chunks, g_in, g_rest, g_down, err, errd)
    chunks = add_chunks(pieces)

    same = lambda value: shape(value.shape, F32)
    replicas = lax.axis_size("rep")
    small = (vectors, vec_mom, final_norm, final_mom, embed, embed_mom, head_t, head_mom.T)
    given = (
        *chunks, shared, basis, own, ownd, own_in, own_rest, own_down,
        mats_d[0], mats_down[0], mom_d[0], mom_down[0], err, errd, *small,
    )
    shapes = [
        shape((8, 128), F32), shape((8, wide), F32), shape((8, D), F32),
        same(mats_d[0]), same(mats_down[0]), same(mats_d[0]), same(mats_down[0]), same(err), same(errd),
    ] + [same(item) for item in small]
    outs = call(
        partial(finish_kernel, replicas), "finish", (1,),
        [whole(item.shape) for item in given], [whole(item.shape) for item in shapes], shapes,
        [pltpu.VMEM((8, span * members), F32)],
    )(group, *given)
    (norm, new_q, new_qd, new_wide, new_down, new_mom_wide, new_mom_dn, new_err, new_errd,
     new_vec, new_vmom, new_fin, new_fmom, new_emb, new_emom, new_head, new_hmom) = outs
    return (
        shared[47, 0],
        counted[0, 0],
        norm[0, 0],
        new_wide[None],
        new_down[None],
        new_mom_wide[None],
        new_mom_dn[None],
        new_err[None, None],
        new_errd[None, None],
        own.T[None],
        ownd.T[None],
        new_q.T[None],
        new_qd.T[None],
        new_vec,
        new_vmom,
        new_fin,
        new_fmom,
        new_emb,
        new_emom,
        new_head.T,
        new_hmom.T,
    )


def solution(mesh):
    whole_seq = P(("rep", "grp"), None)
    by_rows = P(None, "grp", None)
    by_replica = P("rep", None, "grp", None)
    placed = (
        (whole_seq,) * 3 + (by_rows,) * 4 + (by_replica,) * 2 + (P(),) * 10
    )
    given = (P(),) * 3 + (by_rows,) * 4 + (by_replica,) * 2 + (by_rows,) * 2 + (P(),) * 10
    return jax.shard_map(shards, mesh=mesh, in_specs=placed, out_specs=given, check_vma=False)
```

time: 320 us -> 268 us (0.84)
  waiting for transfers between devices: 84.5 us -> 37.4 us
  local copies, waits for them, and re-layouts: 21.4 us -> 6.78 us
  starting transfers between devices: 24 us -> 31.2 us
  Pallas kernels: 166 us -> 172 us
    ppermute x17 -> x25, waiting for transfers between devices: 69.3 us -> 34.2 us  [swap(): return lax.ppermute(value, axis, [(i, i ^ bit) for i in range(size)])]
    unnamed x6 -> x5, waiting for transfers between devices: 15.1 us -> 0.59 us
    slice x9 -> x4, local copies, waits for them, and re-layouts: 11.2 us -> 1.85 us  [the longest x1 1.2 us: shards(): shared[47, 0]]
    ppermute x17 -> x25, starting transfers between devices: 23.8 us -> 31 us  [swap(): return lax.ppermute(value, axis, [(i, i ^ bit) for i in range(size)])]
    pallas_call x7 -> x9, Pallas kernels: 159 us -> 165 us  [the longest x2 50.4 us: shards(): pl.pallas_call(attend_back_kernel, grid=(turned,), in_specs=[pl.BlockSpec...]
    reshape x4 -> x0, local copies, waits for them, and re-layouts: 4.3 us -> none  [the longest x1 1.46 us: shards(): new_vec.reshape(1, -1)]
  transfers between devices with their start and end apart: 22 -> 30, of which waited for: 16 -> 17; matrix products, arithmetic and copies ran while one was open for 7% -> 3% of each run, Pallas kernels for 19% -> 47%
where the time goes in v2:
time: 268 us
  Pallas kernels  172 us (64%)
  waiting for transfers between devices  37.4 us (14%)
  starting transfers between devices  31.2 us (12%)
  between operations  14.1 us (5%)
  local copies, waits for them, and re-layouts  6.78 us (3%)
  other arithmetic  6.49 us (2%)
    pallas_call x2, Pallas kernels, shards(): pl.pallas_call(attend_back_kernel, grid=(turned,), in_specs=[pl.BlockSpec...  50.4 us
    pallas_call x2, Pallas kernels, shards(): pl.pallas_call(attend_kernel, grid=(half,), in_specs=[one, one, one], out...  43.1 us
    pallas_call x1, Pallas kernels, shards(): pl.pallas_call(middle_kernel, grid=(steps,), in_specs=[pl.BlockSpec((half...  38.1 us
    ppermute x25, waiting for transfers between devices, swap(): return lax.ppermute(value, axis, [(i, i ^ bit) for i in range(size)])  34.2 us
    ppermute x25, starting transfers between devices, swap(): return lax.ppermute(value, axis, [(i, i ^ bit) for i in range(size)])  31 us
    pallas_call x1, Pallas kernels, shards(): call(input_kernel, 'input_grads', (steps,), [cols, act, act, ext, flat, f...  11.6 us
    pallas_call x1, Pallas kernels, shards(): call(partial(finish_kernel, replicas), 'finish', (1,), [whole(item.shape)...  9.23 us
    pallas_call x1, Pallas kernels, shards(): call(factor_kernel, 'left_factors', (1,), [whole((size, WIDE))] * members...  7.42 us
  transfers between devices with their start and end apart: 30, of which 17 were waited for; matrix products, arithmetic and copies ran while one was open for 3% of the time, Pallas kernels for 47%

profile of v2, /device:TPU:0, one launch (start us, length us, event | category | flops | bytes accessed | tf_op | source)
XLA Modules:
  0.0 267.9 jit_solution(9101041126122103269)
XLA Ops:
  7.2 2.2 bitcast_convert_fusion
  9.8 0.9 pad_maximum_fusion.2
  10.7 3.0 %collective-permute-start = (bf16[1,120,1440]{2,1,0:T(8,128)(2,1)S(1)}, bf16[1,120,1440]{2,1,0:T(8,128)(2,1)S(1)}, u32[]{:S(2)}, u32[]{:S(2)}) collective-permute-start(bf16[1,120,1440]{2,1,0:T(8,128)(2,1)S(1)} %slice_bitcast_fusion), channel_id=1, source_target_pairs={{0,2},{1,3},{2,0},{3,1},{4,6},{5,7},{6,4},{7,5},{8,10},{9,11},{10,... | collective-permute-start | bytes 1036808 | tf_op jit(solution)/shard_map/ppermute | solution.py:483
  13.8 0.6 convert_reduce_fusion
  14.4 0.6 broadcast_in_dim.37
  15.1 4.8 %error_sketch.1.serr_ref = f32[40,512]{1,0:T(8,128)} custom-call(s32[1]{0:T(128)} %bitcast.group, f32[120,3840]{1,0:T(8,128)} %bitcast.56, f32[480,480]{1,0:T(8,128)} %bitcast.61, f32[8,3840]{1,0:T(8,128)} %bitcast.67, f32[8,480]{1,0:T(8,128)} %bitcast.74), custom_call_target="tpu_custom_call" | custom-call | tf_op jit(solution)/shard_map/error_sketch/pallas_call | solution.py:555
  19.9 0.6 broadcast_add_fusion
  20.6 3.0 %collective-permute-done = bf16[1,120,1440]{2,1,0:T(8,128)(2,1)S(1)} collective-permute-done((bf16[1,120,1440]{2,1,0:T(8,128)(2,1)S(1)}, bf16[1,120,1440]{2,1,0:T(8,128)(2,1)S(1)}, u32[]{:S(2)}, u32[]{:S(2)}) %collective-permute-start) | collective-permute-done | bytes 345632 | tf_op jit(solution)/shard_map/ppermute | solution.py:483
  23.8 2.5 collective-permute-start.3
  26.4 1.6 collective-permute-done.3
  28.0 1.1 collective-permute-start.4
  29.1 0.1 select_bitcast_fusion.1
  29.2 0.1 pad_maximum_fusion
  29.4 1.2 copy.43
  30.6 7.3 %embed_project.1 = (f32[1024,480]{1,0:T(8,128)}, bf16[496,1024]{1,0:T(8,128)(2,1)}, bf16[20,32,1024]{2,1,0:T(8,128)(2,1)}, bf16[20,32,1024]{2,1,0:T(8,128)(2,1)}, bf16[20,32,1024]{2,1,0:T(8,128)(2,1)}) custom-call(s32[1,1024]{1,0:T(1,128)} %tok_ref.3, f32[33,480]{1,0:T(8,128)} %refs_21_.1, bf16[480,1440]{1,0:T(8,128)(2,1)} %bitcast.59, f32[1,6240]{1,0:T(1,128)} %refs_17_.1, ...), custom_call_target="tpu_custom_call" | custom-call | tf_op jit(solution)/shard_map/embed_project/pallas_call | solution.py:578
  37.9 1.9 collective-permute-start.5
  39.7 21.5 %attend.2 = (f32[240,1024]{1,0:T(8,128)}, f32[10,1,1024]{2,1,0:T(1,128)}, bf16[10,1024,1024]{2,1,0:T(8,128)(2,1)}) custom-call(bf16[20,32,1024]{2,1,0:T(8,128)(2,1)} %get-tuple-element.111.q_ref, bf16[20,32,1024]{2,1,0:T(8,128)(2,1)} %get-tuple-element.95.k_ref, bf16[20,32,1024]{2,1,0:T(8,128)(2,1)} %get-tuple-element.96.v_ref), custom_call_target="tpu_custom_call" | custom-call | tf_op jit(solution)/shard_map/attend/pallas_call | solution.py:596
  61.3 3.0 %collective-permute-start.6 = (f32[8,128]{1,0:T(8,128)S(1)}, f32[8,128]{1,0:T(8,128)S(1)}, u32[]{:S(2)}, u32[]{:S(2)}) collective-permute-start(f32[8,128]{1,0:T(8,128)S(1)} %add.60), channel_id=1, source_target_pairs={{0,16},{4,20},{8,24},{12,28},{16,0},{20,4},{24,8},{28,12},{1,17},{... | collective-permute-start | bytes 12296 | tf_op jit(solution)/shard_map/ppermute | solution.py:483
  64.3 21.5 %attend.3 = (f32[240,1024]{1,0:T(8,128)}, f32[10,1,1024]{2,1,0:T(1,128)}, bf16[10,1024,1024]{2,1,0:T(8,128)(2,1)}) custom-call(bf16[20,32,1024]{2,1,0:T(8,128)(2,1)} %get-tuple-element.111.q_ref, bf16[20,32,1024]{2,1,0:T(8,128)(2,1)} %get-tuple-element.95.k_ref, bf16[20,32,1024]{2,1,0:T(8,128)(2,1)} %get-tuple-element.96.v_ref), custom_call_target="tpu_custom_call" | custom-call | tf_op jit(solution)/shard_map/attend/pallas_call | solution.py:596
  85.8 0.5 slice.19.count_ref
  86.3 38.1 %feed_and_loss.1 = (bf16[20,32,1024]{2,1,0:T(8,128)(2,1)}, f32[1024,480]{1,0:T(8,128)}, bf16[480,2400]{1,0:T(8,128)(2,1)}, bf16[1920,480]{1,0:T(8,128)(2,1)}, f32[40,512]{1,0:T(8,128)}, /*index=5*/f32[56,512]{1,0:T(8,128)}) custom-call(f32[240,1024]{1,0:T(8,128)} %get-tuple-element.99.mixa_ref, f32[240,1024]{1,0:T(8,128)} %get-tuple-element.103.mixb_ref, ...), custom_call_target="tpu_custom_call" | custom-call | tf_op jit(solution)/shard_map/feed_and_loss/pallas_call | solution.py:619
  124.5 0.5 reduce-scatter.10.cloned.1.call-update
  125.1 25.4 %attend_back.2.daa_ref = bf16[3,240,1024]{2,1,0:T(8,128)(2,1)} custom-call(bf16[10,1024,1024]{2,1,0:T(8,128)(2,1)} %get-tuple-element.110.p_ref, bf16[20,32,1024]{2,1,0:T(8,128)(2,1)} %get-tuple-element.111.q_ref, bf16[20,32,1024]{2,1,0:T(8,128)(2,1)} %get-tuple-element.95.k_ref, bf16[20,32,1024]{2,1,0:T(8,128)(2,1)} %get-tuple-element.96.v_ref, ...), custom_call_target="tpu_custom_call" | custom-call | tf_op jit(solution)/shard_map/attend_back/pallas_call | solution.py:661
  150.4 2.6 reduce-scatter.6.cloned.1.call-done.refs_10_
  153.0 25.0 %attend_back.3.dab_ref = bf16[3,240,1024]{2,1,0:T(8,128)(2,1)} custom-call(bf16[10,1024,1024]{2,1,0:T(8,128)(2,1)} %get-tuple-element.114.p_ref, bf16[20,32,1024]{2,1,0:T(8,128)(2,1)} %get-tuple-element.111.q_ref, bf16[20,32,1024]{2,1,0:T(8,128)(2,1)} %get-tuple-element.95.k_ref, bf16[20,32,1024]{2,1,0:T(8,128)(2,1)} %get-tuple-element.96.v_ref, ...), custom_call_target="tpu_custom_call" | custom-call | tf_op jit(solution)/shard_map/attend_back/pallas_call | solution.py:661
  178.0 11.6 %input_grads.1 = (bf16[480,1440]{1,0:T(8,128)(2,1)}, f32[32,512]{1,0:T(8,128)}, f32[32,512]{1,0:T(8,128)}, f32[32,512]{1,0:T(8,128)}, f32[32,512]{1,0:T(8,128)}) custom-call(s32[1]{0:T(128)} %bitcast.group, s32[1,1024]{1,0:T(1,128)} %tok_ref.3, bf16[3,240,1024]{2,1,0:T(8,128)(2,1)} %attend_back.2.daa_ref, bf16[3,240,1024]{2,1,0:T(8,128)(2,1)} %attend_back.3.dab_ref, ...), custom_call_target="tpu_custom_call" | custom-call | tf_op jit(solution)/shard_map/input_grads/pallas_call | solution.py:679
  189.8 0.4 collective-permute-start.8
  190.2 1.5 collective-permute-start.9
  191.7 3.3 %collective-permute-done.8 = f32[32,512]{1,0:T(8,128)S(1)} collective-permute-done((f32[32,512]{1,0:T(8,128)}, f32[32,512]{1,0:T(8,128)S(1)}, u32[]{:S(2)}, u32[]{:S(2)}) %collective-permute-start.8) | collective-permute-done | bytes 65568 | tf_op jit(solution)/shard_map/ppermute | solution.py:483
  195.0 0.5 collective-permute-done.9
  195.5 0.9 add_add_fusion
  196.3 1.6 collective-permute-start.10
  197.9 2.7 %collective-permute-done.10 = f32[32,512]{1,0:T(8,128)S(1)} collective-permute-done((f32[32,512]{1,0:T(8,128)S(1)}, f32[32,512]{1,0:T(8,128)S(1)}, u32[]{:S(2)}, u32[]{:S(2)}) %collective-permute-start.10) | collective-permute-done | bytes 65568 | tf_op jit(solution)/shard_map/ppermute | solution.py:483
  200.7 1.5 collective-permute-start.11
  202.2 2.8 %collective-permute-done.11 = f32[32,512]{1,0:T(8,128)S(1)} collective-permute-done((f32[32,512]{1,0:T(8,128)S(1)}, f32[32,512]{1,0:T(8,128)S(1)}, u32[]{:S(2)}, u32[]{:S(2)}) %collective-permute-start.11) | collective-permute-done | bytes 65568 | tf_op jit(solution)/shard_map/ppermute | solution.py:483
  205.0 2.5 collective-permute-start.12
  207.5 2.8 %collective-permute-done.12 = f32[32,512]{1,0:T(8,128)S(1)} collective-permute-done((f32[32,512]{1,0:T(8,128)S(1)}, f32[32,512]{1,0:T(8,128)S(1)}, u32[]{:S(2)}, u32[]{:S(2)}) %collective-permute-start.12) | collective-permute-done | bytes 65568 | tf_op jit(solution)/shard_map/ppermute | solution.py:483
  210.4 0.8 collective-permute-start.14
  211.2 1.0 collective-permute-start.13
  212.2 3.9 %collective-permute-done.15.refs_3_ = f32[32,512]{1,0:T(8,128)S(1)} collective-permute-done((f32[32,512]{1,0:T(8,128)S(1)}, f32[32,512]{1,0:T(8,128)S(1)}, u32[]{:S(2)}, u32[]{:S(2)}) %collective-permute-start.15) | collective-permute-done | bytes 65568 | tf_op jit(solution)/shard_map/ppermute | solution.py:483
  216.1 1.9 collective-permute-done.14.refs_2_
  218.0 0.6 copy-done.4
  218.7 0.6 copy-done.5
  219.3 7.4 %left_factors.1 = (f32[128,512]{1,0:T(8,128)}, f32[40,512]{1,0:T(8,128)}, f32[8,120]{1,0:T(8,128)}, f32[8,480]{1,0:T(8,128)}, f32[8,1152]{1,0:T(8,128)}, /*index...) custom-call(s32[1]{0:T(128)} %bitcast.group, f32[32,512]{1,0:T(8,128)} %copy-done.1, f32[32,512]{1,0:T(8,128)} %copy-done.5, ...), custom_call_target="tpu_custom_call" | custom-call | tf_op jit(solution)/shard_map/left_factors/pallas_call | solution.py:694
  226.7 0.9 collective-permute-start.16
  227.6 0.9 collective-permute-start.17
  228.5 0.5 collective-permute-start.18
  229.0 2.9 %collective-permute-done.17 = f32[8,1152]{1,0:T(8,128)S(1)} collective-permute-done((f32[8,1152]{1,0:T(8,128)}, f32[8,1152]{1,0:T(8,128)S(1)}, u32[]{:S(2)}, u32[]{:S(2)}) %collective-permute-start.17) | collective-permute-done | bytes 36896 | tf_op jit(solution)/shard_map/ppermute | solution.py:483
  231.9 0.5 collective-permute-done.18
  232.4 0.8 add_add_fusion.1
  233.2 1.6 collective-permute-start.19
  234.8 2.4 collective-permute-done.19
  237.2 1.5 collective-permute-start.20
  238.7 2.5 collective-permute-done.20
  241.2 2.6 collective-permute-start.21
  243.8 2.2 collective-permute-done.21
  246.1 1.2 collective-permute-start.23
  247.3 0.6 collective-permute-start.22
  248.0 1.2 slice.22
  249.2 0.4 collective-permute-done.24.refs_3_
  249.6 0.7 collective-permute-done.23.refs_2_
  250.3 0.6 copy-done.7
  250.9 9.2 %finish.1 = (f32[8,128]{1,0:T(8,128)}, f32[8,3840]{1,0:T(8,128)}, f32[8,480]{1,0:T(8,128)}, f32[120,3840]{1,0:T(8,128)}, f32[480,480]{1,0:T(8,128)}, /*index=5*/...) custom-call(s32[1]{0:T(128)} %bitcast.group, ...), custom_call_target="tpu_custom_call" | custom-call | tf_op jit(solution)/shard_map/finish/pallas_call | solution.py:722
  260.2 1.2 slice.23
  (60 shorter events, 1.2 us)
Async XLA Ops:
  7.2 2.3 copy-start
  7.2 79.1 %all-gather.5.cloned.1.call-start = ((), (), s32[]{:S(2)}) async-start(), calls=%async_computation.4 | async-start | bytes 2457600 | tf_op jit(solution)/shard_map/all_gather | solution.py:570
  9.4 76.9 %all-gather.3.cloned.1.call-start = ((), (), s32[]{:S(2)}) async-start(), calls=%async_computation.3 | async-start | bytes 2918400 | tf_op jit(solution)/shard_map/all_gather | solution.py:567
  9.6 4.2 %copy-start.9 = (s32[1,1024]{1,0:T(1,128)S(1)}, s32[1,1024]{1,0:T(1,128)}, u32[]{:S(2)}) copy-start(s32[1,1024]{1,0:T(1,128)} %mask_ref.1) | copy-start | bytes 12292
  10.7 142.4 %reduce-scatter.6.cloned.1.call-start = ((), (), s32[]{:S(2)}) async-start(), calls=%async_computation.5 | async-start | bytes 2457600 | tf_op jit(solution)/shard_map/reduce_scatter | solution.py:654
  10.7 12.9 %collective-permute-start = (bf16[1,120,1440]{2,1,0:T(8,128)(2,1)S(1)}, bf16[1,120,1440]{2,1,0:T(8,128)(2,1)S(1)}, u32[]{:S(2)}, u32[]{:S(2)}) collective-permute-start(bf16[1,120,1440]{2,1,0:T(8,128)(2,1)S(1)} %slice_bitcast_fusion), channel_id=1, source_target_pairs={{0,2},{1,3},{2,0},{3,1},{4,6},{5,7},{6,4},{7,5},{8,10},{9,11},{10,... | collective-permute-start | bytes 1036808 | tf_op jit(solution)/shard_map/ppermute | solution.py:483
  15.0 4.9 %collective-permute-start.1 = (f32[8,128]{1,0:T(8,128)S(1)}, f32[8,128]{1,0:T(8,128)S(1)}, u32[]{:S(2)}, u32[]{:S(2)}) collective-permute-start(f32[8,128]{1,0:T(8,128)S(1)} %broadcast_in_dim.37), channel_id=1, source_target_pairs={{0,1},{1,0},{2,3},{3,2},{4,5},{5,4},{6,7},{7,6},{8,9},{9,8},{10,11... | collective-permute-start | bytes 12296 | tf_op jit(solution)/shard_map/ppermute | solution.py:483
  23.8 4.3 %collective-permute-start.2 = (bf16[1,2,120,1440]{3,2,1,0:T(8,128)(2,1)S(1)}, bf16[1,2,120,1440]{3,2,1,0:T(8,128)(2,1)S(1)}, u32[]{:S(2)}, u32[]{:S(2)}) collective-permute-start(bf16[1,2,120,1440]{3,2,1,0:T(8,128)(2,1)S(1)} %pad_maximum_fusion.1), channel_id=1, source_target_pairs={{0,1},{1,0},{2,3},{3,2},{4,5},{5,4},{6,7},{7,6},{8,9},{9,8},{10,11... | collective-permute-start | bytes 2073608 | tf_op jit(solution)/shard_map/ppermute | solution.py:483
  23.8 4.2 %collective-permute-start.3 = (f32[8,128]{1,0:T(8,128)S(1)}, f32[8,128]{1,0:T(8,128)S(1)}, u32[]{:S(2)}, u32[]{:S(2)}) collective-permute-start(f32[8,128]{1,0:T(8,128)S(1)} %broadcast_add_fusion), channel_id=1, source_target_pairs={{0,2},{1,3},{2,0},{3,1},{4,6},{5,7},{6,4},{7,5},{8,10},{9,11},{10,... | collective-permute-start | bytes 12296 | tf_op jit(solution)/shard_map/ppermute | solution.py:483
  28.0 9.8 %collective-permute-start.4 = (f32[8,128]{1,0:T(8,128)S(1)}, f32[8,128]{1,0:T(8,128)S(1)}, u32[]{:S(2)}, u32[]{:S(2)}) collective-permute-start(f32[8,128]{1,0:T(8,128)S(1)} %add.58), channel_id=1, source_target_pairs={{0,4},{4,0},{8,12},{12,8},{16,20},{20,16},{24,28},{28,24},{1,5},{5... | collective-permute-start | bytes 12296 | tf_op jit(solution)/shard_map/ppermute | solution.py:483
  37.9 23.4 %collective-permute-start.5 = (f32[8,128]{1,0:T(8,128)S(1)}, f32[8,128]{1,0:T(8,128)S(1)}, u32[]{:S(2)}, u32[]{:S(2)}) collective-permute-start(f32[8,128]{1,0:T(8,128)S(1)} %add.59), channel_id=1, source_target_pairs={{0,8},{4,12},{8,0},{12,4},{16,24},{20,28},{24,16},{28,20},{1,9},{5... | collective-permute-start | bytes 12296 | tf_op jit(solution)/shard_map/ppermute | solution.py:483
  61.3 24.5 %collective-permute-start.6 = (f32[8,128]{1,0:T(8,128)S(1)}, f32[8,128]{1,0:T(8,128)S(1)}, u32[]{:S(2)}, u32[]{:S(2)}) collective-permute-start(f32[8,128]{1,0:T(8,128)S(1)} %add.60), channel_id=1, source_target_pairs={{0,16},{4,20},{8,24},{12,28},{16,0},{20,4},{24,8},{28,12},{1,17},{... | collective-permute-start | bytes 12296 | tf_op jit(solution)/shard_map/ppermute | solution.py:483
  124.4 65.3 %reduce-scatter.10.cloned.1.call-start = ((), (), s32[]{:S(2)}) async-start(), calls=%async_computation.7 | async-start | bytes 2918400
  125.0 125.3 %reduce-scatter.8.cloned.1.call-start = ((), (), s32[]{:S(2)}) async-start(), calls=%async_computation.6 | async-start | bytes 1843200 | tf_op jit(solution)/shard_map/reduce_scatter | solution.py:690
  189.7 1.9 collective-permute-start.7
  189.8 5.2 %collective-permute-start.8 = (f32[32,512]{1,0:T(8,128)}, f32[32,512]{1,0:T(8,128)S(1)}, u32[]{:S(2)}, u32[]{:S(2)}) collective-permute-start(f32[32,512]{1,0:T(8,128)} %get-tuple-element.127), channel_id=1, source_target_pairs={{0,2},{1,3},{2,0},{3,1},{4,6},{5,7},{6,4},{7,5},{8,10},{9,11},{10,... | collective-permute-start | bytes 196616 | tf_op jit(solution)/shard_map/ppermute | solution.py:483
  190.2 5.3 %collective-permute-start.9 = (f32[32,512]{1,0:T(8,128)}, f32[32,512]{1,0:T(8,128)S(1)}, u32[]{:S(2)}, u32[]{:S(2)}) collective-permute-start(f32[32,512]{1,0:T(8,128)} %get-tuple-element.128), channel_id=1, source_target_pairs={{0,3},{1,2},{2,1},{3,0},{4,7},{5,6},{6,5},{7,4},{8,11},{9,10},{10,... | collective-permute-start | bytes 196616 | tf_op jit(solution)/shard_map/ppermute | solution.py:483
  196.3 4.3 %collective-permute-start.10 = (f32[32,512]{1,0:T(8,128)S(1)}, f32[32,512]{1,0:T(8,128)S(1)}, u32[]{:S(2)}, u32[]{:S(2)}) collective-permute-start(f32[32,512]{1,0:T(8,128)S(1)} %add_add_fusion), channel_id=1, source_target_pairs={{0,4},{4,0},{8,12},{12,8},{16,20},{20,16},{24,28},{28,24},{1,5},{5... | collective-permute-start | bytes 196616 | tf_op jit(solution)/shard_map/ppermute | solution.py:483
  200.7 4.3 %collective-permute-start.11 = (f32[32,512]{1,0:T(8,128)S(1)}, f32[32,512]{1,0:T(8,128)S(1)}, u32[]{:S(2)}, u32[]{:S(2)}) collective-permute-start(f32[32,512]{1,0:T(8,128)S(1)} %add.65), channel_id=1, source_target_pairs={{0,8},{4,12},{8,0},{12,4},{16,24},{20,28},{24,16},{28,20},{1,9},{5... | collective-permute-start | bytes 196616 | tf_op jit(solution)/shard_map/ppermute | solution.py:483
  205.0 5.2 %collective-permute-start.12 = (f32[32,512]{1,0:T(8,128)S(1)}, f32[32,512]{1,0:T(8,128)S(1)}, u32[]{:S(2)}, u32[]{:S(2)}) collective-permute-start(f32[32,512]{1,0:T(8,128)S(1)} %add.66), channel_id=1, source_target_pairs={{0,16},{4,20},{8,24},{12,28},{16,0},{20,4},{24,8},{28,12},{1,17},{... | collective-permute-start | bytes 196616 | tf_op jit(solution)/shard_map/ppermute | solution.py:483
  210.3 7.8 %copy-start.1 = (f32[32,512]{1,0:T(8,128)}, f32[32,512]{1,0:T(8,128)S(1)}, u32[]{:S(2)}) copy-start(f32[32,512]{1,0:T(8,128)S(1)} %add.67.refs_0_) | copy-start | bytes 196612
  210.3 5.8 %collective-permute-start.15 = (f32[32,512]{1,0:T(8,128)S(1)}, f32[32,512]{1,0:T(8,128)S(1)}, u32[]{:S(2)}, u32[]{:S(2)}) collective-permute-start(f32[32,512]{1,0:T(8,128)S(1)} %add.67.refs_0_), channel_id=1, source_target_pairs={{0,3},{1,2},{2,1},{3,0},{4,7},{5,6},{6,5},{7,4},{8,11},{9,10},{10,... | collective-permute-start | bytes 196616 | tf_op jit(solution)/shard_map/ppermute | solution.py:483
  210.4 7.7 %collective-permute-start.14 = (f32[32,512]{1,0:T(8,128)S(1)}, f32[32,512]{1,0:T(8,128)S(1)}, u32[]{:S(2)}, u32[]{:S(2)}) collective-permute-start(f32[32,512]{1,0:T(8,128)S(1)} %add.67.refs_0_), channel_id=1, source_target_pairs={{0,2},{1,3},{2,0},{3,1},{4,6},{5,7},{6,4},{7,5},{8,10},{9,11},{10,... | collective-permute-start | bytes 196616 | tf_op jit(solution)/shard_map/ppermute | solution.py:483
  211.2 6.8 %collective-permute-start.13 = (f32[32,512]{1,0:T(8,128)S(1)}, f32[32,512]{1,0:T(8,128)S(1)}, u32[]{:S(2)}, u32[]{:S(2)}) collective-permute-start(f32[32,512]{1,0:T(8,128)S(1)} %add.67.refs_0_), channel_id=1, source_target_pairs={{0,1},{1,0},{2,3},{3,2},{4,5},{5,4},{6,7},{7,6},{8,9},{9,8},{10,11... | collective-permute-start | bytes 196616 | tf_op jit(solution)/shard_map/ppermute | solution.py:483
  216.1 1.9 copy-start.3
  218.0 0.6 copy-start.4
  218.7 0.6 copy-start.5
  226.7 2.3 collective-permute-start.16
  227.6 4.3 %collective-permute-start.17 = (f32[8,1152]{1,0:T(8,128)}, f32[8,1152]{1,0:T(8,128)S(1)}, u32[]{:S(2)}, u32[]{:S(2)}) collective-permute-start(f32[8,1152]{1,0:T(8,128)} %get-tuple-element.133), channel_id=1, source_target_pairs={{0,2},{1,3},{2,0},{3,1},{4,6},{5,7},{6,4},{7,5},{8,10},{9,11},{10,... | collective-permute-start | bytes 110600 | tf_op jit(solution)/shard_map/ppermute | solution.py:483
  228.5 3.9 %collective-permute-start.18 = (f32[8,1152]{1,0:T(8,128)}, f32[8,1152]{1,0:T(8,128)S(1)}, u32[]{:S(2)}, u32[]{:S(2)}) collective-permute-start(f32[8,1152]{1,0:T(8,128)} %get-tuple-element.134), channel_id=1, source_target_pairs={{0,3},{1,2},{2,1},{3,0},{4,7},{5,6},{6,5},{7,4},{8,11},{9,10},{10,... | collective-permute-start | bytes 110600 | tf_op jit(solution)/shard_map/ppermute | solution.py:483
  233.2 4.0 %collective-permute-start.19 = (f32[8,1152]{1,0:T(8,128)S(1)}, f32[8,1152]{1,0:T(8,128)S(1)}, u32[]{:S(2)}, u32[]{:S(2)}) collective-permute-start(f32[8,1152]{1,0:T(8,128)S(1)} %add_add_fusion.1), channel_id=1, source_target_pairs={{0,4},{4,0},{8,12},{12,8},{16,20},{20,16},{24,28},{28,24},{1,5},{5... | collective-permute-start | bytes 110600 | tf_op jit(solution)/shard_map/ppermute | solution.py:483
  237.2 4.0 %collective-permute-start.20 = (f32[8,1152]{1,0:T(8,128)S(1)}, f32[8,1152]{1,0:T(8,128)S(1)}, u32[]{:S(2)}, u32[]{:S(2)}) collective-permute-start(f32[8,1152]{1,0:T(8,128)S(1)} %add.71), channel_id=1, source_target_pairs={{0,8},{4,12},{8,0},{12,4},{16,24},{20,28},{24,16},{28,20},{1,9},{5... | collective-permute-start | bytes 110600 | tf_op jit(solution)/shard_map/ppermute | solution.py:483
  241.2 4.9 %collective-permute-start.21 = (f32[8,1152]{1,0:T(8,128)S(1)}, f32[8,1152]{1,0:T(8,128)S(1)}, u32[]{:S(2)}, u32[]{:S(2)}) collective-permute-start(f32[8,1152]{1,0:T(8,128)S(1)} %add.72), channel_id=1, source_target_pairs={{0,16},{4,20},{8,24},{12,28},{16,0},{20,4},{24,8},{28,12},{1,17},{... | collective-permute-start | bytes 110600 | tf_op jit(solution)/shard_map/ppermute | solution.py:483
  246.0 4.3 %copy-start.2 = (f32[8,1152]{1,0:T(8,128)}, f32[8,1152]{1,0:T(8,128)S(1)}, u32[]{:S(2)}) copy-start(f32[8,1152]{1,0:T(8,128)S(1)} %add.73.refs_0_) | copy-start | bytes 110596
  246.0 3.6 %collective-permute-start.24 = (f32[8,1152]{1,0:T(8,128)S(1)}, f32[8,1152]{1,0:T(8,128)S(1)}, u32[]{:S(2)}, u32[]{:S(2)}) collective-permute-start(f32[8,1152]{1,0:T(8,128)S(1)} %add.73.refs_0_), channel_id=1, source_target_pairs={{0,3},{1,2},{2,1},{3,0},{4,7},{5,6},{6,5},{7,4},{8,11},{9,10},{10,... | collective-permute-start | bytes 110600 | tf_op jit(solution)/shard_map/ppermute | solution.py:483
  246.1 4.2 %collective-permute-start.23 = (f32[8,1152]{1,0:T(8,128)S(1)}, f32[8,1152]{1,0:T(8,128)S(1)}, u32[]{:S(2)}, u32[]{:S(2)}) collective-permute-start(f32[8,1152]{1,0:T(8,128)S(1)} %add.73.refs_0_), channel_id=1, source_target_pairs={{0,2},{1,3},{2,0},{3,1},{4,6},{5,7},{6,4},{7,5},{8,10},{9,11},{10,... | collective-permute-start | bytes 110600 | tf_op jit(solution)/shard_map/ppermute | solution.py:483
  247.3 3.0 %collective-permute-start.22 = (f32[8,1152]{1,0:T(8,128)S(1)}, f32[8,1152]{1,0:T(8,128)S(1)}, u32[]{:S(2)}, u32[]{:S(2)}) collective-permute-start(f32[8,1152]{1,0:T(8,128)S(1)} %add.73.refs_0_), channel_id=1, source_target_pairs={{0,1},{1,0},{2,3},{3,2},{4,5},{5,4},{6,7},{7,6},{8,9},{9,8},{10,11... | collective-permute-start | bytes 110600 | tf_op jit(solution)/shard_map/ppermute | solution.py:483
  249.6 0.8 copy-start.6
  250.3 0.6 copy-start.7
  250.3 0.6 copy-start.8
Sparse Core Ops, SparseCore 0:
  10.2 24.6 all-gather.4
  37.0 25.0 all-gather.2
  124.6 28.4 reduce-scatter.5
  155.7 33.1 reduce-scatter.9
  191.4 30.3 reduce-scatter.7

commit v3 on v2

--- a/solution.py
+++ b/solution.py
@@ -124,8 +124,7 @@
     out_ref[pl.ds(start, 8), 0:D] = exact_nt(qd_ref[...], errd_ref[...])
 
 
-def embed_kernel(tok_ref, emb_ref, w_ref, vec_ref, cos_ref, sin_ref,
-                 x_ref, h_ref, q_ref, k_ref, v_ref, emb_s):
+def embed_kernel(tok_ref, emb_ref, vec_ref, x_ref, h_ref, ht_ref, emb_s):
     step = tok_ref.shape[1]
 
     @pl.when(pl.program_id(0) == 0)
@@ -140,8 +139,30 @@
     x_ref[...] = x
     unit, _ = norm_parts(x)
     normed = unit * vec_ref[:, 0:D] + vec_ref[:, D : 2 * D]
-    act = nn(normed.astype(B16), w_ref[...]) + vec_ref[:, 2 * D : 5 * D]
-    h_ref[...] = jnp.concatenate([normed.T, tail(16, step, 1)], 0).astype(B16)
+    h_ref[...] = normed.astype(B16)
+    ht_ref[...] = jnp.concatenate([normed.T, tail(16, step, 1)], 0).astype(B16)
+
+
+def spot(group, place, size, unit):
+    return pl.ds(pl.multiple_of((group[0] ^ place) * size, unit), size)
+
+
+def assemble(group, chunks, wide_s, out_s):
+    for place, ref in enumerate(chunks):
+        wide_s[spot(group, place, ref.shape[0], 8), :] = ref[...].astype(F32)
+    out_s[...] = wide_s[...].astype(B16)
+
+
+def project_kernel(members, group, h_ref, *refs):
+    chunks = refs[:members]
+    vec_ref, cos_ref, sin_ref, q_ref, k_ref, v_ref, wide_s, w_s = refs[members:]
+    step = h_ref.shape[0]
+
+    @pl.when(pl.program_id(0) == 0)
+    def _():
+        assemble(group, chunks, wide_s, w_s)
+
+    act = nn(h_ref[...], w_s[...]) + vec_ref[:, 2 * D : 5 * D]
     turned = act.T
     cosine, sine = cos_ref[...], sin_ref[...]
     zeros = tail(PAD - HDIM, step, 0)
@@ -183,10 +204,12 @@
     return upper * cdf, cdf + upper * (0.3989422804014327 * bell)
 
 
-def middle_kernel(mixa_ref, mixb_ref, inva_ref, invb_ref, x_ref, mask_ref, tgt_ref, count_ref, vec_ref, fin_ref,
-                  head_ref, wr_ref, wd_ref, q_ref, qd_ref,
-                  dm_ref, dx_ref, gr_ref, gd_ref, s_ref, e_ref,
-                  acc_o, acc_u, acc_d, head_s, hid_s, slope_s):
+def middle_kernel(members, group, mixa_ref, mixb_ref, inva_ref, invb_ref, x_ref, mask_ref, tgt_ref,
+                  count_ref, vec_ref, fin_ref, head_ref, q_ref, qd_ref, *refs):
+    chunks, chunks_down, refs = refs[:members], refs[members : 2 * members], refs[2 * members :]
+    dm_ref, dx_ref, s_ref, e_ref, *refs = refs
+    outs, outs_down, refs = refs[:members], refs[members : 2 * members], refs[2 * members :]
+    acc_o, acc_u, acc_d, head_s, hid_s, slope_s, wide_s, wr_ref, wd_ref = refs
     pid = pl.program_id(0)
     step = x_ref.shape[0]
     wide = wd_ref.shape[0]
@@ -201,6 +224,9 @@
         s_ref[...] = jnp.zeros_like(s_ref)
         head_s[...] = jnp.zeros_like(head_s)
         head_s[0:V, 0 : D + 1] = head_ref[...]
+        assemble(group, chunks, wide_s, wr_ref)
+        for place, ref in enumerate(chunks_down):
+            wd_ref[spot(group, place, ref.shape[0], 16), :] = ref[...]
 
     mix = jnp.concatenate([mixa_ref[...], mixb_ref[...]], 0)
     half = inva_ref.shape[0]
@@ -235,7 +261,7 @@
     weight = mask_ref[...].astype(F32)
     picked = jnp.sum(jnp.where(picks, shifted, 0.0), 0, keepdims=True)
     loss = jnp.sum((jnp.log(total) - picked) * weight, 1, keepdims=True)
-    grad_logits = (expo / total - jnp.where(picks, 1.0, 0.0)) * (weight * (1.0 / count_ref[...]))
+    grad_logits = (expo / total - jnp.where(picks, 1.0, 0.0)) * (weight * (1.0 / count_ref[0:1, 0:1]))
     grad_logits = grad_logits.astype(B16)
     e_ref[16 : 16 + TOK, :] += nn(grad_logits, final)
     grad_resid, grad_fg, grad_fb = norm_back(tn(grad_logits, table), unit3, rstd3, fin_ref[0:1, :])
@@ -277,15 +303,18 @@
             e_ref[4 + part : 5 + part, 0:D] = acc_u[D : D + 1, D * part : D * part + D]
         go = acc_o[0:D, :].astype(B16)
         gu = acc_u[0:D, :].astype(B16)
-        gr_ref[:, 0:wide] = gu
-        gr_ref[:, wo] = go
-        gd_ref[...] = acc_d[...].astype(B16)
         sketch = nt(thirds_rows(q_ref[:, 3 * D : 4 * D]), go) + nt(thirds_rows(q_ref[:, 4 * D :]), gu)
         s_ref[0:8, 0:D] = fold_rows(sketch)
         start = thirds_rows(qd_ref[...])
         for part in range(wide // D):
-            piece = nt(start, gd_ref[D * part : D * part + D, :])
+            piece = nt(start, acc_d[D * part : D * part + D, :].astype(B16))
             s_ref[8 + 8 * part : 16 + 8 * part, 0:D] = fold_rows(piece)
+        for place, ref in enumerate(outs):
+            at = spot(group, place, ref.shape[0], 8)
+            ref[:, 0:wide] = acc_u[at, :].astype(B16)
+            ref[:, wo] = acc_o[at, :].astype(B16)
+        for place, ref in enumerate(outs_down):
+            ref[...] = acc_d[spot(group, place, ref.shape[0], 8), :].astype(B16)
 
 
 def attend_back_kernel(p_ref, q_ref, k_ref, v_ref, dm_ref, cos_ref, sin_ref, da_ref):
@@ -306,9 +335,11 @@
         da_ref[index] = jnp.concatenate(parts[index], 0).astype(B16)
 
 
-def input_kernel(group, tok_ref, daa_ref, dab_ref, h_ref, x_ref, dx_ref, w_ref, vec_ref, q_ref, s_ref, serr_ref, e_ref,
-                 g_ref, *rest):
-    *out_refs, out_ref, acc_w, acc_e = rest
+def input_kernel(members, group, tok_ref, daa_ref, dab_ref, h_ref, x_ref, dx_ref, vec_ref, q_ref,
+                 s_ref, serr_ref, e_ref, *refs):
+    chunks, refs = refs[:members], refs[members:]
+    outs, pieces, refs = refs[:members], refs[members : 2 * members], refs[2 * members :]
+    out_ref, acc_w, acc_e, wide_s, w_s = refs
     pid = pl.program_id(0)
     step = x_ref.shape[0]
 
@@ -317,10 +348,11 @@
         acc_w[...] = jnp.zeros_like(acc_w)
         acc_e[...] = jnp.zeros_like(acc_e)
         out_ref[...] = jnp.zeros_like(out_ref)
+        assemble(group, chunks, wide_s, w_s)
 
     da = jnp.concatenate([ref[part] for part in range(3) for ref in (daa_ref, dab_ref)], 0)
     acc_w[...] += nt(h_ref[...], da)
-    grad = nn(w_ref[...], da).T
+    grad = nn(w_s[...], da).T
     unit, rstd = norm_parts(x_ref[...])
     grad_x, grad_g, grad_b = norm_back(grad, unit, rstd, vec_ref[:, 0:D])
     grad_x = grad_x + dx_ref[...]
@@ -335,17 +367,16 @@
     def _():
         for part in range(3):
             out_ref[42 + part : 43 + part, 0:D] = acc_w[D : D + 1, D * part : D * part + D]
-        g = acc_w[0:D, :].astype(B16)
-        g_ref[...] = g
         out_ref[0:40, :] = s_ref[...] + serr_ref[...]
-        out_ref[0:8, 0:D] += fold_rows(nt(thirds_rows(q_ref[:, 0 : 3 * D]), g))
+        out_ref[0:8, 0:D] += fold_rows(nt(thirds_rows(q_ref[:, 0 : 3 * D]), acc_w[0:D, :].astype(B16)))
         out_ref[45:48, :] = e_ref[8:11, :]
         out_ref[48:56, :] = e_ref[0:8, :]
         out_ref[56 : 56 + V, 0:D] = acc_e[0:V, :]
         out_ref[56 + V : 56 + 2 * V, :] = e_ref[16 : 16 + V, :]
-        size = out_refs[0].shape[0]
-        for place, ref in enumerate(out_refs):
-            ref[...] = out_ref[pl.ds(pl.multiple_of((group[0] ^ place) * size, 8), size), :]
+        for place, ref in enumerate(outs):
+            ref[...] = acc_w[spot(group, place, ref.shape[0], 8), :].astype(B16)
+        for place, ref in enumerate(pieces):
+            ref[...] = out_ref[spot(group, place, ref.shape[0], 8), :]
 
 
 def orthonormal(sketch, gram):
@@ -368,17 +399,15 @@
     return out
 
 
-def factor_kernel(group, *refs):
-    count = (len(refs) - 10) // 2
-    chunks, rest = refs[:count], refs[count:]
-    gi_ref, gr_ref, gd_ref, err_ref, errd_ref, a_ref, p_ref, own_ref, ownd_ref = rest[:9]
-    out_refs, f_s = rest[9:-1], rest[-1]
+def factor_kernel(members, group, *refs):
+    chunks, ins, rests, downs = (refs[members * part : members * part + members] for part in range(4))
+    err_ref, errd_ref, a_ref, p_ref, own_ref, ownd_ref, *refs = refs[4 * members :]
+    outs, f_s = refs[:members], refs[members]
     rows, wide_cols = err_ref.shape
-    parts = gd_ref.shape[0] // D
-    hidden = gd_ref.shape[0]
-    size = chunks[0].shape[0]
+    hidden = wide_cols - 4 * D
+    parts = hidden // D
     for place, ref in enumerate(chunks):
-        a_ref[pl.ds(pl.multiple_of((group[0] ^ place) * size, 8), size), :] = ref[...]
+        a_ref[spot(group, place, ref.shape[0], 8), :] = ref[...]
     wide = a_ref[0:8, 0:D]
     down = [a_ref[8 + 8 * part : 16 + 8 * part, 0:D] for part in range(parts)]
     gram = exact_nt(wide, wide)
@@ -391,23 +420,48 @@
     p_ref[0:8, 0:D] = wide
     for part in range(parts):
         p_ref[8 + 8 * part : 16 + 8 * part, 0:D] = down[part]
-    own = pltpu.roll(p_ref[0:8, :], (WIDE - rows * group[0]) % WIDE, 1)[:, 0:rows]
-    own_down = p_ref[pl.ds(pl.multiple_of(8 + 8 * group[0], 8), 8), :][:, 0:D]
-    own_ref[...] = own
-    ownd_ref[...] = own_down
-    three = thirds_rows(wide)
     f_s[...] = jnp.zeros_like(f_s)
-    f_s[:, 0:wide_cols] = exact_nn(own, err_ref[...])
-    f_s[:, 0 : 3 * D] += fold_rows(nn(three, gi_ref[...]))
-    f_s[:, 4 * D : 4 * D + hidden] += fold_rows(nn(three, gr_ref[:, 0:hidden]))
-    f_s[:, 3 * D : 4 * D] += fold_rows(nn(three, gr_ref[:, hidden:]))
-    total = exact_nn(own_down, errd_ref[...])
-    for part in range(parts):
-        total = total + fold_rows(nn(thirds_rows(down[part]), gd_ref[D * part : D * part + D, :]))
-    f_s[:, wide_cols : wide_cols + D] = total
-    size = out_refs[0].shape[1]
-    for place, ref in enumerate(out_refs):
-        ref[...] = f_s[:, pl.ds(pl.multiple_of((group[0] ^ place) * size, 128), size)]
+    for place in range(members):
+        piece = pltpu.roll(p_ref[0:8, :], (WIDE - rows * (group[0] ^ place)) % WIDE, 1)[:, 0:rows]
+        piece_down = p_ref[pl.ds(pl.multiple_of(8 + 8 * (group[0] ^ place), 8), 8), :][:, 0:D]
+        if place == 0:
+            own_ref[...] = piece
+            ownd_ref[...] = piece_down
+            f_s[:, 0:wide_cols] = exact_nn(piece, err_ref[...])
+            f_s[:, wide_cols : wide_cols + D] = exact_nn(piece_down, errd_ref[...])
+        three = thirds_rows(piece)
+        f_s[:, 0 : 3 * D] += fold_rows(nn(three, ins[place][...]))
+        f_s[:, 4 * D : wide_cols] += fold_rows(nn(three, rests[place][:, 0:hidden]))
+        f_s[:, 3 * D : 4 * D] += fold_rows(nn(three, rests[place][:, hidden:]))
+        f_s[:, wide_cols : wide_cols + D] += fold_rows(nn(thirds_rows(piece_down), downs[place][...]))
+    for place, ref in enumerate(outs):
+        ref[...] = f_s[:, spot(group, place, ref.shape[1], 128)]
+
+
+def merge_kernel(*refs):
+    *chunks, err_ref, out_ref = refs
+    value = err_ref[...]
+    for ref in chunks:
+        value = value + ref[...].astype(F32)
+    out_ref[...] = value
+
+
+def merge_rest_kernel(*refs):
+    *chunks, err_ref, out_ref = refs
+    value = chunks[0][...].astype(F32)
+    for ref in chunks[1:]:
+        value = value + ref[...].astype(F32)
+    hidden = value.shape[1] - D
+    out_ref[:, 0:hidden] = value[:, 0:hidden] + err_ref[:, 4 * D :]
+    out_ref[:, hidden:] = value[:, hidden:] + err_ref[:, 3 * D : 4 * D]
+
+
+def merge_in_kernel(*refs):
+    *chunks, err_ref, out_ref = refs
+    value = err_ref[:, 0 : 3 * D]
+    for ref in chunks:
+        value = value + ref[...].astype(F32)
+    out_ref[...] = value
 
 
 def six(left, right):
@@ -423,19 +477,17 @@
     return weight - rate * new_moment, new_moment
 
 
-def finish_kernel(replicas, group, *refs):
-    count = len(refs) - 39
-    chunks, rest = refs[:count], refs[count:]
-    (a_ref, p_ref, own_ref, ownd_ref, gi_ref, gr_ref, gd_ref,
-     w_ref, wd_ref, m_ref, md_ref, err_ref, errd_ref,
+def finish_kernel(members, replicas, group, *refs):
+    chunks, rest = refs[:members], refs[members:]
+    (a_ref, p_ref, own_ref, ownd_ref,
+     w_ref, wd_ref, m_ref, md_ref, ein_ref, erest_ref, errd_ref, count_ref,
      vec_ref, vmom_ref, fin_ref, fmom_ref, emb_ref, emom_ref, head_ref, hmom_ref,
-     norm_ref, nq_ref, nqd_ref, nw_ref, nwd_ref, nm_ref, nmd_ref, ne_ref, ned_ref,
+     loss_ref, total_ref, norm_ref, nq_ref, nqd_ref, nw_ref, nwd_ref, nm_ref, nmd_ref, ne_ref, ned_ref,
      nvec_ref, nvmom_ref, nfin_ref, nfmom_ref, nemb_ref, nemom_ref, nhead_ref, nhmom_ref, f_s) = rest
-    wide_cols = err_ref.shape[1]
+    wide_cols = w_ref.shape[1]
     hidden = wide_cols - 4 * D
-    size = chunks[0].shape[1]
     for place, ref in enumerate(chunks):
-        f_s[:, pl.ds(pl.multiple_of((group[0] ^ place) * size, 128), size)] = ref[...]
+        f_s[:, spot(group, place, ref.shape[1], 128)] = ref[...]
     factor, factor_down = f_s[:, 0:wide_cols], f_s[:, wide_cols : wide_cols + D]
     nq_ref[...] = factor
     nqd_ref[...] = factor_down
@@ -453,19 +505,19 @@
     square = square + jnp.sum(gram * exact_nt(factor_down, factor_down))
     norm = jnp.sqrt(square)
     norm_ref[...] = jnp.broadcast_to(norm, norm_ref.shape)
+    loss_ref[...] = a[47:48, 0:1]
+    total_ref[...] = count_ref[0:1, 0:1]
     scale = jnp.minimum(1.0, CLIP / norm)
 
     approx = six(own_ref[...], factor)
     nw_ref[...], nm_ref[...] = renew(w_ref[...], m_ref[...], approx, scale, RATE_WIDE)
     share = approx * (1.0 / replicas)
-    for cut, ref, start in (
-        (slice(0, 3 * D), gi_ref, 0), (slice(3 * D, 4 * D), gr_ref, hidden), (slice(4 * D, wide_cols), gr_ref, 0),
-    ):
-        size = cut.stop - cut.start
-        ne_ref[:, cut] = ref[:, start : start + size].astype(F32) + err_ref[:, cut] - share[:, cut]
+    ne_ref[:, 0 : 3 * D] = ein_ref[...] - share[:, 0 : 3 * D]
+    ne_ref[:, 3 * D : 4 * D] = erest_ref[:, hidden:] - share[:, 3 * D : 4 * D]
+    ne_ref[:, 4 * D :] = erest_ref[:, 0:hidden] - share[:, 4 * D :]
     approx = six(ownd_ref[...], factor_down)
     nwd_ref[...], nmd_ref[...] = renew(wd_ref[...], md_ref[...], approx, scale, RATE_LOWER)
-    ned_ref[...] = gd_ref[...].astype(F32) + errd_ref[...] - approx * (1.0 / replicas)
+    ned_ref[...] = errd_ref[...] - approx * (1.0 / replicas)
 
     places = (40, 41, 42, 43, 44, 48, 49, 50, 51, 52, 53, 54, 55)
     for row, place in enumerate(places):
@@ -495,14 +547,61 @@
     return lax.optimization_barrier(values)
 
 
-def add_chunks(pieces):
-    got = [swap(piece, "grp", place) for place, piece in enumerate(pieces) if place]
-    total = pieces[0]
-    for piece in got:
+def send_chunks(pieces):
+    return [pieces[0]] + [swap(piece, "grp", place) for place, piece in enumerate(pieces) if place]
+
+
+def add_chunks(pieces, work=()):
+    work, results = dict(work), {}
+
+    def beside(turn, moved):
+        if turn in work:
+            moved, results[turn] = tie(moved, work[turn]())
+        return moved
+
+    got = beside(0, send_chunks(pieces))
+    total = got[0]
+    for piece in got[1:]:
         total = total + piece
-    for bit in bits_of("rep"):
-        total = total + swap(total, "rep", bit)
-    return [total] + [swap(total, "grp", place) for place in range(1, len(pieces))]
+    for turn, bit in enumerate(bits_of("rep")):
+        total = total + beside(turn + 1, swap(total, "rep", bit))
+    got = [total] + [swap(total, "grp", place) for place in range(1, len(pieces))]
+    return beside(-1, got), results
+
+
+def gather_start(value):
+    first, *bits = reversed(bits_of("grp"))
+    return [value, swap(value, "grp", first)]
+
+
+def gather_end(pieces):
+    first, *bits = reversed(bits_of("grp"))
+    order = [0, first]
+    for bit in bits:
+        pieces = pieces + [swap(piece, "grp", bit) for piece in pieces]
+        order = order + [place ^ bit for place in order]
+    return [pieces[order.index(place)] for place in range(len(order))]
+
+
+def halve_start(pieces):
+    first, *bits = bits_of("grp")
+    keep = [place for place in range(len(pieces)) if not place & first]
+    return [(place, pieces[place], swap(pieces[place | first], "grp", first)) for place in keep]
+
+
+def halve_end(pairs):
+    first, *bits = bits_of("grp")
+    (_, own, other), *others = pairs
+    kept = [own, other]
+    sums = {place: (mine.astype(F32) + theirs.astype(F32)).astype(B16) for place, mine, theirs in others}
+    for bit in bits:
+        kept.append(swap(sums[bit], "grp", bit))
+        sums = {
+            place: (sums[place].astype(F32) + swap(sums[place | bit], "grp", bit).astype(F32)).astype(B16)
+            for place in sums
+            if not place & bit
+        }
+    return kept
 
 
 def whole(shape):
@@ -545,47 +644,44 @@
             value = value + swap(value, *rounds.pop(0))
         return value
 
-    wide16 = mats_d[0].astype(B16)
-    w_in = wide16[None, :, : 3 * D]
-    counted = jnp.broadcast_to(jnp.sum(mask.astype(F32)), (8, 128))
-    for turn, bit in enumerate(reversed(bits_of("grp"))):
-        other = swap(w_in, "grp", bit)
-        more = advance(counted)
-        if turn == 0:
-            err_sketch = call(
-                error_kernel, "error_sketch", (1,),
-                [whole((rows, wide)), whole((rows_down, D)), whole((8, wide)), whole((8, D))],
-                whole((40, WIDE)), shape((40, WIDE), F32), [pltpu.VMEM((8, WIDE), F32)],
-            )(group, err, errd, q_t, qd_t)
-            other, more, err_sketch = tie(other, more, err_sketch)
-        else:
-            other, more = tie(other, more)
-        counted = more
-        mine = (index & bit) == 0
-        w_in = jnp.stack([jnp.where(mine, w_in, other), jnp.where(mine, other, w_in)], -3)
-    w_in = w_in.reshape(-1, 3 * D)
-    w_rest = lax.all_gather(
-        jnp.concatenate([wide16[:, 4 * D :], wide16[:, 3 * D : 4 * D]], 1), "grp", axis=0, tiled=True
-    )
-    w_down = lax.all_gather(mats_down[0].astype(B16), "grp", axis=0, tiled=True)
-
     cols = pl.BlockSpec((1, step), lambda i, *_: (0, i))
     flat = pl.BlockSpec((step, D), lambda i, *_: (i, 0))
     heads = pl.BlockSpec((HEADS, PAD, step), lambda i, *_: (0, 0, i))
     wave = pl.BlockSpec((HDIM, step), lambda i, *_: (0, i))
     ext = pl.BlockSpec((D + 16, step), lambda i, *_: (0, i))
+
+    w_in = gather_start(mats_d[0][:, : 3 * D].astype(B16))
+    counted = jnp.broadcast_to(jnp.sum(mask.astype(F32)), (8, 128))
     more = advance(counted)
-    x, h_t, query, keys, value = pl.pallas_call(
+    err_sketch = call(
+        error_kernel, "error_sketch", (1,),
+        [whole((rows, wide)), whole((rows_down, D)), whole((8, wide)), whole((8, D))],
+        whole((40, WIDE)), shape((40, WIDE), F32), [pltpu.VMEM((8, WIDE), F32)],
+    )(group, err, errd, q_t, qd_t)
+    x, h, h_t = pl.pallas_call(
         embed_kernel,
         grid=(steps,),
-        in_specs=[cols, whole((V, D)), whole((D, 3 * D)), whole(vectors.shape), wave, wave],
-        out_specs=[flat, ext, heads, heads, heads],
-        out_shape=[shape((length, D), F32), shape((D + 16, length), B16)]
-        + [shape((HEADS, PAD, length), B16)] * 3,
+        in_specs=[cols, whole((V, D)), whole(vectors.shape)],
+        out_specs=[flat, flat, ext],
+        out_shape=[shape((length, D), F32), shape((length, D), B16), shape((D + 16, length), B16)],
         scratch_shapes=[pltpu.VMEM((TOK, D), F32)],
         compiler_params=params(),
-        name="embed_project",
-    )(tokens, embed, w_in, vectors, cosine, sine)
+        name="embed",
+    )(tokens, embed, vectors)
+    w_in, err_sketch, h, counted = tie(w_in, err_sketch, h, more)
+    w_in = gather_end(w_in)
+    rest = jnp.concatenate([mats_d[0][:, 4 * D :], mats_d[0][:, 3 * D : 4 * D]], 1).astype(B16)
+    down = mats_down[0].astype(B16)
+    more = advance(counted)
+    w_in, counted, rest, down = tie(w_in, more, rest, down)
+    w_rest, w_down = gather_start(rest), gather_start(down)
+    more = advance(counted)
+    query, keys, value = call(
+        partial(project_kernel, members), "project", (steps,),
+        [flat] + [whole((rows, 3 * D))] * members + [whole(vectors.shape), wave, wave],
+        [heads] * 3, [shape((HEADS, PAD, length), B16)] * 3,
+        [pltpu.VMEM((D, 3 * D), F32), pltpu.VMEM((D, 3 * D), B16)],
+    )(group, h, *w_in, vectors, cosine, sine)
     query, counted = tie(query, more)
 
     half = HEADS // 2
@@ -610,49 +706,48 @@
             compiler_params=params(),
             name="attend",
         )(query, keys, value)
-        mix, query, counted = tie(mix, query, more)
+        mix, query, counted, w_rest, w_down = tie(mix, query, more, w_rest, w_down)
+        if part == 0:
+            w_rest, w_down = gather_end(w_rest), gather_end(w_down)
         mixes.append(mix)
         inverses.append(inverse)
         probs.append(prob)
-    counted = counted[0:1, 0:1]
-
-    grad_mix, grad_mid, g_rest, g_down, sketch, early = pl.pallas_call(
-        middle_kernel,
-        grid=(steps,),
-        in_specs=[pl.BlockSpec((half * HDIM, step), lambda i: (0, i))] * 2
-        + [pl.BlockSpec((half, 1, step), lambda i: (0, 0, i))] * 2
+
+    everyone = [(rows, D + hidden)] * members + [(rows_down, D)] * members
+    grad_mix, grad_mid, sketch, early, *grads = call(
+        partial(middle_kernel, members), "feed_and_loss", (steps,),
+        [pl.BlockSpec((half * HDIM, step), lambda i, *_: (0, i))] * 2
+        + [pl.BlockSpec((half, 1, step), lambda i, *_: (0, 0, i))] * 2
         + [
-            flat, cols, cols, whole((1, 1)), whole(vectors.shape), whole((2, D)),
-            whole((V, D + 1)), whole((D, D + hidden)), whole((hidden, D)),
-            whole((8, wide)), whole((8, D)),
-        ],
-        out_specs=[
-            heads, flat, whole((D, D + hidden)), whole((hidden, D)), whole((40, WIDE)), whole((56, WIDE)),
-        ],
-        out_shape=[
+            flat, cols, cols, whole((8, 128)), whole(vectors.shape), whole((2, D)),
+            whole((V, D + 1)), whole((8, wide)), whole((8, D)),
+        ]
+        + [whole(item) for item in everyone],
+        [heads, flat, whole((40, WIDE)), whole((56, WIDE))] + [whole(item) for item in everyone],
+        [
             shape((HEADS, PAD, length), B16),
             shape((length, D), F32),
-            shape((D, D + hidden), B16),
-            shape((hidden, D), B16),
             shape((40, WIDE), F32),
             shape((56, WIDE), F32),
-        ],
-        scratch_shapes=[
+        ]
+        + [shape(item, B16) for item in everyone],
+        [
             pltpu.VMEM((D + 16, D), F32),
             pltpu.VMEM((WIDE, hidden), F32),
             pltpu.VMEM((hidden, D), F32),
             pltpu.VMEM((TOK, WIDE), F32),
             pltpu.VMEM((step, hidden), B16),
             pltpu.VMEM((step, hidden), F32),
+            pltpu.VMEM((D, D + hidden), F32),
+            pltpu.VMEM((D, D + hidden), B16),
+            pltpu.VMEM((hidden, D), B16),
         ],
-        compiler_params=params(),
-        name="feed_and_loss",
-    )(*mixes, *inverses, x, mask, targets, counted, vectors, final_norm, head_t,
-      w_rest, w_down, q_t, qd_t)
-
-    scatter = partial(lax.psum_scatter, axis_name="grp", scatter_dimension=0, tiled=True)
-    own_down = scatter(g_down)
-    own_rest = scatter(g_rest)
+    )(group, *mixes, *inverses, x, mask, targets, counted, vectors, final_norm, head_t, q_t, qd_t,
+      *w_rest, *w_down)
+    g_rest, g_down = grads[:members], grads[members:]
+    all_down = send_chunks(g_down)
+    all_rest = send_chunks(g_rest)
+
     pair = 2
     turned = half // pair
     grad_acts = []
@@ -670,34 +765,48 @@
             compiler_params=params(),
             name="attend_back",
         )(probs[part], query, keys, value, grad_mix, cosine, sine)
-        if part == 0:
-            own_down, grad_act, grad_mix = tie(own_down, grad_act, grad_mix)
         grad_acts.append(grad_act)
+    all_down, all_rest, grad_acts = tie(all_down, all_rest, grad_acts)
 
     act = pl.BlockSpec((3, half * HDIM, step), lambda i, *_: (0, 0, i))
     size = 128 // members
-    g_in, *pieces = call(
-        input_kernel, "input_grads", (steps,),
+    ins = [(rows, 3 * D)] * members
+    grads = call(
+        partial(input_kernel, members), "input_grads", (steps,),
         [
-            cols, act, act, ext, flat, flat, whole((D, 3 * D)),
+            cols, act, act, ext, flat, flat,
             whole(vectors.shape), whole((8, wide)), whole((40, WIDE)), whole((40, WIDE)), whole((56, WIDE)),
+        ]
+        + [whole(item) for item in ins],
+        [whole(item) for item in ins] + [whole((size, WIDE))] * members,
+        [shape(item, B16) for item in ins] + [shape((size, WIDE), F32)] * members,
+        [
+            pltpu.VMEM((128, WIDE), F32), pltpu.VMEM((D + 16, 3 * D), F32), pltpu.VMEM((TOK, D), F32),
+            pltpu.VMEM((D, 3 * D), F32), pltpu.VMEM((D, 3 * D), B16),
         ],
-        [whole((D, 3 * D))] + [whole((size, WIDE))] * members,
-        [shape((D, 3 * D), B16)] + [shape((size, WIDE), F32)] * members,
-        [pltpu.VMEM((128, WIDE), F32), pltpu.VMEM((D + 16, 3 * D), F32), pltpu.VMEM((TOK, D), F32)],
-    )(group, tokens, *grad_acts, h_t, x, grad_mid, w_in, vectors, q_t, sketch, err_sketch, early)
-    own_rest, *pieces = tie(own_rest, *pieces)
-    own_in = scatter(g_in)
-
-    chunks = add_chunks(pieces)
+    )(group, tokens, *grad_acts, h_t, x, grad_mid, vectors, q_t, sketch, err_sketch, early, *w_in)
+    g_in, pieces = grads[:members], grads[members:]
+    half_in = halve_start(g_in)
+
+    def merge(kernel, name, chunks, err, result):
+        return lambda: pl.pallas_call(
+            kernel, out_shape=shape(result, F32), compiler_params=params(), name=name
+        )(*chunks, err)
+
+    chunks, merged = add_chunks(
+        pieces,
+        (
+            (0, merge(merge_kernel, "merge_down", all_down, errd, errd.shape)),
+            (1, lambda: halve_end(half_in)),
+            (2, merge(merge_rest_kernel, "merge_rest", all_rest, err, (rows, D + hidden))),
+        ),
+    )
+    merged_down, all_in, merged_rest = (merged[turn] for turn in range(3))
     span = -(-(wide + WIDE) // (128 * members)) * 128
     shared, basis, own, ownd, *pieces = call(
-        factor_kernel, "left_factors", (1,),
-        [whole((size, WIDE))] * members
-        + [
-            whole((D, 3 * D)), whole((D, D + hidden)), whole((hidden, D)),
-            whole((rows, wide)), whole((rows_down, D)),
-        ],
+        partial(factor_kernel, members), "left_factors", (1,),
+        [whole((size, WIDE))] * members + [whole(item) for item in ins + everyone]
+        + [whole((rows, wide)), whole((rows_down, D))],
         [whole((128, WIDE)), whole((40, WIDE)), whole((8, rows)), whole((8, rows_down))]
         + [whole((8, span))] * members,
         [
@@ -705,31 +814,35 @@
         ]
         + [shape((8, span), F32)] * members,
         [pltpu.VMEM((8, span * members), F32)],
-    )(group, *chunks, g_in, g_rest, g_down, err, errd)
-    chunks = add_chunks(pieces)
+    )(group, *chunks, *g_in, *g_rest, *g_down, err, errd)
+
+    chunks, merged = add_chunks(
+        pieces, ((0, merge(merge_in_kernel, "merge_in", all_in, err, (rows, 3 * D))),)
+    )
+    merged_in = merged[0]
 
     same = lambda value: shape(value.shape, F32)
     replicas = lax.axis_size("rep")
     small = (vectors, vec_mom, final_norm, final_mom, embed, embed_mom, head_t, head_mom.T)
     given = (
-        *chunks, shared, basis, own, ownd, own_in, own_rest, own_down,
-        mats_d[0], mats_down[0], mom_d[0], mom_down[0], err, errd, *small,
+        *chunks, shared, basis, own, ownd,
+        mats_d[0], mats_down[0], mom_d[0], mom_down[0], merged_in, merged_rest, merged_down, counted, *small,
     )
     shapes = [
-        shape((8, 128), F32), shape((8, wide), F32), shape((8, D), F32),
+        shape((1, 1), F32), shape((1, 1), F32), shape((1, 1), F32), shape((8, wide), F32), shape((8, D), F32),
         same(mats_d[0]), same(mats_down[0]), same(mats_d[0]), same(mats_down[0]), same(err), same(errd),
     ] + [same(item) for item in small]
     outs = call(
-        partial(finish_kernel, replicas), "finish", (1,),
+        partial(finish_kernel, members, replicas), "finish", (1,),
         [whole(item.shape) for item in given], [whole(item.shape) for item in shapes], shapes,
         [pltpu.VMEM((8, span * members), F32)],
     )(group, *given)
-    (norm, new_q, new_qd, new_wide, new_down, new_mom_wide, new_mom_dn, new_err, new_errd,
+    (loss, total, norm, new_q, new_qd, new_wide, new_down, new_mom_wide, new_mom_dn, new_err, new_errd,
      new_vec, new_vmom, new_fin, new_fmom, new_emb, new_emom, new_head, new_hmom) = outs
     return (
-        shared[47, 0],
-        counted[0, 0],
-        norm[0, 0],
+        loss.reshape(()),
+        total.reshape(()),
+        norm.reshape(()),
         new_wide[None],
         new_down[None],
         new_mom_wide[None],

time: 268 us -> 257 us (0.959)
  Pallas kernels: 172 us -> 186 us
  between operations: 14.1 us -> 1.38 us
  waiting for transfers between devices: 37.4 us -> 31 us
  local copies, waits for them, and re-layouts: 6.78 us -> 4.04 us
    pallas_call x4 -> x8, Pallas kernels: 66.3 us -> 83.2 us  [the longest x1 38.2 us: shards(): call(partial(middle_kernel, members), 'feed_and_loss', (steps,), [pl.Bloc...]
    ppermute x25 -> x41, waiting for transfers between devices: 34.2 us -> 31 us  [swap(): return lax.ppermute(value, axis, [(i, i ^ bit) for i in range(size)])]
    slice x5 -> x3, local copies, waits for them, and re-layouts: 3.04 us -> 0.16 us  [the longest x1 0.1 us: shards(): mats_d[0][:, 3 * D:4 * D]]
    pallas_call x1, Pallas kernels: 7.28 us -> 4.45 us  [shards(): pl.pallas_call(embed_kernel, grid=(steps,), in_specs=[cols, whole((V, D))...]
    ppermute x25 -> x41, starting transfers between devices: 31 us -> 30 us  [swap(): return lax.ppermute(value, axis, [(i, i ^ bit) for i in range(size)])]
  transfers between devices with their start and end apart: 30 -> 41, of which waited for: 17 -> 12; matrix products, arithmetic and copies ran while one was open for 3% -> 2% of each run, Pallas kernels for 47% -> 46%
where the time goes in v3:
time: 257 us
  Pallas kernels  186 us (72%)
  waiting for transfers between devices  31 us (12%)
  starting transfers between devices  30 us (12%)
  other arithmetic  4.76 us (2%)
  local copies, waits for them, and re-layouts  4.04 us (2%)
    pallas_call x2, Pallas kernels, shards(): pl.pallas_call(attend_back_kernel, grid=(turned,), in_specs=[pl.BlockSpec...  50 us
    pallas_call x2, Pallas kernels, shards(): pl.pallas_call(attend_kernel, grid=(half,), in_specs=[one, one, one], out...  43.1 us
    pallas_call x1, Pallas kernels, shards(): call(partial(middle_kernel, members), 'feed_and_loss', (steps,), [pl.Bloc...  38.2 us
    ppermute x41, waiting for transfers between devices, swap(): return lax.ppermute(value, axis, [(i, i ^ bit) for i in range(size)])  31 us
    ppermute x41, starting transfers between devices, swap(): return lax.ppermute(value, axis, [(i, i ^ bit) for i in range(size)])  30 us
    pallas_call x1, Pallas kernels, shards(): call(partial(input_kernel, members), 'input_grads', (steps,), [cols, act,...  12.9 us
    pallas_call x3, Pallas kernels, merge(): pl.pallas_call(kernel, out_shape=shape(result, F32), compiler_params=para...  9.65 us
    pallas_call x1, Pallas kernels, shards(): call(partial(finish_kernel, members, replicas), 'finish', (1,), [whole(it...  8.95 us
  transfers between devices with their start and end apart: 41, of which 12 were waited for; matrix products, arithmetic and copies ran while one was open for 2% of the time, Pallas kernels for 46%

profile of v3, /device:TPU:0, one launch (start us, length us, event | category | flops | bytes accessed | tf_op | source)
XLA Modules:
  0.0 256.8 jit_solution(14320619288596352032)
XLA Ops:
  0.7 1.6 bitcast_convert_fusion.1
  2.3 3.0 %collective-permute-start = (bf16[120,1440]{1,0:T(8,128)(2,1)S(1)}, bf16[120,1440]{1,0:T(8,128)(2,1)S(1)}, u32[]{:S(2)}, u32[]{:S(2)}) collective-permute-start(bf16[120,1440]{1,0:T(8,128)(2,1)S(1)} %slice.15.refs_0_), channel_id=1, source_target_pairs={{0,2},{1,3},{2,0},{3,1},{4,6},{5,7},{6,4},{7,5},{8,10},{9,11},{10,... | collective-permute-start | bytes 1036808 | tf_op jit(solution)/shard_map/ppermute | solution.py:535
  5.3 0.6 convert_reduce_fusion
  5.9 0.6 broadcast_in_dim.33
  6.8 4.5 %embed.1 = (f32[1024,480]{1,0:T(8,128)}, bf16[1024,480]{1,0:T(8,128)(2,1)}, bf16[496,1024]{1,0:T(8,128)(2,1)}) custom-call(s32[1,1024]{1,0:T(1,128)} %tok_ref.3, f32[33,480]{1,0:T(8,128)} %refs_20_.1, f32[1,6240]{1,0:T(1,128)} %refs_16_.1), custom_call_target="tpu_custom_call" | custom-call | tf_op jit(solution)/shard_map/embed/pallas_call | solution.py:661
  11.3 4.9 %error_sketch.1.serr_ref = f32[40,512]{1,0:T(8,128)} custom-call(s32[1]{0:T(128)} %bitcast.group, f32[120,3840]{1,0:T(8,128)} %bitcast.40, f32[480,480]{1,0:T(8,128)} %bitcast.44, f32[8,3840]{1,0:T(8,128)} %bitcast.50, f32[8,480]{1,0:T(8,128)} %bitcast.57), custom_call_target="tpu_custom_call" | custom-call | tf_op jit(solution)/shard_map/error_sketch/pallas_call | solution.py:656
  16.2 0.6 broadcast_add_fusion
  16.9 0.5 collective-permute-start.2
  17.7 3.5 %collective-permute-done.4 = f32[8,128]{1,0:T(8,128)S(1)} collective-permute-done((f32[8,128]{1,0:T(8,128)S(1)}, f32[8,128]{1,0:T(8,128)S(1)}, u32[]{:S(2)}, u32[]{:S(2)}) %collective-permute-start.4) | collective-permute-done | bytes 4128 | tf_op jit(solution)/shard_map/ppermute | solution.py:535
  21.4 2.0 collective-permute-start.8
  23.4 1.5 collective-permute-start.5
  24.9 6.1 %project.1 = (bf16[20,32,1024]{2,1,0:T(8,128)(2,1)}, bf16[20,32,1024]{2,1,0:T(8,128)(2,1)}, bf16[20,32,1024]{2,1,0:T(8,128)(2,1)}) custom-call(s32[1]{0:T(128)} %bitcast.group, bf16[1024,480]{1,0:T(8,128)(2,1)} %get-tuple-element.139.h_ref, bf16[120,1440]{1,0:T(8,128)(2,1)} %copy-done.1, bf16[120,1440]{1,0:T(8,128)(2,1)} %copy-done.5, ...), custom_call_target="tpu_custom_call" | custom-call | tf_op jit(solution)/shard_map/project/pallas_call | solution.py:679
  31.0 1.6 collective-permute-start.6
  32.7 21.5 %attend.2 = (f32[240,1024]{1,0:T(8,128)}, f32[10,1,1024]{2,1,0:T(1,128)}, bf16[10,1024,1024]{2,1,0:T(8,128)(2,1)}) custom-call(bf16[20,32,1024]{2,1,0:T(8,128)(2,1)} %get-tuple-element.186.q_ref, bf16[20,32,1024]{2,1,0:T(8,128)(2,1)} %get-tuple-element.150.k_ref, bf16[20,32,1024]{2,1,0:T(8,128)(2,1)} %get-tuple-element.151.v_ref), custom_call_target="tpu_custom_call" | custom-call | tf_op jit(solution)/shard_map/attend/pallas_call | solution.py:692
  54.3 0.5 collective-permute-start.11
  54.9 0.4 collective-permute-start.13
  55.3 2.6 %collective-permute-start.9 = (f32[8,128]{1,0:T(8,128)S(1)}, f32[8,128]{1,0:T(8,128)S(1)}, u32[]{:S(2)}, u32[]{:S(2)}) collective-permute-start(f32[8,128]{1,0:T(8,128)S(1)} %add.57), channel_id=1, source_target_pairs={{0,16},{4,20},{8,24},{12,28},{16,0},{20,4},{24,8},{28,12},{1,17},{... | collective-permute-start | bytes 12296 | tf_op jit(solution)/shard_map/ppermute | solution.py:535
  57.9 21.5 %attend.3 = (f32[240,1024]{1,0:T(8,128)}, f32[10,1,1024]{2,1,0:T(1,128)}, bf16[10,1024,1024]{2,1,0:T(8,128)(2,1)}) custom-call(bf16[20,32,1024]{2,1,0:T(8,128)(2,1)} %get-tuple-element.186.q_ref, bf16[20,32,1024]{2,1,0:T(8,128)(2,1)} %get-tuple-element.150.k_ref, bf16[20,32,1024]{2,1,0:T(8,128)(2,1)} %get-tuple-element.151.v_ref), custom_call_target="tpu_custom_call" | custom-call | tf_op jit(solution)/shard_map/attend/pallas_call | solution.py:692
  79.5 0.6 add.58.count_ref.refs_15_
  80.2 0.7 copy-done.17
  81.4 38.2 %feed_and_loss.1 = (bf16[20,32,1024]{2,1,0:T(8,128)(2,1)}, f32[1024,480]{1,0:T(8,128)}, f32[40,512]{1,0:T(8,128)}, f32[56,512]{1,0:T(8,128)}, bf16[120,2400]{1,0...) custom-call(s32[1]{0:T(128)} %bitcast.group, ...), custom_call_target="tpu_custom_call" | custom-call | tf_op jit(solution)/shard_map/feed_and_loss/pallas_call | solution.py:717
  119.8 0.5 collective-permute-start.17
  120.3 0.5 collective-permute-start.18
  120.8 0.9 collective-permute-start.19
  121.7 0.6 collective-permute-start.15
  122.3 1.4 collective-permute-start.16
  123.8 25.0 %attend_back.3.dab_ref = bf16[3,240,1024]{2,1,0:T(8,128)(2,1)} custom-call(bf16[10,1024,1024]{2,1,0:T(8,128)(2,1)} %get-tuple-element.188.p_ref, bf16[20,32,1024]{2,1,0:T(8,128)(2,1)} %get-tuple-element.186.q_ref, bf16[20,32,1024]{2,1,0:T(8,128)(2,1)} %get-tuple-element.150.k_ref, bf16[20,32,1024]{2,1,0:T(8,128)(2,1)} %get-tuple-element.151.v_ref, ...), custom_call_target="tpu_custom_call" | custom-call | tf_op jit(solution)/shard_map/attend_back/pallas_call | solution.py:756
  148.8 25.0 %attend_back.2.daa_ref = bf16[3,240,1024]{2,1,0:T(8,128)(2,1)} custom-call(bf16[10,1024,1024]{2,1,0:T(8,128)(2,1)} %get-tuple-element.185.p_ref, bf16[20,32,1024]{2,1,0:T(8,128)(2,1)} %get-tuple-element.186.q_ref, bf16[20,32,1024]{2,1,0:T(8,128)(2,1)} %get-tuple-element.150.k_ref, bf16[20,32,1024]{2,1,0:T(8,128)(2,1)} %get-tuple-element.151.v_ref, ...), custom_call_target="tpu_custom_call" | custom-call | tf_op jit(solution)/shard_map/attend_back/pallas_call | solution.py:756
  173.9 12.9 %input_grads.1 = (bf16[120,1440]{1,0:T(8,128)(2,1)}, bf16[120,1440]{1,0:T(8,128)(2,1)}, bf16[120,1440]{1,0:T(8,128)(2,1)}, bf16[120,1440]{1,0:T(8,128)(2,1)}, f3...) custom-call(s32[1]{0:T(128)} %bitcast.group, s32[1,1024]{1,0:T(1,128)} %tok_ref.3, ...), custom_call_target="tpu_custom_call" | custom-call | tf_op jit(solution)/shard_map/input_grads/pallas_call | solution.py:774
  187.0 0.4 collective-permute-start.20
  187.4 0.5 collective-permute-start.21
  188.0 0.9 collective-permute-start.22
  188.9 0.7 collective-permute-start.24
  189.6 1.1 add_convert_fusion
  190.7 0.6 collective-permute-start.26
  191.3 3.0 %merge_down.1.refs_14_ = f32[480,480]{1,0:T(8,128)} custom-call(bf16[480,480]{1,0:T(8,128)(2,1)} %get-tuple-element.200.refs_0_.refs_12_, bf16[480,480]{1,0:T(8,128)(2,1)} %copy-done.13, bf16[480,480]{1,0:T(8,128)(2,1)} %copy-done.14, bf16[480,480]{1,0:T(8,128)(2,1)} %copy-done.15, f32[480,480]{1,0:T(8,128)} %bitcast.45), custom_call_target="tpu_custom_call" | custom-call | tf_op jit(solution)/shard_map/merge_down/pallas_call | solution.py:792
  194.3 0.6 collective-permute-start.23
  194.9 3.7 %collective-permute-done.23 = f32[32,512]{1,0:T(8,128)S(1)} collective-permute-done((f32[32,512]{1,0:T(8,128)S(1)}, f32[32,512]{1,0:T(8,128)S(1)}, u32[]{:S(2)}, u32[]{:S(2)}) %collective-permute-start.23) | collective-permute-done | bytes 65568 | tf_op jit(solution)/shard_map/ppermute | solution.py:535
  198.7 2.6 %collective-permute-done.26.refs_2_ = bf16[120,1440]{1,0:T(8,128)(2,1)S(1)} collective-permute-done((bf16[120,1440]{1,0:T(8,128)(2,1)S(1)}, bf16[120,1440]{1,0:T(8,128)(2,1)S(1)}, u32[]{:S(2)}, u32[]{:S(2)}) %collective-permute-start.26) | collective-permute-done | bytes 345632 | tf_op jit(solution)/shard_map/ppermute | solution.py:535
  201.3 0.5 collective-permute-start.27
  201.8 3.8 %merge_rest.1.refs_13_ = f32[120,2400]{1,0:T(8,128)} custom-call(bf16[120,2400]{1,0:T(8,128)(2,1)} %get-tuple-element.213.refs_0_.refs_8_, bf16[120,2400]{1,0:T(8,128)(2,1)} %copy-done.7, bf16[120,2400]{1,0:T(8,128)(2,1)} %copy-done.8, bf16[120,2400]{1,0:T(8,128)(2,1)} %copy-done.9, f32[120,3840]{1,0:T(8,128)} %bitcast.41), custom_call_target="tpu_custom_call" | custom-call | tf_op jit(solution)/shard_map/merge_rest/pallas_call | solution.py:792
  206.0 4.8 %collective-permute-done.28 = f32[32,512]{1,0:T(8,128)S(1)} collective-permute-done((f32[32,512]{1,0:T(8,128)S(1)}, f32[32,512]{1,0:T(8,128)S(1)}, u32[]{:S(2)}, u32[]{:S(2)}) %collective-permute-start.28) | collective-permute-done | bytes 65568 | tf_op jit(solution)/shard_map/ppermute | solution.py:535
  210.9 0.8 collective-permute-start.30
  211.7 1.1 collective-permute-start.29
  212.8 1.9 collective-permute-done.31.refs_3_
  214.7 1.2 collective-permute-done.30.refs_2_
  216.0 0.6 copy-done.24
  216.6 0.6 copy-done.25
  217.2 7.3 %left_factors.1 = (f32[128,512]{1,0:T(8,128)}, f32[40,512]{1,0:T(8,128)}, f32[8,120]{1,0:T(8,128)}, f32[8,480]{1,0:T(8,128)}, f32[8,1152]{1,0:T(8,128)}, /*index...) custom-call(s32[1]{0:T(128)} %bitcast.group, f32[32,512]{1,0:T(8,128)} %copy-done.21, f32[32,512]{1,0:T(8,128)} %copy-done.25, ...), custom_call_target="tpu_custom_call" | custom-call | tf_op jit(solution)/shard_map/left_factors/pallas_call | solution.py:806
  224.7 1.3 collective-permute-start.33
  226.0 0.5 collective-permute-start.34
  226.5 2.9 %merge_in.1.refs_12_ = f32[120,1440]{1,0:T(8,128)} custom-call(bf16[120,1440]{1,0:T(8,128)(2,1)} %get-tuple-element.222.refs_4_.refs_0_, bf16[120,1440]{1,0:T(8,128)(2,1)} %copy-done.19, bf16[120,1440]{1,0:T(8,128)(2,1)} %copy-done.20, f32[120,3840]{1,0:T(8,128)} %bitcast.43), custom_call_target="tpu_custom_call" | custom-call | tf_op jit(solution)/shard_map/merge_in/pallas_call | solution.py:792
  229.7 0.6 collective-permute-start.35
  230.3 3.5 %collective-permute-done.35 = f32[8,1152]{1,0:T(8,128)S(1)} collective-permute-done((f32[8,1152]{1,0:T(8,128)S(1)}, f32[8,1152]{1,0:T(8,128)S(1)}, u32[]{:S(2)}, u32[]{:S(2)}) %collective-permute-start.35) | collective-permute-done | bytes 36896 | tf_op jit(solution)/shard_map/ppermute | solution.py:535
  233.8 1.5 collective-permute-start.36
  235.3 2.4 collective-permute-done.36
  237.7 0.5 collective-permute-start.37
  238.2 4.4 %collective-permute-done.37 = f32[8,1152]{1,0:T(8,128)S(1)} collective-permute-done((f32[8,1152]{1,0:T(8,128)S(1)}, f32[8,1152]{1,0:T(8,128)S(1)}, u32[]{:S(2)}, u32[]{:S(2)}) %collective-permute-start.37) | collective-permute-done | bytes 36896 | tf_op jit(solution)/shard_map/ppermute | solution.py:535
  242.7 1.0 collective-permute-start.39
  243.7 0.8 collective-permute-start.38
  244.5 1.5 collective-permute-done.40.refs_3_
  246.1 1.0 collective-permute-done.39.refs_2_
  247.1 0.6 copy-done.28
  247.7 8.9 %finish.1 = (f32[1,1]{1,0:T(1,128)}, f32[1,1]{1,0:T(1,128)}, f32[1,1]{1,0:T(1,128)}, f32[8,3840]{1,0:T(8,128)}, f32[8,480]{1,0:T(8,128)}, /*index=5*/f32[120,384...) custom-call(s32[1]{0:T(128)} %bitcast.group, ...), custom_call_target="tpu_custom_call" | custom-call | tf_op jit(solution)/shard_map/finish/pallas_call | solution.py:835
  (118 shorter events, 2.9 us)
Async XLA Ops:
  0.7 4.7 %copy-start.31 = (s32[1,1024]{1,0:T(1,128)S(1)}, s32[1,1024]{1,0:T(1,128)}, u32[]{:S(2)}) copy-start(s32[1,1024]{1,0:T(1,128)} %mask_ref.1) | copy-start | bytes 12292
  2.3 14.6 %copy-start.1 = (bf16[120,1440]{1,0:T(8,128)(2,1)}, bf16[120,1440]{1,0:T(8,128)(2,1)S(1)}, u32[]{:S(2)}) copy-start(bf16[120,1440]{1,0:T(8,128)(2,1)S(1)} %slice.15.refs_0_) | copy-start | bytes 1036804
  2.3 14.5 %collective-permute-start = (bf16[120,1440]{1,0:T(8,128)(2,1)S(1)}, bf16[120,1440]{1,0:T(8,128)(2,1)S(1)}, u32[]{:S(2)}, u32[]{:S(2)}) collective-permute-start(bf16[120,1440]{1,0:T(8,128)(2,1)S(1)} %slice.15.refs_0_), channel_id=1, source_target_pairs={{0,2},{1,3},{2,0},{3,1},{4,6},{5,7},{6,4},{7,5},{8,10},{9,11},{10,... | collective-permute-start | bytes 1036808 | tf_op jit(solution)/shard_map/ppermute | solution.py:535
  6.6 9.6 %collective-permute-start.1 = (f32[8,128]{1,0:T(8,128)S(1)}, f32[8,128]{1,0:T(8,128)S(1)}, u32[]{:S(2)}, u32[]{:S(2)}) collective-permute-start(f32[8,128]{1,0:T(8,128)S(1)} %broadcast_in_dim.33), channel_id=1, source_target_pairs={{0,1},{1,0},{2,3},{3,2},{4,5},{5,4},{6,7},{7,6},{8,9},{9,8},{10,11... | collective-permute-start | bytes 12296 | tf_op jit(solution)/shard_map/ppermute | solution.py:535
  11.3 6.4 %copy-start = (f32[1,480,480]{2,1,0:T(8,128)S(1)}, f32[1,480,480]{2,1,0:T(8,128)}, u32[]{:S(2)}) copy-start(f32[1,480,480]{2,1,0:T(8,128)} %param.25) | copy-start | bytes 2764804
  16.9 8.0 %copy-start.4 = (bf16[120,1440]{1,0:T(8,128)(2,1)}, bf16[120,1440]{1,0:T(8,128)(2,1)S(1)}, u32[]{:S(2)}) copy-start(bf16[120,1440]{1,0:T(8,128)(2,1)S(1)} %collective-permute-done.refs_2_) | copy-start | bytes 1036804
  16.9 4.4 %collective-permute-start.2 = (bf16[120,1440]{1,0:T(8,128)(2,1)S(1)}, bf16[120,1440]{1,0:T(8,128)(2,1)S(1)}, u32[]{:S(2)}, u32[]{:S(2)}) collective-permute-start(bf16[120,1440]{1,0:T(8,128)(2,1)S(1)} %slice.15.refs_0_), channel_id=1, source_target_pairs={{0,1},{1,0},{2,3},{3,2},{4,5},{5,4},{6,7},{7,6},{8,9},{9,8},{10,11... | collective-permute-start | bytes 1036808 | tf_op jit(solution)/shard_map/ppermute | solution.py:535
  17.4 3.8 %collective-permute-start.3 = (bf16[120,1440]{1,0:T(8,128)(2,1)S(1)}, bf16[120,1440]{1,0:T(8,128)(2,1)S(1)}, u32[]{:S(2)}, u32[]{:S(2)}) collective-permute-start(bf16[120,1440]{1,0:T(8,128)(2,1)S(1)} %collective-permute-done.refs_2_), channel_id=1, source_target_pairs={{0,1},{1,0},{2,3},{3,2},{4,5},{5,4},{6,7},{7,6},{8,9},{9,8},{10,11... | collective-permute-start | bytes 1036808 | tf_op jit(solution)/shard_map/ppermute | solution.py:535
  17.6 36.7 %copy-start.2 = (bf16[120,2400]{1,0:T(8,128)(2,1)}, bf16[120,2400]{1,0:T(8,128)(2,1)S(1)}, u32[]{:S(2)}) copy-start(bf16[120,2400]{1,0:T(8,128)(2,1)S(1)} %pad_maximum_fusion.refs_0_) | copy-start | bytes 1728004
  17.6 3.7 %collective-permute-start.4 = (f32[8,128]{1,0:T(8,128)S(1)}, f32[8,128]{1,0:T(8,128)S(1)}, u32[]{:S(2)}, u32[]{:S(2)}) collective-permute-start(f32[8,128]{1,0:T(8,128)S(1)} %broadcast_add_fusion), channel_id=1, source_target_pairs={{0,2},{1,3},{2,0},{3,1},{4,6},{5,7},{6,4},{7,5},{8,10},{9,11},{10,... | collective-permute-start | bytes 12296 | tf_op jit(solution)/shard_map/ppermute | solution.py:535
  17.7 37.1 %copy-start.3 = (bf16[480,480]{1,0:T(8,128)(2,1)}, bf16[480,480]{1,0:T(8,128)(2,1)S(1)}, u32[]{:S(2)}) copy-start(bf16[480,480]{1,0:T(8,128)(2,1)S(1)} %bitcast_convert_fusion.refs_4_) | copy-start | bytes 1382404
  21.2 3.6 %copy-start.5 = (bf16[120,1440]{1,0:T(8,128)(2,1)}, bf16[120,1440]{1,0:T(8,128)(2,1)S(1)}, u32[]{:S(2)}) copy-start(bf16[120,1440]{1,0:T(8,128)(2,1)S(1)} %collective-permute-done.2.refs_1_) | copy-start | bytes 1036804
  21.3 3.6 %copy-start.6 = (bf16[120,1440]{1,0:T(8,128)(2,1)}, bf16[120,1440]{1,0:T(8,128)(2,1)S(1)}, u32[]{:S(2)}) copy-start(bf16[120,1440]{1,0:T(8,128)(2,1)S(1)} %collective-permute-done.3.refs_3_) | copy-start | bytes 1036804
  21.3 32.9 %collective-permute-start.7 = (bf16[120,2400]{1,0:T(8,128)(2,1)S(1)}, bf16[120,2400]{1,0:T(8,128)(2,1)S(1)}, u32[]{:S(2)}, u32[]{:S(2)}) collective-permute-start(bf16[120,2400]{1,0:T(8,128)(2,1)S(1)} %pad_maximum_fusion.refs_0_), channel_id=1, source_target_pairs={{0,2},{1,3},{2,0},{3,1},{4,6},{5,7},{6,4},{7,5},{8,10},{9,11},{10,... | collective-permute-start | bytes 1728008 | tf_op jit(solution)/shard_map/ppermute | solution.py:535
  21.4 32.8 %collective-permute-start.8 = (bf16[480,480]{1,0:T(8,128)(2,1)S(1)}, bf16[480,480]{1,0:T(8,128)(2,1)S(1)}, u32[]{:S(2)}, u32[]{:S(2)}) collective-permute-start(bf16[480,480]{1,0:T(8,128)(2,1)S(1)} %bitcast_convert_fusion.refs_4_), channel_id=1, source_target_pairs={{0,2},{1,3},{2,0},{3,1},{4,6},{5,7},{6,4},{7,5},{8,10},{9,11},{10,... | collective-permute-start | bytes 1382408 | tf_op jit(solution)/shard_map/ppermute | solution.py:535
  23.4 7.7 %collective-permute-start.5 = (f32[8,128]{1,0:T(8,128)S(1)}, f32[8,128]{1,0:T(8,128)S(1)}, u32[]{:S(2)}, u32[]{:S(2)}) collective-permute-start(f32[8,128]{1,0:T(8,128)S(1)} %add.55), channel_id=1, source_target_pairs={{0,4},{4,0},{8,12},{12,8},{16,20},{20,16},{24,28},{28,24},{1,5},{5... | collective-permute-start | bytes 12296 | tf_op jit(solution)/shard_map/ppermute | solution.py:535
  31.0 23.2 %collective-permute-start.6 = (f32[8,128]{1,0:T(8,128)S(1)}, f32[8,128]{1,0:T(8,128)S(1)}, u32[]{:S(2)}, u32[]{:S(2)}) collective-permute-start(f32[8,128]{1,0:T(8,128)S(1)} %add.56), channel_id=1, source_target_pairs={{0,8},{4,12},{8,0},{12,4},{16,24},{20,28},{24,16},{28,20},{1,9},{5... | collective-permute-start | bytes 12296 | tf_op jit(solution)/shard_map/ppermute | solution.py:535
  54.2 25.3 %copy-start.16 = (bf16[480,480]{1,0:T(8,128)(2,1)}, bf16[480,480]{1,0:T(8,128)(2,1)S(1)}, u32[]{:S(2)}) copy-start(bf16[480,480]{1,0:T(8,128)(2,1)S(1)} %collective-permute-done.8.refs_6_) | copy-start | bytes 1382404
  54.2 25.3 %copy-start.10 = (bf16[120,2400]{1,0:T(8,128)(2,1)}, bf16[120,2400]{1,0:T(8,128)(2,1)S(1)}, u32[]{:S(2)}) copy-start(bf16[120,2400]{1,0:T(8,128)(2,1)S(1)} %collective-permute-done.7.refs_2_) | copy-start | bytes 1728004
  54.2 25.9 %collective-permute-start.10 = (bf16[120,2400]{1,0:T(8,128)(2,1)S(1)}, bf16[120,2400]{1,0:T(8,128)(2,1)S(1)}, u32[]{:S(2)}, u32[]{:S(2)}) collective-permute-start(bf16[120,2400]{1,0:T(8,128)(2,1)S(1)} %pad_maximum_fusion.refs_0_), channel_id=1, source_target_pairs={{0,1},{1,0},{2,3},{3,2},{4,5},{5,4},{6,7},{7,6},{8,9},{9,8},{10,11... | collective-permute-start | bytes 1728008 | tf_op jit(solution)/shard_map/ppermute | solution.py:535
  54.3 25.8 %collective-permute-start.11 = (bf16[120,2400]{1,0:T(8,128)(2,1)S(1)}, bf16[120,2400]{1,0:T(8,128)(2,1)S(1)}, u32[]{:S(2)}, u32[]{:S(2)}) collective-permute-start(bf16[120,2400]{1,0:T(8,128)(2,1)S(1)} %collective-permute-done.7.refs_2_), channel_id=1, source_target_pairs={{0,1},{1,0},{2,3},{3,2},{4,5},{5,4},{6,7},{7,6},{8,9},{9,8},{10,11... | collective-permute-start | bytes 1728008 | tf_op jit(solution)/shard_map/ppermute | solution.py:535
  54.8 25.3 %collective-permute-start.12 = (bf16[480,480]{1,0:T(8,128)(2,1)S(1)}, bf16[480,480]{1,0:T(8,128)(2,1)S(1)}, u32[]{:S(2)}, u32[]{:S(2)}) collective-permute-start(bf16[480,480]{1,0:T(8,128)(2,1)S(1)} %bitcast_convert_fusion.refs_4_), channel_id=1, source_target_pairs={{0,1},{1,0},{2,3},{3,2},{4,5},{5,4},{6,7},{7,6},{8,9},{9,8},{10,11... | collective-permute-start | bytes 1382408 | tf_op jit(solution)/shard_map/ppermute | solution.py:535
  54.9 25.2 %collective-permute-start.13 = (bf16[480,480]{1,0:T(8,128)(2,1)S(1)}, bf16[480,480]{1,0:T(8,128)(2,1)S(1)}, u32[]{:S(2)}, u32[]{:S(2)}) collective-permute-start(bf16[480,480]{1,0:T(8,128)(2,1)S(1)} %collective-permute-done.8.refs_6_), channel_id=1, source_target_pairs={{0,1},{1,0},{2,3},{3,2},{4,5},{5,4},{6,7},{7,6},{8,9},{9,8},{10,11... | collective-permute-start | bytes 1382408 | tf_op jit(solution)/shard_map/ppermute | solution.py:535
  55.3 24.2 %collective-permute-start.9 = (f32[8,128]{1,0:T(8,128)S(1)}, f32[8,128]{1,0:T(8,128)S(1)}, u32[]{:S(2)}, u32[]{:S(2)}) collective-permute-start(f32[8,128]{1,0:T(8,128)S(1)} %add.57), channel_id=1, source_target_pairs={{0,16},{4,20},{8,24},{12,28},{16,0},{20,4},{24,8},{28,12},{1,17},{... | collective-permute-start | bytes 12296 | tf_op jit(solution)/shard_map/ppermute | solution.py:535
  80.1 1.3 copy-start.12
  119.7 2.6 %collective-permute-start.14 = (bf16[480,480]{1,0:T(8,128)(2,1)}, bf16[480,480]{1,0:T(8,128)(2,1)S(1)}, u32[]{:S(2)}, u32[]{:S(2)}) collective-permute-start(bf16[480,480]{1,0:T(8,128)(2,1)} %get-tuple-element.178.refs_13_), channel_id=1, source_target_pairs={{0,1},{1,0},{2,3},{3,2},{4,5},{5,4},{6,7},{7,6},{8,9},{9,8},{10,11... | collective-permute-start | bytes 1382408 | tf_op jit(solution)/shard_map/ppermute | solution.py:535
  119.8 54.1 %collective-permute-start.17 = (bf16[120,2400]{1,0:T(8,128)(2,1)}, bf16[120,2400]{1,0:T(8,128)(2,1)S(1)}, u32[]{:S(2)}, u32[]{:S(2)}) collective-permute-start(bf16[120,2400]{1,0:T(8,128)(2,1)} %get-tuple-element.182.refs_9_), channel_id=1, source_target_pairs={{0,1},{1,0},{2,3},{3,2},{4,5},{5,4},{6,7},{7,6},{8,9},{9,8},{10,11... | collective-permute-start | bytes 1728008 | tf_op jit(solution)/shard_map/ppermute | solution.py:535
  120.3 53.6 %collective-permute-start.18 = (bf16[120,2400]{1,0:T(8,128)(2,1)}, bf16[120,2400]{1,0:T(8,128)(2,1)S(1)}, u32[]{:S(2)}, u32[]{:S(2)}) collective-permute-start(bf16[120,2400]{1,0:T(8,128)(2,1)} %get-tuple-element.183.refs_10_), channel_id=1, source_target_pairs={{0,2},{1,3},{2,0},{3,1},{4,6},{5,7},{6,4},{7,5},{8,10},{9,11},{10,... | collective-permute-start | bytes 1728008 | tf_op jit(solution)/shard_map/ppermute | solution.py:535
  120.8 53.1 %collective-permute-start.19 = (bf16[120,2400]{1,0:T(8,128)(2,1)}, bf16[120,2400]{1,0:T(8,128)(2,1)S(1)}, u32[]{:S(2)}, u32[]{:S(2)}) collective-permute-start(bf16[120,2400]{1,0:T(8,128)(2,1)} %get-tuple-element.184.refs_11_), channel_id=1, source_target_pairs={{0,3},{1,2},{2,1},{3,0},{4,7},{5,6},{6,5},{7,4},{8,11},{9,10},{10,... | collective-permute-start | bytes 1728008 | tf_op jit(solution)/shard_map/ppermute | solution.py:535
  121.7 52.1 %collective-permute-start.15 = (bf16[480,480]{1,0:T(8,128)(2,1)}, bf16[480,480]{1,0:T(8,128)(2,1)S(1)}, u32[]{:S(2)}, u32[]{:S(2)}) collective-permute-start(bf16[480,480]{1,0:T(8,128)(2,1)} %get-tuple-element.179.refs_14_), channel_id=1, source_target_pairs={{0,2},{1,3},{2,0},{3,1},{4,6},{5,7},{6,4},{7,5},{8,10},{9,11},{10,... | collective-permute-start | bytes 1382408 | tf_op jit(solution)/shard_map/ppermute | solution.py:535
  122.3 26.5 %copy-start.13 = (bf16[480,480]{1,0:T(8,128)(2,1)}, bf16[480,480]{1,0:T(8,128)(2,1)S(1)}, u32[]{:S(2)}) copy-start(bf16[480,480]{1,0:T(8,128)(2,1)S(1)} %collective-permute-done.14.refs_1_) | copy-start | bytes 1382404
  122.3 51.5 %collective-permute-start.16 = (bf16[480,480]{1,0:T(8,128)(2,1)}, bf16[480,480]{1,0:T(8,128)(2,1)S(1)}, u32[]{:S(2)}, u32[]{:S(2)}) collective-permute-start(bf16[480,480]{1,0:T(8,128)(2,1)} %get-tuple-element.180.refs_15_), channel_id=1, source_target_pairs={{0,3},{1,2},{2,1},{3,0},{4,7},{5,6},{6,5},{7,4},{8,11},{9,10},{10,... | collective-permute-start | bytes 1382408 | tf_op jit(solution)/shard_map/ppermute | solution.py:535
  173.8 13.0 %copy-start.14 = (bf16[480,480]{1,0:T(8,128)(2,1)}, bf16[480,480]{1,0:T(8,128)(2,1)S(1)}, u32[]{:S(2)}) copy-start(bf16[480,480]{1,0:T(8,128)(2,1)S(1)} %collective-permute-done.15.refs_2_) | copy-start | bytes 1382404
  173.8 13.0 %copy-start.15 = (bf16[480,480]{1,0:T(8,128)(2,1)}, bf16[480,480]{1,0:T(8,128)(2,1)S(1)}, u32[]{:S(2)}) copy-start(bf16[480,480]{1,0:T(8,128)(2,1)S(1)} %collective-permute-done.16.refs_3_) | copy-start | bytes 1382404
  173.8 13.0 %copy-start.7 = (bf16[120,2400]{1,0:T(8,128)(2,1)}, bf16[120,2400]{1,0:T(8,128)(2,1)S(1)}, u32[]{:S(2)}) copy-start(bf16[120,2400]{1,0:T(8,128)(2,1)S(1)} %collective-permute-done.17.refs_1_) | copy-start | bytes 1728004
  173.9 13.0 %copy-start.8 = (bf16[120,2400]{1,0:T(8,128)(2,1)}, bf16[120,2400]{1,0:T(8,128)(2,1)S(1)}, u32[]{:S(2)}) copy-start(bf16[120,2400]{1,0:T(8,128)(2,1)S(1)} %collective-permute-done.18.refs_2_) | copy-start | bytes 1728004
  173.9 13.0 %copy-start.9 = (bf16[120,2400]{1,0:T(8,128)(2,1)}, bf16[120,2400]{1,0:T(8,128)(2,1)S(1)}, u32[]{:S(2)}) copy-start(bf16[120,2400]{1,0:T(8,128)(2,1)S(1)} %collective-permute-done.19.refs_3_) | copy-start | bytes 1728004
  186.9 2.7 %collective-permute-start.25 = (bf16[120,1440]{1,0:T(8,128)(2,1)}, bf16[120,1440]{1,0:T(8,128)(2,1)S(1)}, u32[]{:S(2)}, u32[]{:S(2)}) collective-permute-start(bf16[120,1440]{1,0:T(8,128)(2,1)} %get-tuple-element.211.refs_7_), channel_id=1, source_target_pairs={{0,1},{1,0},{2,3},{3,2},{4,5},{5,4},{6,7},{7,6},{8,9},{9,8},{10,11... | collective-permute-start | bytes 1036808 | tf_op jit(solution)/shard_map/ppermute | solution.py:535
  187.0 7.3 %collective-permute-start.20 = (f32[32,512]{1,0:T(8,128)}, f32[32,512]{1,0:T(8,128)S(1)}, u32[]{:S(2)}, u32[]{:S(2)}) collective-permute-start(f32[32,512]{1,0:T(8,128)} %get-tuple-element.197), channel_id=1, source_target_pairs={{0,1},{1,0},{2,3},{3,2},{4,5},{5,4},{6,7},{7,6},{8,9},{9,8},{10,11... | collective-permute-start | bytes 196616 | tf_op jit(solution)/shard_map/ppermute | solution.py:535
  187.4 6.9 %collective-permute-start.21 = (f32[32,512]{1,0:T(8,128)}, f32[32,512]{1,0:T(8,128)S(1)}, u32[]{:S(2)}, u32[]{:S(2)}) collective-permute-start(f32[32,512]{1,0:T(8,128)} %get-tuple-element.198), channel_id=1, source_target_pairs={{0,2},{1,3},{2,0},{3,1},{4,6},{5,7},{6,4},{7,5},{8,10},{9,11},{10,... | collective-permute-start | bytes 196616 | tf_op jit(solution)/shard_map/ppermute | solution.py:535
  188.0 6.3 %collective-permute-start.22 = (f32[32,512]{1,0:T(8,128)}, f32[32,512]{1,0:T(8,128)S(1)}, u32[]{:S(2)}, u32[]{:S(2)}) collective-permute-start(f32[32,512]{1,0:T(8,128)} %get-tuple-element.199), channel_id=1, source_target_pairs={{0,3},{1,2},{2,1},{3,0},{4,7},{5,6},{6,5},{7,4},{8,11},{9,10},{10,... | collective-permute-start | bytes 196616 | tf_op jit(solution)/shard_map/ppermute | solution.py:535
  188.9 9.8 %collective-permute-start.24 = (bf16[120,1440]{1,0:T(8,128)(2,1)}, bf16[120,1440]{1,0:T(8,128)(2,1)S(1)}, u32[]{:S(2)}, u32[]{:S(2)}) collective-permute-start(bf16[120,1440]{1,0:T(8,128)(2,1)} %get-tuple-element.209.refs_5_), channel_id=1, source_target_pairs={{0,1},{1,0},{2,3},{3,2},{4,5},{5,4},{6,7},{7,6},{8,9},{9,8},{10,11... | collective-permute-start | bytes 1036808 | tf_op jit(solution)/shard_map/ppermute | solution.py:535
  190.7 3.6 %copy-start.26 = (f32[32,512]{1,0:T(8,128)S(1)}, f32[32,512]{1,0:T(8,128)}, u32[]{:S(2)}) copy-start(f32[32,512]{1,0:T(8,128)} %get-tuple-element.204) | copy-start | bytes 196612
  190.7 10.6 %collective-permute-start.26 = (bf16[120,1440]{1,0:T(8,128)(2,1)S(1)}, bf16[120,1440]{1,0:T(8,128)(2,1)S(1)}, u32[]{:S(2)}, u32[]{:S(2)}) collective-permute-start(bf16[120,1440]{1,0:T(8,128)(2,1)S(1)} %add_convert_fusion), channel_id=1, source_target_pairs={{0,2},{1,3},{2,0},{3,1},{4,6},{5,7},{6,4},{7,5},{8,10},{9,11},{10,... | collective-permute-start | bytes 1036808 | tf_op jit(solution)/shard_map/ppermute | solution.py:535
  194.3 4.3 %collective-permute-start.23 = (f32[32,512]{1,0:T(8,128)S(1)}, f32[32,512]{1,0:T(8,128)S(1)}, u32[]{:S(2)}, u32[]{:S(2)}) collective-permute-start(f32[32,512]{1,0:T(8,128)S(1)} %add_add_fusion), channel_id=1, source_target_pairs={{0,4},{4,0},{8,12},{12,8},{16,20},{20,16},{24,28},{28,24},{1,5},{5... | collective-permute-start | bytes 196616 | tf_op jit(solution)/shard_map/ppermute | solution.py:535
  198.7 6.9 %copy-start.19 = (bf16[120,1440]{1,0:T(8,128)(2,1)}, bf16[120,1440]{1,0:T(8,128)(2,1)S(1)}, u32[]{:S(2)}) copy-start(bf16[120,1440]{1,0:T(8,128)(2,1)S(1)} %collective-permute-done.24.refs_1_) | copy-start | bytes 1036804
  201.3 4.3 %copy-start.20 = (bf16[120,1440]{1,0:T(8,128)(2,1)}, bf16[120,1440]{1,0:T(8,128)(2,1)S(1)}, u32[]{:S(2)}) copy-start(bf16[120,1440]{1,0:T(8,128)(2,1)S(1)} %collective-permute-done.26.refs_2_) | copy-start | bytes 1036804
  201.3 4.3 %collective-permute-start.27 = (f32[32,512]{1,0:T(8,128)S(1)}, f32[32,512]{1,0:T(8,128)S(1)}, u32[]{:S(2)}, u32[]{:S(2)}) collective-permute-start(f32[32,512]{1,0:T(8,128)S(1)} %add.63), channel_id=1, source_target_pairs={{0,8},{4,12},{8,0},{12,4},{16,24},{20,28},{24,16},{28,20},{1,9},{5... | collective-permute-start | bytes 196616 | tf_op jit(solution)/shard_map/ppermute | solution.py:535
  205.6 5.2 %collective-permute-start.28 = (f32[32,512]{1,0:T(8,128)S(1)}, f32[32,512]{1,0:T(8,128)S(1)}, u32[]{:S(2)}, u32[]{:S(2)}) collective-permute-start(f32[32,512]{1,0:T(8,128)S(1)} %add.64), channel_id=1, source_target_pairs={{0,16},{4,20},{8,24},{12,28},{16,0},{20,4},{24,8},{28,12},{1,17},{... | collective-permute-start | bytes 196616 | tf_op jit(solution)/shard_map/ppermute | solution.py:535
  210.9 5.1 %copy-start.21 = (f32[32,512]{1,0:T(8,128)}, f32[32,512]{1,0:T(8,128)S(1)}, u32[]{:S(2)}) copy-start(f32[32,512]{1,0:T(8,128)S(1)} %add.65.refs_0_) | copy-start | bytes 196612
  210.9 3.8 %collective-permute-start.31 = (f32[32,512]{1,0:T(8,128)S(1)}, f32[32,512]{1,0:T(8,128)S(1)}, u32[]{:S(2)}, u32[]{:S(2)}) collective-permute-start(f32[32,512]{1,0:T(8,128)S(1)} %add.65.refs_0_), channel_id=1, source_target_pairs={{0,3},{1,2},{2,1},{3,0},{4,7},{5,6},{6,5},{7,4},{8,11},{9,10},{10,... | collective-permute-start | bytes 196616 | tf_op jit(solution)/shard_map/ppermute | solution.py:535
  210.9 5.0 %collective-permute-start.30 = (f32[32,512]{1,0:T(8,128)S(1)}, f32[32,512]{1,0:T(8,128)S(1)}, u32[]{:S(2)}, u32[]{:S(2)}) collective-permute-start(f32[32,512]{1,0:T(8,128)S(1)} %add.65.refs_0_), channel_id=1, source_target_pairs={{0,2},{1,3},{2,0},{3,1},{4,6},{5,7},{6,4},{7,5},{8,10},{9,11},{10,... | collective-permute-start | bytes 196616 | tf_op jit(solution)/shard_map/ppermute | solution.py:535
  211.7 4.2 %collective-permute-start.29 = (f32[32,512]{1,0:T(8,128)S(1)}, f32[32,512]{1,0:T(8,128)S(1)}, u32[]{:S(2)}, u32[]{:S(2)}) collective-permute-start(f32[32,512]{1,0:T(8,128)S(1)} %add.65.refs_0_), channel_id=1, source_target_pairs={{0,1},{1,0},{2,3},{3,2},{4,5},{5,4},{6,7},{7,6},{8,9},{9,8},{10,11... | collective-permute-start | bytes 196616 | tf_op jit(solution)/shard_map/ppermute | solution.py:535
  224.5 4.8 %collective-permute-start.32 = (f32[8,1152]{1,0:T(8,128)}, f32[8,1152]{1,0:T(8,128)S(1)}, u32[]{:S(2)}, u32[]{:S(2)}) collective-permute-start(f32[8,1152]{1,0:T(8,128)} %get-tuple-element.219), channel_id=1, source_target_pairs={{0,1},{1,0},{2,3},{3,2},{4,5},{5,4},{6,7},{7,6},{8,9},{9,8},{10,11... | collective-permute-start | bytes 110600 | tf_op jit(solution)/shard_map/ppermute | solution.py:535
  224.7 4.7 %collective-permute-start.33 = (f32[8,1152]{1,0:T(8,128)}, f32[8,1152]{1,0:T(8,128)S(1)}, u32[]{:S(2)}, u32[]{:S(2)}) collective-permute-start(f32[8,1152]{1,0:T(8,128)} %get-tuple-element.220), channel_id=1, source_target_pairs={{0,2},{1,3},{2,0},{3,1},{4,6},{5,7},{6,4},{7,5},{8,10},{9,11},{10,... | collective-permute-start | bytes 110600 | tf_op jit(solution)/shard_map/ppermute | solution.py:535
  226.0 3.7 %copy-start.30 = (f32[8,1152]{1,0:T(8,128)S(1)}, f32[8,1152]{1,0:T(8,128)}, u32[]{:S(2)}) copy-start(f32[8,1152]{1,0:T(8,128)} %get-tuple-element.225) | copy-start | bytes 110596
  226.0 3.7 %collective-permute-start.34 = (f32[8,1152]{1,0:T(8,128)}, f32[8,1152]{1,0:T(8,128)S(1)}, u32[]{:S(2)}, u32[]{:S(2)}) collective-permute-start(f32[8,1152]{1,0:T(8,128)} %get-tuple-element.221), channel_id=1, source_target_pairs={{0,3},{1,2},{2,1},{3,0},{4,7},{5,6},{6,5},{7,4},{8,11},{9,10},{10,... | collective-permute-start | bytes 110600 | tf_op jit(solution)/shard_map/ppermute | solution.py:535
  229.7 4.0 %collective-permute-start.35 = (f32[8,1152]{1,0:T(8,128)S(1)}, f32[8,1152]{1,0:T(8,128)S(1)}, u32[]{:S(2)}, u32[]{:S(2)}) collective-permute-start(f32[8,1152]{1,0:T(8,128)S(1)} %add_add_fusion.1), channel_id=1, source_target_pairs={{0,4},{4,0},{8,12},{12,8},{16,20},{20,16},{24,28},{28,24},{1,5},{5... | collective-permute-start | bytes 110600 | tf_op jit(solution)/shard_map/ppermute | solution.py:535
  233.8 4.0 %collective-permute-start.36 = (f32[8,1152]{1,0:T(8,128)S(1)}, f32[8,1152]{1,0:T(8,128)S(1)}, u32[]{:S(2)}, u32[]{:S(2)}) collective-permute-start(f32[8,1152]{1,0:T(8,128)S(1)} %add.69), channel_id=1, source_target_pairs={{0,8},{4,12},{8,0},{12,4},{16,24},{20,28},{24,16},{28,20},{1,9},{5... | collective-permute-start | bytes 110600 | tf_op jit(solution)/shard_map/ppermute | solution.py:535
  237.7 4.9 %collective-permute-start.37 = (f32[8,1152]{1,0:T(8,128)S(1)}, f32[8,1152]{1,0:T(8,128)S(1)}, u32[]{:S(2)}, u32[]{:S(2)}) collective-permute-start(f32[8,1152]{1,0:T(8,128)S(1)} %add.70), channel_id=1, source_target_pairs={{0,16},{4,20},{8,24},{12,28},{16,0},{20,4},{24,8},{28,12},{1,17},{... | collective-permute-start | bytes 110600 | tf_op jit(solution)/shard_map/ppermute | solution.py:535
  242.6 4.5 %copy-start.22 = (f32[8,1152]{1,0:T(8,128)}, f32[8,1152]{1,0:T(8,128)S(1)}, u32[]{:S(2)}) copy-start(f32[8,1152]{1,0:T(8,128)S(1)} %add.71.refs_0_) | copy-start | bytes 110596
  242.6 3.4 %collective-permute-start.40 = (f32[8,1152]{1,0:T(8,128)S(1)}, f32[8,1152]{1,0:T(8,128)S(1)}, u32[]{:S(2)}, u32[]{:S(2)}) collective-permute-start(f32[8,1152]{1,0:T(8,128)S(1)} %add.71.refs_0_), channel_id=1, source_target_pairs={{0,3},{1,2},{2,1},{3,0},{4,7},{5,6},{6,5},{7,4},{8,11},{9,10},{10,... | collective-permute-start | bytes 110600 | tf_op jit(solution)/shard_map/ppermute | solution.py:535
  242.7 4.4 %collective-permute-start.39 = (f32[8,1152]{1,0:T(8,128)S(1)}, f32[8,1152]{1,0:T(8,128)S(1)}, u32[]{:S(2)}, u32[]{:S(2)}) collective-permute-start(f32[8,1152]{1,0:T(8,128)S(1)} %add.71.refs_0_), channel_id=1, source_target_pairs={{0,2},{1,3},{2,0},{3,1},{4,6},{5,7},{6,4},{7,5},{8,10},{9,11},{10,... | collective-permute-start | bytes 110600 | tf_op jit(solution)/shard_map/ppermute | solution.py:535
  243.7 3.3 %collective-permute-start.38 = (f32[8,1152]{1,0:T(8,128)S(1)}, f32[8,1152]{1,0:T(8,128)S(1)}, u32[]{:S(2)}, u32[]{:S(2)}) collective-permute-start(f32[8,1152]{1,0:T(8,128)S(1)} %add.71.refs_0_), channel_id=1, source_target_pairs={{0,1},{1,0},{2,3},{3,2},{4,5},{5,4},{6,7},{7,6},{8,9},{9,8},{10,11... | collective-permute-start | bytes 110600 | tf_op jit(solution)/shard_map/ppermute | solution.py:535
  (9 other events, 7.6 us)
